TPU v7x, 32 devices: a whole 2x2x4 slice. The times are simulated.
32 devices in a mesh: section: 2 (over core), dp: 16 (over z, y, x).
Axes of the slice: x: 2, y: 2, z: 4, core: 2. Of those that a mesh axis runs over, the one named last changes fastest.
Arguments:
- patches: bfloat16 [64, 529, 768], P('dp'), may hold values from -6 to 6
- visible: int32 [64], P('dp'), may hold values from 40 to 529, as said below
- source: int32 [64, 529], P('dp'), may hold values from -1 to 528, as said below
- enc_gains: bfloat16 [3, 768], replicated, may hold values from 0.5 to 1.5
- enc_shifts: bfloat16 [3, 768], replicated, may hold values from -1.25 to 1.25
- enc_qkv: bfloat16 [768, 2304], replicated, may hold values from -0.21875 to 0.21875
- enc_out: bfloat16 [768, 768], replicated, may hold values from -2.5 to 2.5
- enc_bias_out: bfloat16 [2, 768], replicated, may hold values from -1.25 to 1.25
- enc_up: bfloat16 [768, 3072], replicated, may hold values from -0.21875 to 0.21875
- enc_bias_up: bfloat16 [3072], replicated, may hold values from -1.25 to 1.25
- enc_down: bfloat16 [3072, 768], replicated, may hold values from -0.109375 to 0.109375
- enc_proj: bfloat16 [768, 512], replicated, may hold values from -0.21875 to 0.21875
- proj_bias: bfloat16 [512], replicated, may hold values from -1.25 to 1.25
- mask_token: bfloat16 [512], replicated, may hold values from -6 to 6
- dec_gains: bfloat16 [2, 512], replicated, may hold values from 0.5 to 1.5
- dec_shifts: bfloat16 [2, 512], replicated, may hold values from -1.25 to 1.25
- dec_qkv: bfloat16 [512, 1536], replicated, may hold values from -0.25 to 0.25
- dec_out: bfloat16 [512, 512], replicated, may hold values from -3 to 3
- dec_bias_out: bfloat16 [2, 512], replicated, may hold values from -1.25 to 1.25
- dec_up: bfloat16 [512, 2048], replicated, may hold values from -0.25 to 0.25
- dec_bias_up: bfloat16 [2048], replicated, may hold values from -1.25 to 1.25
- dec_down: bfloat16 [2048, 512], replicated, may hold values from -0.125 to 0.125
- cotangent: bfloat16 [64, 529, 512], P('dp'), may hold values from -6 to 6
Outputs:
- decoded: bfloat16 [64, 529, 512], P('dp', None, 'section')
- patch_grad: bfloat16 [64, 529, 768], P('dp', None, 'section')
- grad_enc_gains: float32 [3, 768], P(None, ('section', 'dp'))
- grad_enc_shifts: float32 [3, 768], P(None, ('section', 'dp'))
- grad_enc_qkv: float32 [768, 2304], P(('section', 'dp'))
- grad_enc_out: float32 [768, 768], P(('section', 'dp'))
- grad_enc_bias_out: float32 [2, 768], P(None, ('section', 'dp'))
- grad_enc_up: float32 [768, 3072], P(('section', 'dp'))
- grad_enc_bias_up: float32 [3072], P(('section', 'dp'))
- grad_enc_down: float32 [3072, 768], P(('section', 'dp'))
- grad_enc_proj: float32 [768, 512], P(('section', 'dp'))
- grad_proj_bias: float32 [512], P(('section', 'dp'))
- grad_mask_token: float32 [512], P(('section', 'dp'))
- grad_dec_gains: float32 [2, 512], P(None, ('section', 'dp'))
- grad_dec_shifts: float32 [2, 512], P(None, ('section', 'dp'))
- grad_dec_qkv: float32 [512, 1536], P(('section', 'dp'))
- grad_dec_out: float32 [512, 512], P(('section', 'dp'))
- grad_dec_bias_out: float32 [2, 512], P(None, ('section', 'dp'))
- grad_dec_up: float32 [512, 2048], P(('section', 'dp'))
- grad_dec_bias_up: float32 [2048], P(('section', 'dp'))
- grad_dec_down: float32 [2048, 512], P(('section', 'dp'))
Inputs may be any that keep to these rules, and one draw needn't show every extreme that they name: Rows of a strip at and after its count are padding. Some strip has 529 visible patches and some has 40. `source`: the non-negative entries of row i are 0 to visible[i] - 1, each once; all other entries are -1.
All inputs are finite; a program needn't handle non-finite values.
Results may differ from a plain program's by a relative error of at most 0.018.
Values may be sent and summed in bfloat16 or wider, within the bound.
No kernel may reach another device: no remote copies, remote signals or barrier semaphores. Data moves between devices by JAX's collectives and lax.ppermute only.
A program may use at most 576 MiB of HBM per device.

v0:
```python
import math

import jax
import jax.numpy as jnp
from jax import lax
from jax.sharding import PartitionSpec as P

HEADS_ENC = 12
HEADS_DEC = 16
MICRO = 4


epsilon = 1e-06


def from_behind(value, axis, steps):
    count = lax.axis_size(axis)
    initial, last = (max(0, -steps), min(count, count - steps))
    return lax.ppermute(value, axis, [(source, source + steps) for source in range(initial, last)])


def swapped(block, axis, bit):
    count = lax.axis_size(axis)
    route = []
    for low in range(count):
        high = low | 1 << bit
        if high != low and high < count:
            route += [(low, high), (high, low)]
    return lax.ppermute(block, axis, route)


def apply_norm(values, gain_row, shift_row):
    center = values - jnp.mean(values, axis=-1, keepdims=True)
    inverse = lax.rsqrt(jnp.mean(center * center, axis=-1, keepdims=True) + epsilon)
    normed = center * inverse
    return (normed * gain_row + shift_row, normed, inverse)


def norm_grad(grad_out, normed, inverse, gain_row):
    scaled = grad_out * gain_row
    grad_in = inverse * (
        scaled
        - jnp.mean(scaled, axis=-1, keepdims=True)
        - normed * jnp.mean(scaled * normed, axis=-1, keepdims=True)
    )
    return (grad_in, jnp.sum(grad_out * normed, axis=(0, 1)), jnp.sum(grad_out, axis=(0, 1)))


def gelu_exact(values):
    return jax.nn.gelu(values, approximate=False)


def place_table(length_rows, model_width):
    halfway = model_width // 2
    places = jnp.arange(length_rows, dtype=jnp.float32)[:, None]
    rates = jnp.exp(jnp.arange(halfway, dtype=jnp.float32) * (-math.log(10000.0) / halfway))[
        None, :
    ]
    return jnp.concatenate([jnp.sin(places * rates), jnp.cos(places * rates)], axis=1)


def forward_product(left_side, right_side):
    return jnp.einsum("bld,df->blf", left_side, right_side, preferred_element_type=jnp.float32)


def backward_product(left_side, right_side):
    return jnp.einsum("blf,df->bld", left_side, right_side, preferred_element_type=jnp.float32)


def weight_product(left_side, right_side):
    return jnp.einsum("bld,blf->df", left_side, right_side, preferred_element_type=jnp.float32)


def split_heads(packed, head_count):
    batch_size, length, triple = packed.shape
    model_width = triple // 3
    head_size = model_width // head_count
    head_shape = (batch_size, length, head_count, head_size)
    queries = packed[..., :model_width].reshape(head_shape)
    key_rows = packed[..., model_width : 2 * model_width].reshape(head_shape)
    value_rows = packed[..., 2 * model_width :].reshape(head_shape)
    return (queries, key_rows, value_rows, head_size ** (-0.5))


def masked_scores(queries, key_rows, key_valid, factor):
    scores = (
        jnp.einsum("bqhd,bkhd->bhqk", queries, key_rows, preferred_element_type=jnp.float32)
        * factor
    )
    return jnp.where(key_valid[:, None, None, :], scores, -1e30)


def attend(packed, key_valid, head_count):
    queries, key_rows, value_rows, factor = split_heads(packed, head_count)
    scores = masked_scores(queries, key_rows, key_valid, factor)
    highest = jnp.max(scores, axis=-1, keepdims=True)
    exp_terms = jnp.exp(scores - highest)
    totals = jnp.sum(exp_terms, axis=-1, keepdims=True)
    weights_low = (exp_terms / totals).astype(jnp.bfloat16)
    mixed_rows = jnp.einsum(
        "bhqk,bkhd->bqhd", weights_low, value_rows, preferred_element_type=jnp.float32
    )
    mixed_rows = mixed_rows.reshape(packed.shape[0], packed.shape[1], -1).astype(jnp.bfloat16)
    return (mixed_rows, (highest, totals))


def attend_grad(packed, key_valid, head_count, softmax_kept, grad_mixed):
    queries, key_rows, value_rows, factor = split_heads(packed, head_count)
    highest, totals = softmax_kept
    weights_full = jnp.exp(masked_scores(queries, key_rows, key_valid, factor) - highest) / totals
    grad_heads = grad_mixed.reshape(queries.shape)
    grad_weights = jnp.einsum(
        "bqhd,bkhd->bhqk", grad_heads, value_rows, preferred_element_type=jnp.float32
    )
    grad_scores = (
        weights_full * (grad_weights - jnp.sum(weights_full * grad_weights, axis=-1, keepdims=True))
    ).astype(jnp.bfloat16)
    grad_queries = (
        jnp.einsum("bhqk,bkhd->bqhd", grad_scores, key_rows, preferred_element_type=jnp.float32)
        * factor
    )
    grad_keys = (
        jnp.einsum("bhqk,bqhd->bkhd", grad_scores, queries, preferred_element_type=jnp.float32)
        * factor
    )
    grad_values = jnp.einsum(
        "bhqk,bqhd->bkhd",
        weights_full.astype(jnp.bfloat16),
        grad_heads,
        preferred_element_type=jnp.float32,
    )
    flat_shape = (packed.shape[0], packed.shape[1], -1)
    return jnp.concatenate(
        [
            grad_queries.reshape(flat_shape),
            grad_keys.reshape(flat_shape),
            grad_values.reshape(flat_shape),
        ],
        axis=-1,
    ).astype(jnp.bfloat16)


def block_forward(inputs, key_valid, weights, head_count):
    gain_rows, shifts, w_qkv, w_out, bias_out, w_up, bias_up, w_down = weights
    normed_one, unit_one, inverse_one = apply_norm(inputs, gain_rows[0], shifts[0])
    low_one = normed_one.astype(jnp.bfloat16)
    packed = forward_product(low_one, w_qkv).astype(jnp.bfloat16)
    mixed_rows, softmax_kept = attend(packed, key_valid, head_count)
    middle = inputs + forward_product(mixed_rows, w_out) + bias_out[0]
    normed_two, unit_two, inverse_two = apply_norm(middle, gain_rows[1], shifts[1])
    low_two = normed_two.astype(jnp.bfloat16)
    hidden = forward_product(low_two, w_up) + bias_up
    active = gelu_exact(hidden).astype(jnp.bfloat16)
    result = middle + forward_product(active, w_down) + bias_out[1]
    return (
        result,
        (
            unit_one,
            inverse_one,
            low_one,
            packed,
            mixed_rows,
            softmax_kept,
            unit_two,
            inverse_two,
            low_two,
            hidden,
            active,
        ),
    )


def kept_zeros(batch_size, length, model_width, head_count, hidden_units):
    full_rows = (batch_size, length, model_width)
    column = (batch_size, length, 1)
    stats = (batch_size, head_count, length, 1)
    block_kept = (
        jnp.zeros(full_rows, jnp.float32),
        jnp.zeros(column, jnp.float32),
        jnp.zeros(full_rows, jnp.bfloat16),
        jnp.zeros((batch_size, length, 3 * model_width), jnp.bfloat16),
        jnp.zeros(full_rows, jnp.bfloat16),
        (jnp.zeros(stats, jnp.float32), jnp.zeros(stats, jnp.float32)),
        jnp.zeros(full_rows, jnp.float32),
        jnp.zeros(column, jnp.float32),
        jnp.zeros(full_rows, jnp.bfloat16),
        jnp.zeros((batch_size, length, hidden_units), jnp.float32),
        jnp.zeros((batch_size, length, hidden_units), jnp.bfloat16),
    )
    return (
        jnp.zeros(full_rows, jnp.bfloat16),
        block_kept,
        jnp.zeros(full_rows, jnp.float32),
        jnp.zeros(column, jnp.float32),
    )


def block_backward(grad_result, kept_values, weights, key_valid, head_count):
    gain_rows, shifts, w_qkv, w_out, bias_out, w_up, bias_up, w_down = weights
    (
        unit_one,
        inverse_one,
        low_one,
        packed,
        mixed_rows,
        softmax_kept,
        unit_two,
        inverse_two,
        low_two,
        hidden,
        active,
    ) = kept_values
    grad_low = grad_result.astype(jnp.bfloat16)
    grad_down = weight_product(active, grad_low)
    grad_bias_two = jnp.sum(grad_low.astype(jnp.float32), axis=(0, 1))
    grad_active = backward_product(grad_low, w_down)
    gelu_value, gelu_pull = jax.vjp(gelu_exact, hidden)
    grad_hidden = gelu_pull(grad_active)[0].astype(jnp.bfloat16)
    grad_up = weight_product(low_two, grad_hidden)
    grad_bias_up = jnp.sum(grad_hidden.astype(jnp.float32), axis=(0, 1))
    grad_norm_two = backward_product(grad_hidden, w_up)
    grad_from_two, grad_gain_two, grad_shift_two = norm_grad(
        grad_norm_two, unit_two, inverse_two, gain_rows[1]
    )
    grad_middle = grad_result + grad_from_two
    grad_middle_low = grad_middle.astype(jnp.bfloat16)
    grad_out = weight_product(mixed_rows, grad_middle_low)
    grad_bias_one = jnp.sum(grad_middle_low.astype(jnp.float32), axis=(0, 1))
    grad_mixed = backward_product(grad_middle_low, w_out).astype(jnp.bfloat16)
    grad_packed = attend_grad(packed, key_valid, head_count, softmax_kept, grad_mixed)
    grad_qkv = weight_product(low_one, grad_packed)
    grad_norm_one = backward_product(grad_packed, w_qkv)
    grad_from_one, grad_gain_one, grad_shift_one = norm_grad(
        grad_norm_one, unit_one, inverse_one, gain_rows[0]
    )
    grad_inputs = grad_middle + grad_from_one
    block_grads = (
        jnp.stack([grad_gain_one, grad_gain_two]),
        jnp.stack([grad_shift_one, grad_shift_two]),
        grad_qkv,
        grad_out,
        jnp.stack([grad_bias_one, grad_bias_two]),
        grad_up,
        grad_bias_up,
        grad_down,
    )
    return (grad_inputs, block_grads)


def unpack_group(flat_row, grad_values, axis_values, block_count):
    portions = []
    offset = 0
    for grad_value, axis_dim in zip(grad_values, axis_values):
        reordered = jnp.moveaxis(grad_value, axis_dim, 0)
        local_shape = (reordered.shape[0] // block_count,) + reordered.shape[1:]
        length = math.prod(local_shape)
        portion = flat_row[offset : offset + length].reshape(local_shape)
        portions.append(jnp.moveaxis(portion, 0, axis_dim))
        offset += length
    return portions


def zero_floats(arrays):
    return tuple((jnp.zeros(array.shape, jnp.float32) for array in arrays))


def local(
    patches,
    visible,
    source,
    enc_gains,
    enc_shifts,
    enc_qkv,
    enc_out,
    enc_bias_out,
    enc_up,
    enc_bias_up,
    enc_down,
    enc_proj,
    proj_bias,
    mask_token,
    dec_gains,
    dec_shifts,
    dec_qkv,
    dec_out,
    dec_bias_out,
    dec_up,
    dec_bias_up,
    dec_down,
    cotangent,
):
    section_index = lax.axis_index("section")
    on_encoder = section_index == 0
    strip_count = patches.shape[0]
    strip_len = patches.shape[1]
    enc_width = patches.shape[2]
    dec_width = dec_qkv.shape[0]
    per_micro = strip_count // MICRO
    enc_gain_f = enc_gains.astype(jnp.float32)
    enc_shift_f = enc_shifts.astype(jnp.float32)
    enc_weights = (
        enc_gain_f,
        enc_shift_f,
        enc_qkv,
        enc_out,
        enc_bias_out.astype(jnp.float32),
        enc_up,
        enc_bias_up.astype(jnp.float32),
        enc_down,
    )
    dec_weights = (
        dec_gains.astype(jnp.float32),
        dec_shifts.astype(jnp.float32),
        dec_qkv,
        dec_out,
        dec_bias_out.astype(jnp.float32),
        dec_up,
        dec_bias_up.astype(jnp.float32),
        dec_down,
    )
    bias_proj = proj_bias.astype(jnp.float32)
    mask_row = mask_token.astype(jnp.float32)
    positions = jnp.arange(strip_len, dtype=jnp.int32)
    places = place_table(strip_len, dec_width)
    send_shape = (per_micro, strip_len, enc_width)
    enc_sums = zero_floats(
        (enc_gains, enc_shifts, enc_qkv, enc_out, enc_bias_out, enc_up, enc_bias_up, enc_down)
    )
    mid_sums = zero_floats((enc_proj, proj_bias))
    dec_sums = zero_floats(
        (
            dec_gains,
            dec_shifts,
            dec_qkv,
            dec_out,
            dec_bias_out,
            dec_up,
            dec_bias_up,
            dec_down,
            mask_token,
        )
    )
    decoded_parts = []
    grad_parts = []
    for micro_step in range(MICRO):
        start_row = micro_step * per_micro
        end_row = start_row + per_micro
        enc_valid = positions[None, :] < visible[start_row:end_row][:, None]
        dec_source = source[start_row:end_row]
        dec_valid = jnp.ones(dec_source.shape, dtype=jnp.bool_)

        def encode_step(unused):
            enc_in = patches[start_row:end_row].astype(jnp.float32)
            enc_result, enc_kept = block_forward(enc_in, enc_valid, enc_weights, HEADS_ENC)
            final_normed, final_unit, final_inverse = apply_norm(
                enc_result, enc_gain_f[2], enc_shift_f[2]
            )
            encoded = final_normed.astype(jnp.bfloat16)
            return (encoded, (encoded, enc_kept, final_unit, final_inverse))

        def encode_spare(unused):
            return (
                jnp.zeros(send_shape, jnp.bfloat16),
                kept_zeros(per_micro, strip_len, enc_width, HEADS_ENC, enc_up.shape[1]),
            )

        outgoing, kept_all = lax.cond(on_encoder, encode_step, encode_spare, 0)
        arrived = from_behind(outgoing, "section", 1)

        def decode_step(carry):
            dec_carry, mid_carry = carry
            rows_in = (forward_product(arrived, enc_proj) + bias_proj).astype(jnp.bfloat16)
            picker = (dec_source[:, :, None] == positions[None, None, :]).astype(jnp.bfloat16)
            missing = (dec_source < 0).astype(jnp.float32)[:, :, None]
            dec_in = (
                jnp.einsum("bjr,brc->bjc", picker, rows_in, preferred_element_type=jnp.float32)
                + missing * mask_row
                + places
            )
            dec_result, dec_kept = block_forward(dec_in, dec_valid, dec_weights, HEADS_DEC)
            grad_dec_in, dec_grads = block_backward(
                cotangent[start_row:end_row].astype(jnp.float32),
                dec_kept,
                dec_weights,
                dec_valid,
                HEADS_DEC,
            )
            grad_mask = jnp.sum(grad_dec_in * missing, axis=(0, 1))
            grad_rows = jnp.einsum(
                "bjr,bjc->brc",
                picker.astype(jnp.float32),
                grad_dec_in,
                preferred_element_type=jnp.float32,
            ).astype(jnp.bfloat16)
            grad_proj = weight_product(arrived, grad_rows)
            grad_bias_proj = jnp.sum(grad_rows.astype(jnp.float32), axis=(0, 1))
            back_rows = backward_product(grad_rows, enc_proj).astype(jnp.bfloat16)
            mid_carry = (mid_carry[0] + grad_proj, mid_carry[1] + grad_bias_proj)
            dec_carry = tuple(
                (earlier + later for earlier, later in zip(dec_carry, dec_grads + (grad_mask,)))
            )
            return (back_rows, dec_result.astype(jnp.bfloat16), dec_carry, mid_carry)

        def decode_spare(carry):
            return (
                jnp.zeros(send_shape, jnp.bfloat16),
                jnp.zeros((per_micro, strip_len, dec_width), jnp.bfloat16),
                carry[0],
                carry[1],
            )

        back_rows, decoded_micro, dec_sums, mid_sums = lax.cond(
            on_encoder, decode_spare, decode_step, (dec_sums, mid_sums)
        )
        decoded_parts.append(decoded_micro)
        returned = from_behind(back_rows, "section", -1)

        def encode_back(carry):
            enc_carry, mid_carry = carry
            encoded, enc_kept, final_unit, final_inverse = kept_all
            grad_enc_result, grad_gain_final, grad_shift_final = norm_grad(
                returned.astype(jnp.float32), final_unit, final_inverse, enc_gain_f[2]
            )
            grad_inputs, enc_grads = block_backward(
                grad_enc_result, enc_kept, enc_weights, enc_valid, HEADS_ENC
            )
            micro_grads = (
                jnp.concatenate([enc_grads[0], grad_gain_final[None]], axis=0),
                jnp.concatenate([enc_grads[1], grad_shift_final[None]], axis=0),
            ) + enc_grads[2:]
            enc_carry = tuple((earlier + later for earlier, later in zip(enc_carry, micro_grads)))
            return (grad_inputs.astype(jnp.bfloat16), enc_carry, mid_carry)

        def back_spare(carry):
            return (jnp.zeros((per_micro, strip_len, enc_width), jnp.bfloat16), carry[0], carry[1])

        grad_micro, enc_sums, mid_sums = lax.cond(
            on_encoder, encode_back, back_spare, (enc_sums, mid_sums)
        )
        grad_parts.append(grad_micro)
    patch_full = jnp.concatenate(grad_parts, axis=0)
    decoded_full = jnp.concatenate(decoded_parts, axis=0)
    half_enc = enc_width // 2
    half_dec = dec_width // 2
    outgoing_halves = jnp.concatenate(
        [patch_full[..., half_enc:], decoded_full[..., :half_dec]], axis=-1
    )
    arrived_halves = swapped(outgoing_halves, "section", 0)
    patch_grad = jnp.where(on_encoder, patch_full[..., :half_enc], arrived_halves[..., :half_enc])
    decoded = jnp.where(on_encoder, arrived_halves[..., half_enc:], decoded_full[..., half_dec:])
    axis_list = (1, 1, 0, 0, 1, 0, 0, 0, 0, 0, 0, 1, 1, 0, 0, 1, 0, 0, 0)
    grad_list = list(enc_sums) + list(mid_sums) + [dec_sums[8]] + list(dec_sums[:8])
    dp_count = lax.axis_size("dp")
    block_count = 2 * dp_count
    flat_all = jnp.concatenate(
        [
            jnp.moveaxis(grad_value, axis_dim, 0).reshape(block_count, -1)
            for grad_value, axis_dim in zip(grad_list, axis_list)
        ],
        axis=1,
    )
    summed = lax.psum_scatter(flat_all, ("section", "dp"), scatter_dimension=0, tiled=True)
    finals = unpack_group(summed[0], grad_list, axis_list, block_count)
    return (decoded, patch_grad) + tuple(finals)


def solution(mesh):
    return jax.shard_map(
        local,
        mesh=mesh,
        in_specs=(
            P("dp", None, None),
            P("dp"),
            P("dp", None),
            P(),
            P(),
            P(),
            P(),
            P(),
            P(),
            P(),
            P(),
            P(),
            P(),
            P(),
            P(),
            P(),
            P(),
            P(),
            P(),
            P(),
            P(),
            P(),
            P("dp", None, None),
        ),
        out_specs=(
            P("dp", None, "section"),
            P("dp", None, "section"),
            P(None, ("section", "dp")),
            P(None, ("section", "dp")),
            P(("section", "dp"), None),
            P(("section", "dp"), None),
            P(None, ("section", "dp")),
            P(("section", "dp"), None),
            P(("section", "dp")),
            P(("section", "dp"), None),
            P(("section", "dp"), None),
            P(("section", "dp")),
            P(("section", "dp")),
            P(None, ("section", "dp")),
            P(None, ("section", "dp")),
            P(("section", "dp"), None),
            P(("section", "dp"), None),
            P(None, ("section", "dp")),
            P(("section", "dp"), None),
            P(("section", "dp")),
            P(("section", "dp"), None),
        ),
        check_vma=False,
    )
```

profile of v0, /device:TPU:0, one launch (start us, length us, event | category | flops | bytes accessed | tf_op | source)
XLA Modules:
  0.0 1831.9 jit_solution(18380059373321517530)
XLA Ops:
  12.7 73.3 %conditional.12 = (bf16[1,529,768]{2,1,0:T(8,128)(2,1)}, f32[1,529,768]{2,1,0:T(8,128)}, f32[1,529,1]{1,2,0:T(1,128)S(1)}, bf16[1,529,768]{2,1,0:T(8,128)(2,1)},...) conditional(s32[]{:T(128)} %convert_element_type.828, ...), branch_computations={%region_0.0_spmd, %region_1.10_spmd} | conditional | flops 8511463424 | bytes 206905952 | solution.py:367
  26.1 10.7 fusion
  60.3 20.3 %add_bitcast_fusion = (f32[1,529,3072]{2,1,0:T(8,128)}, bf16[529,3072]{1,0:T(8,128)(2,1)S(1)}) fusion(f32[3072]{0:T(1024)S(1)} %copy-done.260, bf16[768,3072]{1,0:T(8,128)(2,1)S(1)} %bitcast.1344, bf16[1,529,768]{2,1,0:T(8,128)(2,1)} %get-tuple-element.2822), kind=kOutput, calls=%fused_computation.25 | convolution fusion | flops 2603390976 | bytes 15293952 | tf_op jit(solution)/shard_map/cond/branch_1_fun/bld,df->blf/dot_general | solution.py:63
  89.5 74.2 %conditional.15 = (bf16[1,529,768]{2,1,0:T(8,128)(2,1)}, f32[1,529,768]{2,1,0:T(8,128)}, f32[1,529,1]{1,2,0:T(1,128)S(1)}, bf16[1,529,768]{2,1,0:T(8,128)(2,1)},...) conditional(s32[]{:T(128)} %convert_element_type.828, ...), branch_computations={%region_50.51_spmd, %region_51.60_spmd} | conditional | flops 8511463424 | bytes 203655744 | solution.py:367
  103.1 10.7 fusion.150
  138.2 20.3 %add_bitcast_fusion.1 = (f32[1,529,3072]{2,1,0:T(8,128)}, bf16[529,3072]{1,0:T(8,128)(2,1)S(1)}) fusion(f32[3072]{0:T(1024)S(1)} %copy-done.261, bf16[768,3072]{1,0:T(8,128)(2,1)S(1)} %bitcast.1346, bf16[1,529,768]{2,1,0:T(8,128)(2,1)} %get-tuple-element.2792), kind=kOutput, calls=%fused_computation.306 | convolution fusion | flops 2603390976 | bytes 15293952 | tf_op jit(solution)/shard_map/cond/branch_1_fun/bld,df->blf/dot_general | solution.py:63
  167.3 74.3 %conditional.18 = (bf16[1,529,768]{2,1,0:T(8,128)(2,1)}, f32[1,529,768]{2,1,0:T(8,128)}, f32[1,529,1]{1,2,0:T(1,128)S(1)}, bf16[1,529,768]{2,1,0:T(8,128)(2,1)},...) conditional(s32[]{:T(128)} %convert_element_type.828, ...), branch_computations={%region_100.101_spmd, %region_101.110_spmd} | conditional | flops 8511463424 | bytes 203655744 | solution.py:367
  215.6 20.6 %add_bitcast_fusion.2 = (f32[1,529,3072]{2,1,0:T(8,128)}, bf16[529,3072]{1,0:T(8,128)(2,1)S(1)}) fusion(f32[3072]{0:T(1024)S(1)} %copy-done.262, bf16[768,3072]{1,0:T(8,128)(2,1)S(1)} %bitcast.1348, bf16[1,529,768]{2,1,0:T(8,128)(2,1)} %get-tuple-element.2762), kind=kOutput, calls=%fused_computation.587 | convolution fusion | flops 2603390976 | bytes 15293952 | tf_op jit(solution)/shard_map/cond/branch_1_fun/bld,df->blf/dot_general | solution.py:63
  245.0 80.1 %conditional.21 = (bf16[1,529,768]{2,1,0:T(8,128)(2,1)}, f32[1,529,768]{2,1,0:T(8,128)}, f32[1,529,1]{1,2,0:T(1,128)S(1)}, bf16[1,529,768]{2,1,0:T(8,128)(2,1)},...) conditional(s32[]{:T(128)} %convert_element_type.828, ...), branch_computations={%region_150.151_spmd, %region_151.160_spmd} | conditional | flops 8511463424 | bytes 200340896 | solution.py:367
  260.3 11.6 fusion.442
  283.1 11.3 fusion.461
  299.4 20.1 %add_bitcast_fusion.3 = (f32[1,529,3072]{2,1,0:T(8,128)}, bf16[529,3072]{1,0:T(8,128)(2,1)S(1)}) fusion(f32[3072]{0:T(1024)S(1)} %copy-done.263, bf16[768,3072]{1,0:T(8,128)(2,1)S(1)} %bitcast.1350, bf16[1,529,768]{2,1,0:T(8,128)(2,1)} %get-tuple-element.2732), kind=kOutput, calls=%fused_computation.868 | convolution fusion | flops 2603390976 | bytes 15293952 | tf_op jit(solution)/shard_map/cond/branch_1_fun/bld,df->blf/dot_general | solution.py:63
  337.6 16.0 conditional.13
  372.2 30.9 %conditional.22 = (bf16[1,529,768]{2,1,0:T(8,128)(2,1)}, f32[2,512]{1,0:T(2,128)S(1)}, f32[2,512]{1,0:T(2,128)S(1)}, f32[2,512]{1,0:T(2,128)S(1)}, f32[32,24576]...) conditional(s32[]{:T(128)} %convert_element_type.828, ...), branch_computations={%region_160.181_spmd, %region_181.182_spmd} | conditional | flops 13717383168 | bytes 400047200 | solution.py:412
  407.1 124.6 %conditional.14 = (f32[3,768]{1,0:T(4,128)}, f32[3,768]{1,0:T(4,128)}, f32[768,2304]{0,1:T(8,128)S(1)}, f32[768,768]{0,1:T(8,128)S(1)}, f32[2,768]{1,0:T(2,128)}...) conditional(s32[]{:T(128)} %convert_element_type.828, ...), branch_computations={%region_32.33_spmd, %region_33.50_spmd} | conditional | flops 17318418432 | bytes 444978720 | solution.py:437
  413.6 20.2 %convert_reduce_fusion.5 = (f32[3072]{0:T(1024)}, bf16[1,529,3072]{2,1,0:T(8,128)(2,1)S(1)}) fusion(f32[1,529,3072]{2,1,0:T(8,128)} %get-tuple-element.652, bf16[3072,768]{1,0:T(8,128)(2,1)} %get-tuple-element.653, f32[1,529,768]{2,1,0:T(8,128)S(1)} %get-tuple-element.2458), kind=kOutput, calls=%fused_computation.197 | convolution fusion | flops 2616794880 | bytes 16106496 | tf_op jit(solution)/shard_map/cond/branch_1_fun/blf,df->bld/dot_general | solution.py:67
  538.4 140.4 %conditional.17 = (f32[3,768]{1,0:T(4,128)}, f32[3,768]{1,0:T(4,128)}, f32[768,2304]{0,1:T(8,128)}, f32[768,768]{0,1:T(8,128)}, f32[2,768]{1,0:T(2,128)}, /*inde...) conditional(s32[]{:T(128)} %convert_element_type.828, ...), branch_computations={%region_82.83_spmd, %region_83.100_spmd} | conditional | flops 17325508608 | bytes 558421120 | solution.py:437
  546.2 20.2 %convert_reduce_fusion.14 = (f32[3072]{0:T(1024)}, bf16[1,529,3072]{2,1,0:T(8,128)(2,1)S(1)}) fusion(f32[1,529,3072]{2,1,0:T(8,128)} %get-tuple-element.730, bf16[3072,768]{1,0:T(8,128)(2,1)} %get-tuple-element.731, f32[1,529,768]{2,1,0:T(8,128)S(1)} %get-tuple-element.2462), kind=kOutput, calls=%fused_computation.481 | convolution fusion | flops 2616794880 | bytes 16106496 | tf_op jit(solution)/shard_map/cond/branch_1_fun/blf,df->bld/dot_general | solution.py:67
  644.8 10.7 bitcast_add_fusion.7
  678.9 140.5 %conditional.20 = (f32[3,768]{1,0:T(4,128)}, f32[3,768]{1,0:T(4,128)}, f32[768,2304]{0,1:T(8,128)}, f32[768,768]{0,1:T(8,128)}, f32[2,768]{1,0:T(2,128)}, /*inde...) conditional(s32[]{:T(128)} %convert_element_type.828, ...), branch_computations={%region_132.133_spmd, %region_133.150_spmd} | conditional | flops 17325508608 | bytes 558319488 | solution.py:437
  686.7 20.2 %convert_reduce_fusion.23 = (f32[3072]{0:T(1024)}, bf16[1,529,3072]{2,1,0:T(8,128)(2,1)S(1)}) fusion(f32[1,529,3072]{2,1,0:T(8,128)} %get-tuple-element.816, bf16[3072,768]{1,0:T(8,128)(2,1)} %get-tuple-element.817, f32[1,529,768]{2,1,0:T(8,128)S(1)} %get-tuple-element.2466), kind=kOutput, calls=%fused_computation.762 | convolution fusion | flops 2616794880 | bytes 16106496 | tf_op jit(solution)/shard_map/cond/branch_1_fun/blf,df->bld/dot_general | solution.py:67
  785.3 10.7 bitcast_add_fusion.14
  819.4 12.6 collective-permute-done.7
  832.0 139.3 %conditional.23 = (f32[3,768]{1,0:T(4,128)}, f32[3,768]{1,0:T(4,128)}, f32[768,2304]{0,1:T(8,128)}, f32[768,768]{0,1:T(8,128)}, f32[2,768]{1,0:T(2,128)}, /*inde...) conditional(s32[]{:T(128)} %convert_element_type.828, ...), branch_computations={%region_182.183_spmd, %region_183.200_spmd} | conditional | flops 17325508608 | bytes 558258048 | solution.py:437
  839.7 19.6 %convert_reduce_fusion.32 = (f32[3072]{0:T(1024)S(1)}, bf16[1,529,3072]{2,1,0:T(8,128)(2,1)S(1)}) fusion(f32[1,529,3072]{2,1,0:T(8,128)} %get-tuple-element.902, bf16[3072,768]{1,0:T(8,128)(2,1)} %get-tuple-element.903, f32[1,529,768]{2,1,0:T(8,128)S(1)} %get-tuple-element.2470), kind=kOutput, calls=%fused_computation.1043 | convolution fusion | flops 2616794880 | bytes 16106496 | tf_op jit(solution)/shard_map/cond/branch_1_fun/blf,df->bld/dot_general | solution.py:67
  937.3 10.7 bitcast_add_fusion.21
  1032.2 20.5 %dynamic-update-slice.2 = f32[32,332256]{1,0:T(8,128)} dynamic-update-slice(f32[32,332256]{1,0:T(8,128)} %dynamic-update-slice.1, f32[32,55296]{1,0:T(8,128)} %reshape.4129, s32[]{} %constant.1172, s32[]{} %constant.1174) | dynamic-update-slice | bytes 14155780
  1063.1 28.7 %dynamic-update-slice.5 = f32[32,332256]{1,0:T(8,128)} dynamic-update-slice(f32[32,332256]{1,0:T(8,128)} %dynamic-update-slice.4, f32[32,73728]{1,0:T(8,128)} %reshape.4132, s32[]{} %constant.1172, s32[]{} %constant.1177) | dynamic-update-slice | bytes 18874372
  1093.4 28.8 %dynamic-update-slice.7 = f32[32,332256]{1,0:T(8,128)} dynamic-update-slice(f32[32,332256]{1,0:T(8,128)} %dynamic-update-slice.6, f32[32,73728]{1,0:T(8,128)} %reshape.4134, s32[]{} %constant.1172, s32[]{} %constant.1179) | dynamic-update-slice | bytes 18874372
  1139.4 14.8 dynamic-update-slice.16
  1155.7 14.2 dynamic-update-slice.18
  1204.2 589.9 %all-reduce.3.cloned.1.call-done = f32[32,332256]{1,0:T(8,128)} async-done(((f32[32,332256]{1,0:T(8,128)}), f32[32,332256]{1,0:T(8,128)}) %all-reduce.3.cloned.1.call-update) | async-done | bytes 42528784
  (950 shorter events, 853.8 us)
Async XLA Ops:
  7.2 1787.0 %all-reduce.3.cloned.1.call-start = ((), (), s32[]{:S(2)}) async-start(), calls=%async_computation | async-start | bytes 85065728
  7.9 236.6 %copy-start.150 = (f32[3,768]{1,0:T(4,128)}, f32[3,768]{1,0:T(4,128)S(1)}, u32[]{:S(2)}) copy-start(f32[3,768]{1,0:T(4,128)S(1)} %convert_element_type.829) | copy-start | bytes 27652
  86.1 251.5 %collective-permute-start = (bf16[1,529,768]{2,1,0:T(8,128)(2,1)}, bf16[1,529,768]{2,1,0:T(8,128)(2,1)}, u32[]{:S(2)}, u32[]{:S(2)}) collective-permute-start(bf16[1,529,768]{2,1,0:T(8,128)(2,1)} %get-tuple-element.1096), channel_id=1, source_target_pairs={{0,16},{1,17},{2,18},{3,19},{4,20},{5,21},{6,22},{7,23},{8,24},{9,... | collective-permute-start | bytes 2437640 | tf_op jit(solution)/shard_map/ppermute | solution.py:19
  163.8 191.1 %collective-permute-start.2 = (bf16[1,529,768]{2,1,0:T(8,128)(2,1)}, bf16[1,529,768]{2,1,0:T(8,128)(2,1)}, u32[]{:S(2)}, u32[]{:S(2)}) collective-permute-start(bf16[1,529,768]{2,1,0:T(8,128)(2,1)} %get-tuple-element.1121), channel_id=1, source_target_pairs={{0,16},{1,17},{2,18},{3,19},{4,20},{5,21},{6,22},{7,23},{8,24},{9,... | collective-permute-start | bytes 2437640 | tf_op jit(solution)/shard_map/ppermute | solution.py:19
  241.6 119.7 %collective-permute-start.4 = (bf16[1,529,768]{2,1,0:T(8,128)(2,1)}, bf16[1,529,768]{2,1,0:T(8,128)(2,1)}, u32[]{:S(2)}, u32[]{:S(2)}) collective-permute-start(bf16[1,529,768]{2,1,0:T(8,128)(2,1)} %get-tuple-element.1157), channel_id=1, source_target_pairs={{0,16},{1,17},{2,18},{3,19},{4,20},{5,21},{6,22},{7,23},{8,24},{9,... | collective-permute-start | bytes 2437640 | tf_op jit(solution)/shard_map/ppermute | solution.py:19
  244.5 93.1 %copy-start.16 = (bf16[4,529,512]{2,0,1:T(4,128)(2,1)S(1)}, bf16[4,529,512]{2,0,1:T(4,128)(2,1)}, u32[]{:S(2)}) copy-start(bf16[4,529,512]{2,0,1:T(4,128)(2,1)} %param.69) | copy-start | bytes 6500356
  244.5 93.1 %copy-start.17 = (bf16[512,512]{1,0:T(8,128)(2,1)S(1)}, bf16[512,512]{1,0:T(8,128)(2,1)}, u32[]{:S(2)}) copy-start(bf16[512,512]{1,0:T(8,128)(2,1)} %param.64) | copy-start | bytes 1572868
  325.1 47.0 %collective-permute-start.6 = (bf16[1,529,768]{2,1,0:T(8,128)(2,1)}, bf16[1,529,768]{2,1,0:T(8,128)(2,1)}, u32[]{:S(2)}, u32[]{:S(2)}) collective-permute-start(bf16[1,529,768]{2,1,0:T(8,128)(2,1)} %get-tuple-element.1193), channel_id=1, source_target_pairs={{0,16},{1,17},{2,18},{3,19},{4,20},{5,21},{6,22},{7,23},{8,24},{9,... | collective-permute-start | bytes 2437640 | tf_op jit(solution)/shard_map/ppermute | solution.py:19
  353.6 53.4 %collective-permute-start.1 = (bf16[1,529,768]{2,1,0:T(8,128)(2,1)}, bf16[1,529,768]{2,1,0:T(8,128)(2,1)}, u32[]{:S(2)}, u32[]{:S(2)}) collective-permute-start(bf16[1,529,768]{2,1,0:T(8,128)(2,1)} %get-tuple-element.1097), channel_id=1, source_target_pairs={{16,0},{17,1},{18,2},{19,3},{20,4},{21,5},{22,6},{23,7},{24,8},{25... | collective-permute-start | bytes 2437640 | tf_op jit(solution)/shard_map/ppermute | solution.py:19
  360.0 171.8 %collective-permute-start.3 = (bf16[1,529,768]{2,1,0:T(8,128)(2,1)}, bf16[1,529,768]{2,1,0:T(8,128)(2,1)}, u32[]{:S(2)}, u32[]{:S(2)}) collective-permute-start(bf16[1,529,768]{2,1,0:T(8,128)(2,1)} %get-tuple-element.1133), channel_id=1, source_target_pairs={{16,0},{17,1},{18,2},{19,3},{20,4},{21,5},{22,6},{23,7},{24,8},{25... | collective-permute-start | bytes 2437640 | tf_op jit(solution)/shard_map/ppermute | solution.py:19
  370.8 308.1 %collective-permute-start.5 = (bf16[1,529,768]{2,1,0:T(8,128)(2,1)}, bf16[1,529,768]{2,1,0:T(8,128)(2,1)}, u32[]{:S(2)}, u32[]{:S(2)}) collective-permute-start(bf16[1,529,768]{2,1,0:T(8,128)(2,1)} %get-tuple-element.1169), channel_id=1, source_target_pairs={{16,0},{17,1},{18,2},{19,3},{20,4},{21,5},{22,6},{23,7},{24,8},{25... | collective-permute-start | bytes 2437640 | tf_op jit(solution)/shard_map/ppermute | solution.py:19
  372.1 35.0 %copy-start.151 = (f32[3,768]{1,0:T(4,128)S(1)}, f32[3,768]{1,0:T(4,128)}, u32[]{:S(2)}) copy-start(f32[3,768]{1,0:T(4,128)} %copy-done.150) | copy-start | bytes 27652
  372.1 34.9 %copy-start.222 = (pred[1,529]{1,0:T(4,128)(4,1)S(1)}, pred[1,529]{1,0:T(4,128)(4,1)}, u32[]{:S(2)}) copy-start(pred[1,529]{1,0:T(4,128)(4,1)} %copy-done.221) | copy-start | bytes 1591
  372.1 34.9 %copy-start.269 = (f32[1,529,1]{1,2,0:T(1,128)S(1)}, f32[1,529,1]{1,2,0:T(1,128)}, u32[]{:S(2)}) copy-start(f32[1,529,1]{1,2,0:T(1,128)} %copy-done.268) | copy-start | bytes 6352
  372.1 34.9 %copy-start.271 = (f32[1,529,1]{1,2,0:T(1,128)S(1)}, f32[1,529,1]{1,2,0:T(1,128)}, u32[]{:S(2)}) copy-start(f32[1,529,1]{1,2,0:T(1,128)} %copy-done.270) | copy-start | bytes 6352
  403.0 428.9 %collective-permute-start.7 = (bf16[1,529,768]{2,1,0:T(8,128)(2,1)}, bf16[1,529,768]{2,1,0:T(8,128)(2,1)}, u32[]{:S(2)}, u32[]{:S(2)}) collective-permute-start(bf16[1,529,768]{2,1,0:T(8,128)(2,1)} %get-tuple-element.1205), channel_id=1, source_target_pairs={{16,0},{17,1},{18,2},{19,3},{20,4},{21,5},{22,6},{23,7},{24,8},{25... | collective-permute-start | bytes 2437640 | tf_op jit(solution)/shard_map/ppermute | solution.py:19
  407.1 131.4 %copy-start.220 = (pred[1,529]{1,0:T(4,128)(4,1)S(1)}, pred[1,529]{1,0:T(4,128)(4,1)}, u32[]{:S(2)}) copy-start(pred[1,529]{1,0:T(4,128)(4,1)} %copy-done.219) | copy-start | bytes 1591
  410.8 23.1 %slice-start.17 = ((s8[4718592]{0:T(1024)(128)(4,1)}), s8[4194304]{0:T(1024)(128)(4,1)S(1)}, s32[]{:S(2)}) async-start(s8[4718592]{0:T(1024)(128)(4,1)} %bitcast.1351), calls=%async_computation.18 | async-start | bytes 8388608 | tf_op jit(solution)/shard_map/cond
  413.6 27.2 %copy-start.50 = (f32[1,529,768]{2,1,0:T(8,128)}, f32[1,529,768]{2,1,0:T(8,128)S(1)}, u32[]{:S(2)}) copy-start(f32[1,529,768]{2,1,0:T(8,128)S(1)} %get-tuple-element.2458) | copy-start | bytes 4875268 | tf_op jit(solution)/shard_map/cond
  538.4 140.4 %copy-start.156 = (f32[1,12,529,1]{2,1,3,0:T(8,128)S(1)}, f32[1,12,529,1]{2,1,3,0:T(8,128)}, u32[]{:S(2)}) copy-start(f32[1,12,529,1]{2,1,3,0:T(8,128)} %get-tuple-element.1176) | copy-start | bytes 76180
  538.4 140.4 %copy-start.218 = (pred[1,529]{1,0:T(4,128)(4,1)S(1)}, pred[1,529]{1,0:T(4,128)(4,1)}, u32[]{:S(2)}) copy-start(pred[1,529]{1,0:T(4,128)(4,1)} %copy-done.217) | copy-start | bytes 1591
  543.4 23.1 %slice-start.19 = ((s8[4718592]{0:T(1024)(128)(4,1)}), s8[4194304]{0:T(1024)(128)(4,1)S(1)}, s32[]{:S(2)}) async-start(s8[4718592]{0:T(1024)(128)(4,1)} %bitcast.1353), calls=%async_computation.20 | async-start | bytes 8388608 | tf_op jit(solution)/shard_map/cond
  546.2 26.7 %copy-start.33 = (f32[1,529,768]{2,1,0:T(8,128)}, f32[1,529,768]{2,1,0:T(8,128)S(1)}, u32[]{:S(2)}) copy-start(f32[1,529,768]{2,1,0:T(8,128)S(1)} %get-tuple-element.2462) | copy-start | bytes 4875268 | tf_op jit(solution)/shard_map/cond
  678.9 153.1 %copy-start.216 = (pred[1,529]{1,0:T(4,128)(4,1)S(1)}, pred[1,529]{1,0:T(4,128)(4,1)}, u32[]{:S(2)}) copy-start(pred[1,529]{1,0:T(4,128)(4,1)} %copy-done.215) | copy-start | bytes 1591
  683.9 23.1 %slice-start.21 = ((s8[4718592]{0:T(1024)(128)(4,1)}), s8[4194304]{0:T(1024)(128)(4,1)S(1)}, s32[]{:S(2)}) async-start(s8[4718592]{0:T(1024)(128)(4,1)} %bitcast.1355), calls=%async_computation.22 | async-start | bytes 8388608 | tf_op jit(solution)/shard_map/cond
  686.7 26.8 %copy-start.35 = (f32[1,529,768]{2,1,0:T(8,128)}, f32[1,529,768]{2,1,0:T(8,128)S(1)}, u32[]{:S(2)}) copy-start(f32[1,529,768]{2,1,0:T(8,128)S(1)} %get-tuple-element.2466) | copy-start | bytes 4875268 | tf_op jit(solution)/shard_map/cond
  839.7 25.6 %copy-start.37 = (f32[1,529,768]{2,1,0:T(8,128)}, f32[1,529,768]{2,1,0:T(8,128)S(1)}, u32[]{:S(2)}) copy-start(f32[1,529,768]{2,1,0:T(8,128)S(1)} %get-tuple-element.2470) | copy-start | bytes 4875268 | tf_op jit(solution)/shard_map/cond
  1093.4 35.6 %copy-start.189 = (f32[32,16]{1,0:T(8,128)S(1)}, f32[32,16]{1,0:T(8,128)}, u32[]{:S(2)}) copy-start(f32[32,16]{1,0:T(8,128)} %copy-done.188) | copy-start | bytes 6148
  1093.4 37.1 %copy-start.191 = (f32[32,16]{1,0:T(8,128)S(1)}, f32[32,16]{1,0:T(8,128)}, u32[]{:S(2)}) copy-start(f32[32,16]{1,0:T(8,128)} %copy-done.190) | copy-start | bytes 6148
  1093.4 38.6 %copy-start.186 = (f32[32,32]{1,0:T(8,128)S(1)}, f32[32,32]{1,0:T(8,128)}, u32[]{:S(2)}) copy-start(f32[32,32]{1,0:T(8,128)} %reshape.4135) | copy-start | bytes 12292
  1093.4 40.1 %copy-start.187 = (f32[32,32]{1,0:T(8,128)S(1)}, f32[32,32]{1,0:T(8,128)}, u32[]{:S(2)}) copy-start(f32[32,32]{1,0:T(8,128)} %reshape.4136) | copy-start | bytes 12292
  1192.1 5.4 collective-permute-start.8
  (227 other events, 1623.3 us)
Sparse Core Ops, SparseCore 0:
  1170.1 624.0 all-reduce.2
where the time goes:
time: 1840 us; the launch traced here: 1830 us
  waiting for transfers between devices  608 us (33%)
  matrix products  561 us (30%)
  local copies, waits for them, and re-layouts  398 us (22%)
  other arithmetic  206 us (11%)
  loops' own time  29.9 us (2%)
    unnamed x2, waiting for transfers between devices  590 us
    unnamed x128, local copies, waits for them, and re-layouts  142 us
    dot_general x16, matrix products, backward_product(): jnp.einsum('blf,df->bld', left_side, right_side, preferred_element_type=j...  130 us
    dot_general x16, matrix products, forward_product(): jnp.einsum('bld,df->blf', left_side, right_side, preferred_element_type=j...  112 us
    dot_general x16, matrix products, weight_product(): jnp.einsum('bld,blf->df', left_side, right_side, preferred_element_type=j...  102 us
    dot_general x8, matrix products, masked_scores(): jnp.einsum('bqhd,bkhd->bhqk', queries, key_rows, preferred_element_type=j...  83.2 us
    reshape x19, local copies, waits for them, and re-layouts, local(): jnp.moveaxis(grad_value, axis_dim, 0).reshape(block_count, -1)  46 us
    reduce_sum x4, other arithmetic, attend(): totals = jnp.sum(exp_terms, axis=-1, keepdims=True)  39.4 us
  transfers between devices with their start and end apart: 10, of which 3 were waited for; matrix products, arithmetic and copies ran while one was open for 37% of the time, Pallas kernels for 0%

commit v1 on v0

--- a/solution.py
+++ b/solution.py
@@ -7,26 +7,9 @@
 
 HEADS_ENC = 12
 HEADS_DEC = 16
-MICRO = 4
 
 
 epsilon = 1e-06
-
-
-def from_behind(value, axis, steps):
-    count = lax.axis_size(axis)
-    initial, last = (max(0, -steps), min(count, count - steps))
-    return lax.ppermute(value, axis, [(source, source + steps) for source in range(initial, last)])
-
-
-def swapped(block, axis, bit):
-    count = lax.axis_size(axis)
-    route = []
-    for low in range(count):
-        high = low | 1 << bit
-        if high != low and high < count:
-            route += [(low, high), (high, low)]
-    return lax.ppermute(block, axis, route)
 
 
 def apply_norm(values, gain_row, shift_row):
@@ -170,31 +153,6 @@
     )
 
 
-def kept_zeros(batch_size, length, model_width, head_count, hidden_units):
-    full_rows = (batch_size, length, model_width)
-    column = (batch_size, length, 1)
-    stats = (batch_size, head_count, length, 1)
-    block_kept = (
-        jnp.zeros(full_rows, jnp.float32),
-        jnp.zeros(column, jnp.float32),
-        jnp.zeros(full_rows, jnp.bfloat16),
-        jnp.zeros((batch_size, length, 3 * model_width), jnp.bfloat16),
-        jnp.zeros(full_rows, jnp.bfloat16),
-        (jnp.zeros(stats, jnp.float32), jnp.zeros(stats, jnp.float32)),
-        jnp.zeros(full_rows, jnp.float32),
-        jnp.zeros(column, jnp.float32),
-        jnp.zeros(full_rows, jnp.bfloat16),
-        jnp.zeros((batch_size, length, hidden_units), jnp.float32),
-        jnp.zeros((batch_size, length, hidden_units), jnp.bfloat16),
-    )
-    return (
-        jnp.zeros(full_rows, jnp.bfloat16),
-        block_kept,
-        jnp.zeros(full_rows, jnp.float32),
-        jnp.zeros(column, jnp.float32),
-    )
-
-
 def block_backward(grad_result, kept_values, weights, key_valid, head_count):
     gain_rows, shifts, w_qkv, w_out, bias_out, w_up, bias_up, w_down = weights
     (
@@ -247,21 +205,33 @@
     return (grad_inputs, block_grads)
 
 
-def unpack_group(flat_row, grad_values, axis_values, block_count):
+def row_scatter(grad_value):
+    rows, width = grad_value.shape
+    count = lax.axis_size("section") * lax.axis_size("dp")
+    blocks = grad_value.astype(jnp.bfloat16).reshape(count, rows // count, width)
+    out = lax.psum_scatter(blocks, ("section", "dp"), scatter_dimension=0, tiled=True)
+    return out.reshape(rows // count, width).astype(jnp.float32)
+
+
+def small_scatter(grad_values, axis_values):
+    count = lax.axis_size("section") * lax.axis_size("dp")
+    flat = jnp.concatenate(
+        [
+            jnp.moveaxis(grad_value, axis_dim, 0).reshape(count, -1)
+            for grad_value, axis_dim in zip(grad_values, axis_values)
+        ],
+        axis=1,
+    )
+    summed = lax.psum_scatter(flat, ("section", "dp"), scatter_dimension=0, tiled=True)[0]
     portions = []
     offset = 0
     for grad_value, axis_dim in zip(grad_values, axis_values):
-        reordered = jnp.moveaxis(grad_value, axis_dim, 0)
-        local_shape = (reordered.shape[0] // block_count,) + reordered.shape[1:]
+        shape = jnp.moveaxis(grad_value, axis_dim, 0).shape
+        local_shape = (shape[0] // count,) + shape[1:]
         length = math.prod(local_shape)
-        portion = flat_row[offset : offset + length].reshape(local_shape)
-        portions.append(jnp.moveaxis(portion, 0, axis_dim))
+        portions.append(jnp.moveaxis(summed[offset : offset + length].reshape(local_shape), 0, axis_dim))
         offset += length
     return portions
-
-
-def zero_floats(arrays):
-    return tuple((jnp.zeros(array.shape, jnp.float32) for array in arrays))
 
 
 def local(
@@ -290,12 +260,12 @@
     cotangent,
 ):
     section_index = lax.axis_index("section")
-    on_encoder = section_index == 0
-    strip_count = patches.shape[0]
     strip_len = patches.shape[1]
     enc_width = patches.shape[2]
     dec_width = dec_qkv.shape[0]
-    per_micro = strip_count // MICRO
+    mine = patches.shape[0] // 2
+    take = lambda array: lax.dynamic_slice_in_dim(array, section_index * mine, mine, 0)
+    patches, visible, source, cotangent = map(take, (patches, visible, source, cotangent))
     enc_gain_f = enc_gains.astype(jnp.float32)
     enc_shift_f = enc_shifts.astype(jnp.float32)
     enc_weights = (
@@ -322,146 +292,101 @@
     mask_row = mask_token.astype(jnp.float32)
     positions = jnp.arange(strip_len, dtype=jnp.int32)
     places = place_table(strip_len, dec_width)
-    send_shape = (per_micro, strip_len, enc_width)
-    enc_sums = zero_floats(
-        (enc_gains, enc_shifts, enc_qkv, enc_out, enc_bias_out, enc_up, enc_bias_up, enc_down)
-    )
-    mid_sums = zero_floats((enc_proj, proj_bias))
-    dec_sums = zero_floats(
-        (
-            dec_gains,
-            dec_shifts,
-            dec_qkv,
-            dec_out,
-            dec_bias_out,
-            dec_up,
-            dec_bias_up,
-            dec_down,
-            mask_token,
-        )
-    )
-    decoded_parts = []
-    grad_parts = []
-    for micro_step in range(MICRO):
-        start_row = micro_step * per_micro
-        end_row = start_row + per_micro
-        enc_valid = positions[None, :] < visible[start_row:end_row][:, None]
-        dec_source = source[start_row:end_row]
-        dec_valid = jnp.ones(dec_source.shape, dtype=jnp.bool_)
-
-        def encode_step(unused):
-            enc_in = patches[start_row:end_row].astype(jnp.float32)
-            enc_result, enc_kept = block_forward(enc_in, enc_valid, enc_weights, HEADS_ENC)
-            final_normed, final_unit, final_inverse = apply_norm(
-                enc_result, enc_gain_f[2], enc_shift_f[2]
-            )
-            encoded = final_normed.astype(jnp.bfloat16)
-            return (encoded, (encoded, enc_kept, final_unit, final_inverse))
-
-        def encode_spare(unused):
-            return (
-                jnp.zeros(send_shape, jnp.bfloat16),
-                kept_zeros(per_micro, strip_len, enc_width, HEADS_ENC, enc_up.shape[1]),
-            )
-
-        outgoing, kept_all = lax.cond(on_encoder, encode_step, encode_spare, 0)
-        arrived = from_behind(outgoing, "section", 1)
-
-        def decode_step(carry):
-            dec_carry, mid_carry = carry
-            rows_in = (forward_product(arrived, enc_proj) + bias_proj).astype(jnp.bfloat16)
-            picker = (dec_source[:, :, None] == positions[None, None, :]).astype(jnp.bfloat16)
-            missing = (dec_source < 0).astype(jnp.float32)[:, :, None]
-            dec_in = (
-                jnp.einsum("bjr,brc->bjc", picker, rows_in, preferred_element_type=jnp.float32)
-                + missing * mask_row
-                + places
-            )
-            dec_result, dec_kept = block_forward(dec_in, dec_valid, dec_weights, HEADS_DEC)
-            grad_dec_in, dec_grads = block_backward(
-                cotangent[start_row:end_row].astype(jnp.float32),
-                dec_kept,
-                dec_weights,
-                dec_valid,
-                HEADS_DEC,
-            )
-            grad_mask = jnp.sum(grad_dec_in * missing, axis=(0, 1))
-            grad_rows = jnp.einsum(
-                "bjr,bjc->brc",
-                picker.astype(jnp.float32),
-                grad_dec_in,
-                preferred_element_type=jnp.float32,
-            ).astype(jnp.bfloat16)
-            grad_proj = weight_product(arrived, grad_rows)
-            grad_bias_proj = jnp.sum(grad_rows.astype(jnp.float32), axis=(0, 1))
-            back_rows = backward_product(grad_rows, enc_proj).astype(jnp.bfloat16)
-            mid_carry = (mid_carry[0] + grad_proj, mid_carry[1] + grad_bias_proj)
-            dec_carry = tuple(
-                (earlier + later for earlier, later in zip(dec_carry, dec_grads + (grad_mask,)))
-            )
-            return (back_rows, dec_result.astype(jnp.bfloat16), dec_carry, mid_carry)
-
-        def decode_spare(carry):
-            return (
-                jnp.zeros(send_shape, jnp.bfloat16),
-                jnp.zeros((per_micro, strip_len, dec_width), jnp.bfloat16),
-                carry[0],
-                carry[1],
-            )
-
-        back_rows, decoded_micro, dec_sums, mid_sums = lax.cond(
-            on_encoder, decode_spare, decode_step, (dec_sums, mid_sums)
-        )
-        decoded_parts.append(decoded_micro)
-        returned = from_behind(back_rows, "section", -1)
-
-        def encode_back(carry):
-            enc_carry, mid_carry = carry
-            encoded, enc_kept, final_unit, final_inverse = kept_all
-            grad_enc_result, grad_gain_final, grad_shift_final = norm_grad(
-                returned.astype(jnp.float32), final_unit, final_inverse, enc_gain_f[2]
-            )
-            grad_inputs, enc_grads = block_backward(
-                grad_enc_result, enc_kept, enc_weights, enc_valid, HEADS_ENC
-            )
-            micro_grads = (
-                jnp.concatenate([enc_grads[0], grad_gain_final[None]], axis=0),
-                jnp.concatenate([enc_grads[1], grad_shift_final[None]], axis=0),
-            ) + enc_grads[2:]
-            enc_carry = tuple((earlier + later for earlier, later in zip(enc_carry, micro_grads)))
-            return (grad_inputs.astype(jnp.bfloat16), enc_carry, mid_carry)
-
-        def back_spare(carry):
-            return (jnp.zeros((per_micro, strip_len, enc_width), jnp.bfloat16), carry[0], carry[1])
-
-        grad_micro, enc_sums, mid_sums = lax.cond(
-            on_encoder, encode_back, back_spare, (enc_sums, mid_sums)
-        )
-        grad_parts.append(grad_micro)
-    patch_full = jnp.concatenate(grad_parts, axis=0)
-    decoded_full = jnp.concatenate(decoded_parts, axis=0)
+    enc_valid = positions[None, :] < visible[:, None]
+    dec_valid = jnp.ones(source.shape, dtype=jnp.bool_)
+    enc_in = patches.astype(jnp.float32)
+    enc_result, enc_kept = block_forward(enc_in, enc_valid, enc_weights, HEADS_ENC)
+    final_normed, final_unit, final_inverse = apply_norm(enc_result, enc_gain_f[2], enc_shift_f[2])
+    encoded = final_normed.astype(jnp.bfloat16)
+    rows_in = (forward_product(encoded, enc_proj) + bias_proj).astype(jnp.bfloat16)
+    picker = (source[:, :, None] == positions[None, None, :]).astype(jnp.bfloat16)
+    missing = (source < 0).astype(jnp.float32)[:, :, None]
+    dec_in = (
+        jnp.einsum("bjr,brc->bjc", picker, rows_in, preferred_element_type=jnp.float32)
+        + missing * mask_row
+        + places
+    )
+    dec_result, dec_kept = block_forward(dec_in, dec_valid, dec_weights, HEADS_DEC)
+    grad_dec_in, dec_grads = block_backward(
+        cotangent.astype(jnp.float32), dec_kept, dec_weights, dec_valid, HEADS_DEC
+    )
+    grad_mask = jnp.sum(grad_dec_in * missing, axis=(0, 1))
+    grad_rows = jnp.einsum(
+        "bjr,bjc->brc",
+        picker,
+        grad_dec_in.astype(jnp.bfloat16),
+        preferred_element_type=jnp.float32,
+    ).astype(jnp.bfloat16)
+    grad_proj = weight_product(encoded, grad_rows)
+    grad_bias_proj = jnp.sum(grad_rows.astype(jnp.float32), axis=(0, 1))
+    back_rows = backward_product(grad_rows, enc_proj).astype(jnp.bfloat16)
+    grad_enc_result, grad_gain_final, grad_shift_final = norm_grad(
+        back_rows.astype(jnp.float32), final_unit, final_inverse, enc_gain_f[2]
+    )
+    grad_inputs, enc_grads = block_backward(
+        grad_enc_result, enc_kept, enc_weights, enc_valid, HEADS_ENC
+    )
+    enc_small = (
+        jnp.concatenate([enc_grads[0], grad_gain_final[None]], axis=0),
+        jnp.concatenate([enc_grads[1], grad_shift_final[None]], axis=0),
+    )
     half_enc = enc_width // 2
     half_dec = dec_width // 2
-    outgoing_halves = jnp.concatenate(
-        [patch_full[..., half_enc:], decoded_full[..., :half_dec]], axis=-1
-    )
-    arrived_halves = swapped(outgoing_halves, "section", 0)
-    patch_grad = jnp.where(on_encoder, patch_full[..., :half_enc], arrived_halves[..., :half_enc])
-    decoded = jnp.where(on_encoder, arrived_halves[..., half_enc:], decoded_full[..., half_dec:])
-    axis_list = (1, 1, 0, 0, 1, 0, 0, 0, 0, 0, 0, 1, 1, 0, 0, 1, 0, 0, 0)
-    grad_list = list(enc_sums) + list(mid_sums) + [dec_sums[8]] + list(dec_sums[:8])
-    dp_count = lax.axis_size("dp")
-    block_count = 2 * dp_count
-    flat_all = jnp.concatenate(
-        [
-            jnp.moveaxis(grad_value, axis_dim, 0).reshape(block_count, -1)
-            for grad_value, axis_dim in zip(grad_list, axis_list)
-        ],
-        axis=1,
-    )
-    summed = lax.psum_scatter(flat_all, ("section", "dp"), scatter_dimension=0, tiled=True)
-    finals = unpack_group(summed[0], grad_list, axis_list, block_count)
-    return (decoded, patch_grad) + tuple(finals)
+    decoded_full = dec_result.astype(jnp.bfloat16)
+    patch_full = grad_inputs.astype(jnp.bfloat16)
+
+    def swap_halves(full):
+        half = full.shape[-1] // 2
+        low_half, high_half = full[..., :half], full[..., half:]
+        first = section_index == 0
+        kept = jnp.where(first, low_half, high_half)
+        arrived = lax.ppermute(jnp.where(first, high_half, low_half), "section", [(0, 1), (1, 0)])
+        return jnp.concatenate(
+            [jnp.where(first, kept, arrived), jnp.where(first, arrived, kept)], axis=0
+        )
+
+    decoded = swap_halves(decoded_full)
+    patch_grad = swap_halves(patch_full)
+    dec_gain_grad, dec_shift_grad, g_dqkv, g_dout, g_dbias, g_dup, g_dbup, g_ddown = dec_grads
+    _, _, g_eqkv, g_eout, g_ebias, g_eup, g_ebup, g_edown = enc_grads
+    small = small_scatter(
+        (
+            enc_small[0],
+            enc_small[1],
+            g_ebias,
+            g_ebup,
+            grad_bias_proj,
+            grad_mask,
+            dec_gain_grad,
+            dec_shift_grad,
+            g_dbias,
+            g_dbup,
+        ),
+        (1, 1, 1, 0, 0, 0, 1, 1, 1, 0),
+    )
+    return (
+        decoded,
+        patch_grad,
+        small[0],
+        small[1],
+        row_scatter(g_eqkv),
+        row_scatter(g_eout),
+        small[2],
+        row_scatter(g_eup),
+        small[3],
+        row_scatter(g_edown),
+        row_scatter(grad_proj),
+        small[4],
+        small[5],
+        small[6],
+        small[7],
+        row_scatter(g_dqkv),
+        row_scatter(g_dout),
+        small[8],
+        row_scatter(g_dup),
+        small[9],
+        row_scatter(g_ddown),
+    )
 
 
 def solution(mesh):

time: 1840 us -> 1340 us (0.73)
  local copies, waits for them, and re-layouts: 398 us -> 113 us
  matrix products: 561 us -> 409 us
  blocking collectives: 0 us -> 43 us
  other arithmetic: 206 us -> 167 us
  loops' own time: 29.9 us -> 0 us
  waiting for transfers between devices: 608 us -> 583 us
    unnamed x2 -> x9, waiting for transfers between devices: 590 us -> 0.15 us
    reduce_scatter x0 -> x9, waiting for transfers between devices: none -> 583 us  [row_scatter(): lax.psum_scatter(blocks, ('section', 'dp'), scatter_dimension=0, tiled=True)]
    unnamed x128 -> x190, local copies, waits for them, and re-layouts: 142 us -> 14.5 us
    dot_general x8 -> x2, matrix products: 83.2 us -> 8.41 us  [the longest x1 6.78 us: local(): jnp.einsum('bjr,brc->bjc', picker, rows_in, preferred_element_type=jnp.fl...]
    cond x402 -> x0, local copies, waits for them, and re-layouts: 70.9 us -> none  [the longest x8 39 us: local(): lax.cond(on_encoder, encode_back, back_spare, (enc_sums, mid_sums))]
    dot_general x16 -> x8, matrix products: 112 us -> 54.7 us  [forward_product(): jnp.einsum('bld,df->blf', left_side, right_side, preferred_element_type=j...]
    dot_general x16 -> x9, matrix products: 130 us -> 74.2 us  [backward_product(): jnp.einsum('blf,df->bld', left_side, right_side, preferred_element_type=j...]
    reduce_sum x16 -> x1, other arithmetic: 53.3 us -> 1.72 us  [local(): grad_mask = jnp.sum(grad_dec_in * missing, axis=(0, 1))]
  transfers between devices with their start and end apart: 10 -> 11, of which waited for: 3 -> 5; matrix products, arithmetic and copies ran while one was open for 37% -> 32% of each run, Pallas kernels for 0% -> 0%
where the time goes in v1:
time: 1340 us; the launch traced here: 1330 us
  waiting for transfers between devices  583 us (44%)
  matrix products  409 us (31%)
  other arithmetic  167 us (12%)
  local copies, waits for them, and re-layouts  113 us (8%)
  blocking collectives  43 us (3%)
  between operations  15.3 us (1%)
    reduce_scatter x9, waiting for transfers between devices, row_scatter(): lax.psum_scatter(blocks, ('section', 'dp'), scatter_dimension=0, tiled=True)  583 us
    dot_general x9, matrix products, backward_product(): jnp.einsum('blf,df->bld', left_side, right_side, preferred_element_type=j...  74.2 us
    dot_general x2, matrix products, attend_grad(): jnp.einsum('bqhd,bkhd->bhqk', grad_heads, value_rows, preferred_element_t...  64.3 us
    convert_element_type x2, other arithmetic, attend_grad(): grad_scores = (weights_full * (grad_weights - jnp.sum(weights_full * grad...  63.7 us
    dot_general x9, matrix products, weight_product(): jnp.einsum('bld,blf->df', left_side, right_side, preferred_element_type=j...  59.1 us
    convert_element_type x2, other arithmetic, block_forward(): active = gelu_exact(hidden).astype(jnp.bfloat16)  55.6 us
    dot_general x8, matrix products, forward_product(): jnp.einsum('bld,df->blf', left_side, right_side, preferred_element_type=j...  54.7 us
    unnamed x1, blocking collectives  43 us
  transfers between devices with their start and end apart: 11, of which 5 were waited for; matrix products, arithmetic and copies ran while one was open for 32% of the time, Pallas kernels for 0%

profile of v1, /device:TPU:0, one launch (start us, length us, event | category | flops | bytes accessed | tf_op | source)
XLA Modules:
  0.0 1332.0 jit_solution(16715104488275221244)
XLA Ops:
  49.8 18.3 %fusion.141 = (f32[2,12,529]{2,1,0:T(8,128)}, f32[2,12,529,529]{2,3,1,0:T(8,128)}) fusion(pred[2,529]{1,0:T(4,128)(4,1)} %iota_compare_fusion.7, bf16[2,529,12,64]{1,3,2,0:T(8,128)(2,1)} %bitcast.246, bf16[2,529,12,64]{1,3,2,0:T(8,128)(2,1)} %bitcast.249), kind=kOutput, calls=%fused_computation.294 | convolution fusion | flops 886536768 | bytes 30166754 | tf_op jit(solution)/shard_map/sub | solution.py:80
  68.2 15.6 %fusion.81 = bf16[2,12,64,529]{3,2,1,0:T(8,128)(2,1)} fusion(bf16[2,529,12,64]{1,3,2,0:T(8,128)(2,1)} %bitcast.263, f32[2,12,529,529]{2,3,1,0:T(8,128)} %get-tuple-element.157, f32[2,12,529]{2,1,0:T(8,128)} %get-tuple-element.156), kind=kOutput, calls=%fused_computation.177 | convolution fusion | flops 873916480 | bytes 30165696 | tf_op jit(solution)/shard_map/bhqk,bkhd->bqhd/dot_general | solution.py:83
  90.2 17.4 %fusion.68 = (u8[529,3072]{1,0:T(8,128)(4,1)S(1)}, u8[529,3072]{1,0:T(8,128)(4,1)}, f32[2,529,3072]{2,1,0:T(8,128)}) fusion(f32[3072]{0:T(1024)S(1)} %convert_element_type.255, bf16[768,3072]{1,0:T(8,128)(2,1)} %param.31, f32[2,529,768]{2,1,0:T(8,128)} %copy-done.13, f32[768]{0:T(1024)S(1)} %copy-done.78, f32[768]{0:T(1024)S(1)} %get-tuple-element.186, ...), kind=kOutput, calls=%fused_computation.133 | convolution fusion | flops 5038585344 | bytes 24246544 | tf_op jit(solution)/shard_map/bld,df->blf/dot_general | solution.py:46
  107.6 33.6 %multiply_convert_fusion.2 = (bf16[2,529,3072]{2,1,0:T(8,128)(2,1)S(1)}, f32[2,529,3072]{2,1,0:T(8,128)}) fusion(f32[2,529,3072]{2,1,0:T(8,128)} %get-tuple-element.160, f32[3072]{0:T(1024)S(1)} %convert_element_type.255, u8[529,3072]{1,0:T(8,128)(4,1)} %get-tuple-element.85, u8[529,3072]{1,0:T(8,128)(4,1)S(1)} %get-tuple-element.84), kind=kLoop, calls=%fused_computation.29 | loop fusion | flops 230762496 | bytes 35764224 | tf_op jit(solution)/shard_map/convert_element_type | solution.py:136
  141.2 10.4 fusion.143
  177.6 20.8 %fusion.147 = (f32[2,16,529]{2,1,0:T(8,128)}, f32[2,16,529,529]{2,3,1,0:T(8,128)}) fusion(bf16[2,529,16,32]{1,3,2,0:T(8,128)(2,1)} %bitcast.252, bf16[2,529,16,32]{1,3,2,0:T(8,128)(2,1)} %bitcast.255), kind=kOutput, calls=%fused_computation.298 | convolution fusion | flops 599979648 | bytes 38054144 | tf_op jit(solution)/shard_map/sub | solution.py:80
  198.4 17.0 %fusion.89 = bf16[2,16,32,529]{3,2,1,0:T(8,128)(2,1)} fusion(bf16[2,529,16,32]{1,3,2,0:T(8,128)(2,1)} %bitcast.269, f32[2,16,529,529]{2,3,1,0:T(8,128)} %get-tuple-element.166, f32[2,16,529]{2,1,0:T(8,128)} %get-tuple-element.165), kind=kOutput, calls=%fused_computation.182 | convolution fusion | flops 591565888 | bytes 38054144 | tf_op jit(solution)/shard_map/bhqk,bkhd->bqhd/dot_general | solution.py:83
  224.0 21.9 %multiply_convert_fusion.3 = (bf16[2,529,2048]{2,1,0:T(8,128)(2,1)}, f32[2,529,2048]{2,1,0:T(8,128)}) fusion(f32[2,529,2048]{2,1,0:T(8,128)S(1)} %get-tuple-element.169, f32[2048]{0:T(1024)S(1)} %copy-done.47, u8[529,2048]{1,0:T(8,128)(4,1)S(1)} %get-tuple-element.87, u8[529,2048]{1,0:T(8,128)(4,1)S(1)} %get-tuple-element.86), kind=kLoop, calls=%fused_computation.57 | loop fusion | flops 153841664 | bytes 23842816 | tf_op jit(solution)/shard_map/convert_element_type | solution.py:136
  245.9 9.5 convert_reduce_fusion.1
  272.4 18.2 %fusion.92 = bf16[2,16,32,529]{3,2,1,0:T(8,128)(2,1)} fusion(bf16[2,529,16,32]{1,3,2,0:T(8,128)(2,1)} %bitcast.272, f32[2,16,529,529]{2,3,1,0:T(8,128)} %get-tuple-element.166, f32[2,16,529]{2,1,0:T(8,128)} %get-tuple-element.165), kind=kOutput, calls=%fused_computation.183 | convolution fusion | flops 591565888 | bytes 38054144 | tf_op jit(solution)/shard_map/bhqk,bqhd->bkhd/dot_general | solution.py:109
  290.6 37.7 %multiply_reduce_fusion = (f32[2,16,529]{2,1,0:T(8,128)}, f32[2,16,529,529]{2,3,1,0:T(8,128)}) fusion(f32[2,16,529,529]{2,3,1,0:T(8,128)} %get-tuple-element.166, f32[2,16,529]{2,1,0:T(8,128)} %get-tuple-element.165, bf16[2,529,16,32]{1,3,2,0:T(8,128)(2,1)} %bitcast.273, bf16[2,529,16,32]{1,3,2,0:T(8,128)(2,1)} %bitcast.270), kind=kOutput, calls=%fused_computation.3 | convolution fusion | flops 599962112 | bytes 73941504 | tf_op jit(solution)/shard_map/bqhd,bkhd->bhqk/dot_general | solution.py:95
  328.4 36.2 %multiply_convert_fusion = bf16[2,16,529,529]{2,3,1,0:T(8,128)(2,1)} fusion(f32[2,16,529,529]{2,3,1,0:T(8,128)} %get-tuple-element.172, f32[2,16,529]{2,1,0:T(8,128)} %get-tuple-element.171, f32[2,16,529,529]{2,3,1,0:T(8,128)} %get-tuple-element.166, f32[2,16,529]{2,1,0:T(8,128)} %get-tuple-element.165), kind=kLoop, calls=%fused_computation.2 | loop fusion | flops 35819648 | bytes 89684544 | tf_op jit(solution)/shard_map/convert_element_type | solution.py:100
  364.5 12.0 multiply_convert_fusion.6
  376.6 10.4 multiply_convert_fusion.7
  414.6 19.9 %convert_reduce_fusion = (f32[3072]{0:T(1024)}, bf16[2,529,3072]{2,1,0:T(8,128)(2,1)}) fusion(f32[2,529,3072]{2,1,0:T(8,128)} %get-tuple-element.132, bf16[2,529,768]{2,1,0:T(8,128)(2,1)} %get-tuple-element.128, bf16[3072,768]{1,0:T(8,128)(2,1)} %param.33, f32[2,529,3072]{2,1,0:T(8,128)} %get-tuple-element.160, f32[3072]{0:T(1024)S(1)} %copy-done.32), kind=kOutput, calls=%fused_computation.26 | convolution fusion | flops 5047520256 | bytes 38870016 | tf_op jit(solution)/shard_map/blf,df->bld/dot_general | solution.py:50
  434.6 10.9 multiply_reduce_fusion.3
  464.9 7.5 bitcast_convert_fusion.4
  481.2 26.5 %multiply_reduce_fusion.2 = (f32[2,12,529]{2,1,0:T(8,128)}, f32[2,12,529,529]{2,3,1,0:T(8,128)}) fusion(f32[2,12,529,529]{2,3,1,0:T(8,128)} %get-tuple-element.157, f32[2,12,529]{2,1,0:T(8,128)} %get-tuple-element.156, bf16[2,529,12,64]{1,3,2,0:T(8,128)(2,1)} %bitcast.265, bf16[2,529,12,64]{1,3,2,0:T(8,128)(2,1)} %bitcast.264), kind=kOutput, calls=%fused_computation.8 | convolution fusion | flops 879807360 | bytes 57081216 | tf_op jit(solution)/shard_map/bqhd,bkhd->bhqk/dot_general | solution.py:95
  507.8 27.5 %multiply_convert_fusion.1 = bf16[2,12,529,529]{2,3,1,0:T(8,128)(2,1)} fusion(f32[2,12,529,529]{2,3,1,0:T(8,128)} %get-tuple-element.177, f32[2,12,529]{2,1,0:T(8,128)} %get-tuple-element.176, f32[2,12,529,529]{2,3,1,0:T(8,128)} %get-tuple-element.157, f32[2,12,529]{2,1,0:T(8,128)} %get-tuple-element.156), kind=kLoop, calls=%fused_computation.7 | loop fusion | flops 26864736 | bytes 67263408 | tf_op jit(solution)/shard_map/convert_element_type | solution.py:100
  535.2 15.2 %fusion.84 = bf16[2,12,64,529]{3,2,1,0:T(8,128)(2,1)} fusion(bf16[2,529,12,64]{1,3,2,0:T(8,128)(2,1)} %bitcast.266, f32[2,12,529,529]{2,3,1,0:T(8,128)} %get-tuple-element.157, f32[2,12,529]{2,1,0:T(8,128)} %get-tuple-element.156), kind=kOutput, calls=%fused_computation.178 | convolution fusion | flops 873916480 | bytes 30165696 | tf_op jit(solution)/shard_map/bhqk,bqhd->bkhd/dot_general | solution.py:109
  554.3 11.0 multiply_convert_fusion.5
  569.3 10.1 multiply_convert_fusion.4
  583.5 9.8 bitcast_convert_fusion.2
  593.4 10.5 bitcast_convert_fusion
  612.8 11.5 bitcast_convert_fusion.1
  624.3 7.9 fusion.60
  664.8 43.0 %all-reduce = f32[32,480]{1,0:T(8,128)} all-reduce(f32[32,480]{1,0:T(8,128)} %concatenate.33), channel_id=2, replica_groups=mesh['section'=2,'dp'=16] {'section','dp'}, use_global_device_ids=true, to_apply=%region_44.45.clone | all-reduce | flops 15360 | bytes 122880
  734.3 118.2 %reduce-scatter.26.cloned.1.call-done = bf16[1,64,512]{2,1,0:T(8,128)(2,1)} async-done(((bf16[32,64,512]{2,1,0:T(8,128)(2,1)}), bf16[1,64,512]{2,1,0:T(8,128)(2,1)}) %reduce-scatter.26.cloned.1.call-update) | async-done | bytes 65552 | tf_op jit(solution)/shard_map/reduce_scatter | solution.py:212
  853.9 139.7 %reduce-scatter.24.cloned.1.call-done = bf16[1,16,2048]{2,1,0:T(8,128)(2,1)} async-done(((bf16[32,16,2048]{2,1,0:T(8,128)(2,1)}), bf16[1,16,2048]{2,1,0:T(8,128)(2,1)}) %reduce-scatter.24.cloned.1.call-update) | async-done | bytes 65552 | tf_op jit(solution)/shard_map/reduce_scatter | solution.py:212
  995.1 104.4 %reduce-scatter.10.cloned.1.call-done = bf16[1,24,2304]{2,1,0:T(8,128)(2,1)} async-done(((bf16[32,24,2304]{2,1,0:T(8,128)(2,1)}), bf16[1,24,2304]{2,1,0:T(8,128)(2,1)}) %reduce-scatter.10.cloned.1.call-update) | async-done | bytes 110608 | tf_op jit(solution)/shard_map/reduce_scatter | solution.py:212
  1101.2 110.8 %reduce-scatter.16.cloned.1.call-done = bf16[1,96,768]{2,1,0:T(8,128)(2,1)} async-done(((bf16[32,96,768]{2,1,0:T(8,128)(2,1)}), bf16[1,96,768]{2,1,0:T(8,128)(2,1)}) %reduce-scatter.16.cloned.1.call-update) | async-done | bytes 147472 | tf_op jit(solution)/shard_map/reduce_scatter | solution.py:212
  1213.6 110.0 %reduce-scatter.14.cloned.1.call-done = bf16[1,24,3072]{2,1,0:T(8,128)(2,1)} async-done(((bf16[32,24,3072]{2,1,0:T(8,128)(2,1)}), bf16[1,24,3072]{2,1,0:T(8,128)(2,1)}) %reduce-scatter.14.cloned.1.call-update) | async-done | bytes 147472 | tf_op jit(solution)/shard_map/reduce_scatter | solution.py:212
  (361 shorter events, 243.3 us)
Async XLA Ops:
  7.2 24.2 %copy-start = (bf16[768,2304]{1,0:T(8,128)(2,1)S(1)}, bf16[768,2304]{1,0:T(8,128)(2,1)}, u32[]{:S(2)}) copy-start(bf16[768,2304]{1,0:T(8,128)(2,1)} %param.28) | copy-start | bytes 10616836
  7.2 721.5 %reduce-scatter.22.cloned.1.call-start = ((), (), s32[]{:S(2)}) async-start(), calls=%async_computation.15 | async-start | bytes 540672 | tf_op jit(solution)/shard_map/reduce_scatter | solution.py:212
  7.3 20.8 %copy-start.28 = (bf16[4,529,768]{2,0,1:T(4,128)(2,1)S(1)}, bf16[4,529,768]{2,0,1:T(4,128)(2,1)}, u32[]{:S(2)}) copy-start(bf16[4,529,768]{2,0,1:T(4,128)(2,1)} %param.23) | copy-start | bytes 9750532
  20.1 87.5 %copy-start.31 = (f32[3072]{0:T(1024)}, f32[3072]{0:T(1024)S(1)}, u32[]{:S(2)}) copy-start(f32[3072]{0:T(1024)S(1)} %convert_element_type.255) | copy-start | bytes 36868
  31.4 58.8 %copy-start.62 = (f32[768]{0:T(1024)}, f32[768]{0:T(1024)S(1)}, u32[]{:S(2)}) copy-start(f32[768]{0:T(1024)S(1)} %get-tuple-element.186) | copy-start | bytes 9220
  87.9 19.6 %copy-start.37 = (f32[2,529]{1,0:T(2,128)}, f32[2,529]{1,0:T(2,128)S(1)}, u32[]{:S(2)}) copy-start(f32[2,529]{1,0:T(2,128)S(1)} %broadcast_multiply_fusion.13) | copy-start | bytes 12700
  90.1 17.4 %copy-start.50 = (f32[2,529]{1,0:T(2,128)}, f32[2,529]{1,0:T(2,128)S(1)}, u32[]{:S(2)}) copy-start(f32[2,529]{1,0:T(2,128)S(1)} %add_rsqrt_fusion.3) | copy-start | bytes 12700
  107.5 33.6 %copy-start.14 = (f32[2,529,768]{2,1,0:T(8,128)S(1)}, f32[2,529,768]{2,1,0:T(8,128)}, u32[]{:S(2)}) copy-start(f32[2,529,768]{2,1,0:T(8,128)} %copy-done.13) | copy-start | bytes 9750532
  107.6 33.6 %copy-start.73 = (f32[768]{0:T(1024)S(1)}, f32[768]{0:T(1024)}, u32[]{:S(2)}) copy-start(f32[768]{0:T(1024)} %get-tuple-element.119) | copy-start | bytes 9220
  198.4 17.0 %copy-start.67 = (f32[1,512]{1,0:T(1,128)S(1)}, f32[1,512]{1,0:T(1,128)}, u32[]{:S(2)}) copy-start(f32[1,512]{1,0:T(1,128)} %get-tuple-element.149) | copy-start | bytes 6148
  218.6 42.8 %copy-start.10 = (f32[2,529,512]{2,1,0:T(8,128)}, f32[2,529,512]{2,1,0:T(8,128)S(1)}, u32[]{:S(2)}) copy-start(f32[2,529,512]{2,1,0:T(8,128)S(1)} %get-tuple-element.168) | copy-start | bytes 6500356
  218.7 42.8 %copy-start.33 = (f32[2,529]{1,0:T(2,128)}, f32[2,529]{1,0:T(2,128)S(1)}, u32[]{:S(2)}) copy-start(f32[2,529]{1,0:T(2,128)S(1)} %broadcast_multiply_fusion.4) | copy-start | bytes 12700
  219.1 42.3 %copy-start.54 = (f32[2,529]{1,0:T(2,128)}, f32[2,529]{1,0:T(2,128)S(1)}, u32[]{:S(2)}) copy-start(f32[2,529]{1,0:T(2,128)S(1)} %add_rsqrt_fusion) | copy-start | bytes 12700
  223.9 22.0 %copy-start.24 = (bf16[2,529,512]{2,0,1:T(2,128)(2,1)S(1)}, bf16[2,529,512]{2,0,1:T(2,128)(2,1)}, u32[]{:S(2)}) copy-start(bf16[2,529,512]{2,0,1:T(2,128)(2,1)} %constant_dynamic-slice_fusion) | copy-start | bytes 3250180
  223.9 22.0 %copy-start.88 = (bf16[2048,512]{1,0:T(8,128)(2,1)S(1)}, bf16[2048,512]{1,0:T(8,128)(2,1)}, u32[]{:S(2)}) copy-start(bf16[2048,512]{1,0:T(8,128)(2,1)} %param.44) | copy-start | bytes 6291460
  266.1 464.0 %reduce-scatter.18.cloned.1.call-start = ((), (), s32[]{:S(2)}) async-start(), calls=%async_computation.13 | async-start | bytes 811008 | tf_op jit(solution)/shard_map/reduce_scatter | solution.py:212
  364.5 12.0 copy-start.19
  406.7 324.7 %reduce-scatter.12.cloned.1.call-start = ((), (), s32[]{:S(2)}) async-start(), calls=%async_computation.10 | async-start | bytes 1216512 | tf_op jit(solution)/shard_map/reduce_scatter | solution.py:212
  414.6 19.9 %copy-start.38 = (f32[2,529]{1,0:T(2,128)S(1)}, f32[2,529]{1,0:T(2,128)}, u32[]{:S(2)}) copy-start(f32[2,529]{1,0:T(2,128)} %copy-done.37) | copy-start | bytes 12700
  414.6 19.9 %copy-start.51 = (f32[2,529]{1,0:T(2,128)S(1)}, f32[2,529]{1,0:T(2,128)}, u32[]{:S(2)}) copy-start(f32[2,529]{1,0:T(2,128)} %copy-done.50) | copy-start | bytes 12700
  414.6 19.9 %copy-start.63 = (f32[768]{0:T(1024)S(1)}, f32[768]{0:T(1024)}, u32[]{:S(2)}) copy-start(f32[768]{0:T(1024)} %copy-done.62) | copy-start | bytes 9220
  434.5 11.0 copy-start.4
  434.5 11.0 copy-start.15
  434.5 11.0 copy-start.21
  451.3 281.6 %reduce-scatter.20.cloned.1.call-start = ((), (), s32[]{:S(2)}) async-start(), calls=%async_computation.14 | async-start | bytes 1622016 | tf_op jit(solution)/shard_map/reduce_scatter | solution.py:212
  457.5 395.0 %reduce-scatter.26.cloned.1.call-start = ((), (), s32[]{:S(2)}) async-start(), calls=%async_computation.17 | async-start | bytes 2162688 | tf_op jit(solution)/shard_map/reduce_scatter | solution.py:212
  464.8 528.8 %reduce-scatter.24.cloned.1.call-start = ((), (), s32[]{:S(2)}) async-start(), calls=%async_computation.16 | async-start | bytes 2162688 | tf_op jit(solution)/shard_map/reduce_scatter | solution.py:212
  472.4 627.2 %reduce-scatter.10.cloned.1.call-start = ((), (), s32[]{:S(2)}) async-start(), calls=%async_computation.9 | async-start | bytes 3649536 | tf_op jit(solution)/shard_map/reduce_scatter | solution.py:212
  593.4 618.6 %reduce-scatter.16.cloned.1.call-start = ((), (), s32[]{:S(2)}) async-start(), calls=%async_computation.12 | async-start | bytes 4866048 | tf_op jit(solution)/shard_map/reduce_scatter | solution.py:212
  603.9 719.7 %reduce-scatter.14.cloned.1.call-start = ((), (), s32[]{:S(2)}) async-start(), calls=%async_computation.11 | async-start | bytes 4866048 | tf_op jit(solution)/shard_map/reduce_scatter | solution.py:212
  612.5 109.7 %collective-permute-start = (bf16[2,529,256]{2,0,1:T(2,128)(2,1)}, bf16[2,529,256]{2,0,1:T(2,128)(2,1)}, u32[]{:S(2)}, u32[]{:S(2)}) collective-permute-start(bf16[2,529,256]{2,0,1:T(2,128)(2,1)} %copy.144), channel_id=1, source_target_pairs={{0,16},{16,0},{1,17},{17,1},{2,18},{18,2},{3,19},{19,3},{4,20},{20... | collective-permute-start | bytes 1625096 | tf_op jit(solution)/shard_map/ppermute | solution.py:343
  636.4 88.9 %collective-permute-start.1 = (bf16[2,529,384]{2,0,1:T(2,128)(2,1)}, bf16[2,529,384]{2,0,1:T(2,128)(2,1)}, u32[]{:S(2)}, u32[]{:S(2)}) collective-permute-start(bf16[2,529,384]{2,0,1:T(2,128)(2,1)} %copy.162), channel_id=1, source_target_pairs={{0,16},{16,0},{1,17},{17,1},{2,18},{18,2},{3,19},{19,3},{4,20},{20... | collective-permute-start | bytes 2437640 | tf_op jit(solution)/shard_map/ppermute | solution.py:343
  (70 other events, 311.6 us)
Sparse Core Ops, SparseCore 0:
  266.2 140.0 reduce-scatter.21
  412.2 92.8 reduce-scatter.17
  511.0 95.2 reduce-scatter.11
  612.2 96.6 reduce-scatter.19
  711.1 141.3 reduce-scatter.25
  854.5 139.0 reduce-scatter.23
  999.9 99.5 reduce-scatter.9
  1105.9 105.9 reduce-scatter.15
  1217.4 106.1 reduce-scatter.13

commit v2 on v1

v2 whole, which is shorter than its diff:
```python
import functools
import math

import jax
import jax.numpy as jnp
import numpy as np
from jax import lax
from jax.experimental import pallas as pl
from jax.experimental.pallas import tpu as pltpu
from jax.sharding import PartitionSpec as P

HEADS_ENC = 12
HEADS_DEC = 16
ROW_STEP = 32
GROUP = 128
VMEM_BYTES = 56 * 1024 * 1024
MASKED = -1e30
LOG2E = math.log2(math.e)

epsilon = 1e-06

NN = (((1,), (0,)), ((), ()))
NT = (((1,), (1,)), ((), ()))
TN = (((0,), (0,)), ((), ()))


def dot(left_side, right_side, dims):
    return lax.dot_general(left_side, right_side, dims, preferred_element_type=jnp.float32)


def low(values):
    return values.astype(jnp.bfloat16)


def call(
    kernel, out_shape, grid, in_specs, out_specs, flops, moved, scalars=1, exps=0, after=(), name=None, scratch=()
):
    count = scalars + len(in_specs)
    ordered = [pl.BlockSpec(memory_space=pl.ANY)] * len(after)

    def body(*refs):
        kernel(*refs[:count], *refs[count + len(after) :])

    made = pl.pallas_call(
        body,
        out_shape=out_shape,
        grid_spec=pltpu.PrefetchScalarGridSpec(
            num_scalar_prefetch=scalars,
            grid=grid,
            in_specs=list(in_specs) + ordered,
            out_specs=out_specs,
            scratch_shapes=list(scratch),
        ),
        compiler_params=pltpu.CompilerParams(vmem_limit_bytes=VMEM_BYTES),
        cost_estimate=pl.CostEstimate(flops=flops // 256, bytes_accessed=moved // 256, transcendentals=0),
        name=name,
    )
    return lambda *operands: made(*operands, *after)


def whole(array):
    rank = array.ndim
    return pl.BlockSpec(array.shape, lambda *unused: (0,) * rank)


def row_of(ref, place):
    return ref[place : place + 1, :].astype(jnp.float32)


def vector_of(ref):
    return ref[...].astype(jnp.float32).reshape(1, -1)


def live_rows(values, start, count):
    row = lax.broadcasted_iota(jnp.int32, (values.shape[0], 1), 0) + start
    return jnp.where(row < count, values.astype(jnp.float32), 0.0)


def sds(shape, kind=jnp.bfloat16):
    return jax.ShapeDtypeStruct(shape, kind)


def norm(values, gain_row, shift_row):
    center = values - jnp.mean(values, axis=-1, keepdims=True)
    inverse = lax.rsqrt(jnp.mean(center * center, axis=-1, keepdims=True) + epsilon)
    unit = center * inverse
    return unit * gain_row + shift_row, unit, inverse


def norm_back(grad_out, unit, inverse, gain_row):
    scaled = grad_out * gain_row
    return inverse * (
        scaled
        - jnp.mean(scaled, axis=-1, keepdims=True)
        - unit * jnp.mean(scaled * unit, axis=-1, keepdims=True)
    )


def col_sum(values):
    return jnp.sum(values, axis=0, keepdims=True)


def gelu_parts(values):
    size = jnp.abs(values)
    t = 1.0 / (1.0 + (0.3275911 / math.sqrt(2.0)) * size)
    bell = jnp.exp2(values * values * (-0.5 * LOG2E))
    poly = t * (
        0.5 * 0.254829592
        + t
        * (
            0.5 * -0.284496736
            + t * (0.5 * 1.421413741 + t * (0.5 * -1.453152027 + t * (0.5 * 1.061405429)))
        )
    )
    tail = poly * bell
    share = jnp.where(values >= 0.0, 1.0 - tail, tail)
    return values * share, share + values * bell * (1.0 / math.sqrt(2.0 * math.pi))


def add_rows(ref, rows):
    @pl.when((pl.program_id(0) == 0) & (pl.program_id(1) == 0))
    def start():
        ref[...] = jnp.zeros_like(ref)

    for place, row in enumerate(rows):
        ref[place : place + 1, :] += row


BLOCK = 1
STRIP = 2


def place_info(visible, strips):
    section_index = lax.axis_index("section")
    block = section_index * lax.axis_size("dp") + lax.axis_index("dp")
    mine = section_index * strips + jnp.arange(strips, dtype=jnp.int32)
    every = jnp.arange(2 * strips, dtype=jnp.int32)
    return jnp.concatenate(
        [
            jnp.stack([section_index, block]),
            mine,
            lax.dynamic_slice_in_dim(visible, section_index * strips, strips, 0),
            every // strips,
            every % strips,
        ]
    ).astype(jnp.int32)


class Sizes:
    def __init__(self, strips, length, padded):
        self.strips, self.length, self.padded = strips, length, padded
        self.rows = strips * padded
        self.pieces = 2
        self.step = padded // self.pieces
        self.grid = (strips, self.pieces)

    def flat(self, width):
        return pl.BlockSpec((self.step, width), lambda s, i, info: (s * self.pieces + i, 0))

    def flat_three(self, width):
        return pl.BlockSpec((3, self.step, width), lambda s, i, info: (0, s * self.pieces + i, 0))

    def raw(self, width):
        return pl.BlockSpec((None, self.step, width), lambda s, i, info: (info[STRIP + s], i, 0))

    def half(self, width):
        return pl.BlockSpec((None, self.step, width), lambda s, i, info: (s, i, 0))

    def sums(self, width):
        return pl.BlockSpec((8, width), lambda s, i, info: (0, 0))

    def strip(self, width):
        return pl.BlockSpec((None, self.padded, width), lambda s, i, info: (s, 0, 0))


class OneStrip(Sizes):
    def __init__(self, sizes, strip):
        super().__init__(sizes.strips, sizes.length, sizes.padded)
        self.at = strip
        self.grid = (1, self.pieces)

    def flat(self, width):
        return pl.BlockSpec((self.step, width), lambda s, i, info: (self.at * self.pieces + i, 0))

    def flat_three(self, width):
        return pl.BlockSpec(
            (3, self.step, width), lambda s, i, info: (0, self.at * self.pieces + i, 0)
        )

    def raw(self, width):
        return pl.BlockSpec((None, self.step, width), lambda s, i, info: (info[STRIP + self.at], i, 0))

    def half(self, width):
        return pl.BlockSpec((None, self.step, width), lambda s, i, info: (0, i, 0))


def store_halves(info_ref, kept_ref, sent_ref, values):
    half = kept_ref.shape[-1]
    first = info_ref[0] == 0
    kept_ref[...] = low(jnp.where(first, values[:, :half], values[:, half:]))
    sent_ref[...] = low(jnp.where(first, values[:, half:], values[:, :half]))


def packed_kernel(info_ref, x_ref, gain_ref, shift_ref, w_ref, n_ref, packed_ref, *, length):
    x = live_rows(x_ref[...], pl.program_id(1) * x_ref.shape[0], length)
    normed, _, _ = norm(x, row_of(gain_ref, 0), row_of(shift_ref, 0))
    normed = low(normed)
    n_ref[...] = normed
    packed_ref[...] = low(dot(normed, w_ref[...], NN))


def packed_call(sizes, info, x, gains, shifts, w_qkv):
    rows, width = sizes.rows, x.shape[2]
    return call(
        functools.partial(packed_kernel, length=sizes.length),
        (sds((rows, width)), sds((rows, 3 * width))),
        sizes.grid,
        [sizes.raw(width), whole(gains), whole(shifts), whole(w_qkv)],
        (sizes.flat(width), sizes.flat(3 * width)),
        6 * rows * width * width,
        rows * width * 10 + 6 * width * width,
        name="encoder_packed",
    )(info, x, gains, shifts, w_qkv)


def picker_of(source_ref, strip):
    taken = source_ref[pl.ds(strip, 1), :]
    length = taken.shape[1]
    return low(jnp.where(taken == lax.broadcasted_iota(jnp.int32, (length, length), 0), 1.0, 0.0))


def last_row(length):
    return lax.broadcasted_iota(jnp.int32, (length, 1), 0) == length - 1


def decoder_in_kernel(
    info_ref,
    rows_ref,
    source_ref,
    mask_ref,
    places_ref,
    gain_ref,
    shift_ref,
    w_ref,
    x_ref,
    n_ref,
    packed_ref,
):
    picker = picker_of(source_ref, info_ref[STRIP + pl.program_id(0)])
    rows = jnp.where(
        last_row(rows_ref.shape[0]), vector_of(mask_ref), rows_ref[...].astype(jnp.float32)
    )
    x = dot(picker, low(rows), TN) + places_ref[...]
    x_ref[...] = x
    normed, _, _ = norm(x, row_of(gain_ref, 0), row_of(shift_ref, 0))
    normed = low(normed)
    n_ref[...] = normed
    packed_ref[...] = low(dot(normed, w_ref[...], NN))


def decoder_in_call(sizes, info, projected, source, mask_row, places, gains, shifts, w_qkv):
    width = projected.shape[1]
    rows, strips, padded = sizes.rows, sizes.strips, sizes.padded
    weights = (gains, shifts, w_qkv)
    return call(
        decoder_in_kernel,
        (
            sds((strips, padded, width), jnp.float32),
            sds((strips, padded, width)),
            sds((strips, padded, 3 * width)),
        ),
        (strips, 1),
        [sizes.strip(width), whole(source), whole(mask_row), whole(places)]
        + [whole(w) for w in weights],
        (sizes.strip(width), sizes.strip(width), sizes.strip(3 * width)),
        6 * rows * width * width + 2 * rows * padded * width,
        rows * width * 18 + 6 * width * width,
        name="decoder_packed",
    )(info, projected.reshape(strips, padded, width), source, mask_row, places, *weights)


def head_parts(head, heads_here):
    lane = lax.broadcasted_iota(jnp.int32, (1, GROUP), 1)
    size = GROUP // heads_here
    mine = (lane >= head * size) & (lane < (head + 1) * size)
    spare = ((head + 1) % heads_here) * size
    return mine, lane == spare, spare


def key_bias(live, length):
    row = lax.broadcasted_iota(jnp.int32, (length, 1), 0)
    return low(jnp.where(row < live, 0.0, MASKED))


def attend_kernel(info_ref, q_ref, k_ref, v_ref, out_ref, *, heads_here, live):
    length = q_ref.shape[1]
    rate = (GROUP // heads_here) ** -0.5 * LOG2E
    q, k, v = q_ref[0], k_ref[0], v_ref[0]
    bias = key_bias(live(info_ref, pl.program_id(0)), length)
    one = jnp.bfloat16(1.0)
    mixed = jnp.zeros((length, GROUP), jnp.float32)
    for head in range(heads_here):
        mine, at_spare, spare = head_parts(head, heads_here)
        head_q = jnp.where(mine, q, low(jnp.where(at_spare, 1.0, 0.0)))
        scores = dot(head_q, jnp.where(at_spare, bias, k), NT)
        highest = jnp.max(scores, axis=1, keepdims=True)
        terms = low(jnp.exp2((scores - highest) * rate))
        product = dot(terms, jnp.where(at_spare, one, v), NN)
        total = product[:, spare : spare + 1]
        mixed = jnp.where(mine, product * (1.0 / total), mixed)
    out_ref[0] = low(mixed)


def all_live(length):
    return lambda info_ref, strip: length


def visible_live(strips):
    return lambda info_ref, strip: info_ref[STRIP + strips + strip]


def attend_call(packed, info, heads, live, name):
    strips, length, triple = packed.shape
    width = triple // 3
    heads_here = GROUP // (width // heads)
    groups = width // GROUP
    third = lambda j: pl.BlockSpec((1, length, GROUP), lambda s, g, _: (s, 0, g + j * groups))
    return call(
        functools.partial(attend_kernel, heads_here=heads_here, live=live),
        sds((strips, length, width)),
        (strips, groups),
        [third(0), third(1), third(2)],
        third(0),
        strips * heads * length * length * GROUP * 6,
        strips * length * width * 8,
        exps=strips * heads * length * length,
        name=name,
    )(info, packed, packed, packed)


def attend_back_kernel(
    info_ref,
    q_ref,
    k_ref,
    v_ref,
    dout_ref,
    n_ref,
    grad_ref,
    kept_ref,
    sent_ref,
    total_ref,
    *,
    heads_here,
    live
):
    length = q_ref.shape[1]
    factor = (GROUP // heads_here) ** -0.5
    rate = factor * LOG2E
    strip = pl.program_id(1)
    q, k, v, dout = q_ref[0], k_ref[0], v_ref[0], dout_ref[0]
    bias = key_bias(live(info_ref, strip), length)
    k_turned = k.T
    dq_turned = jnp.zeros((GROUP, length), jnp.float32)
    dk = jnp.zeros((length, GROUP), jnp.float32)
    dv = jnp.zeros((length, GROUP), jnp.float32)
    row = lax.broadcasted_iota(jnp.int32, (GROUP, 1), 0)
    size = GROUP // heads_here
    for head in range(heads_here):
        mine, at_spare, _ = head_parts(head, heads_here)
        head_q = jnp.where(mine, q, low(jnp.where(at_spare, 1.0, 0.0)))
        head_dout = jnp.where(mine, dout, jnp.bfloat16(0.0))
        scores = dot(jnp.where(at_spare, bias, k), head_q, NT)
        highest = jnp.max(scores, axis=0, keepdims=True)
        terms = jnp.exp2((scores - highest) * rate)
        probs = terms * (1.0 / jnp.sum(terms, axis=0, keepdims=True))
        weighted = probs * dot(v, head_dout, NT)
        dscores = low(weighted - probs * jnp.sum(weighted, axis=0, keepdims=True))
        dk = jnp.where(mine, dot(dscores, q, NN), dk)
        dv = jnp.where(mine, dot(low(probs), dout, NN), dv)
        mine_row = (row >= head * size) & (row < (head + 1) * size)
        dq_turned = jnp.where(mine_row, dot(k_turned, dscores, NN), dq_turned)
    dq, dk, dv = low(dq_turned.T * factor), low(dk * factor), low(dv)
    grad_ref[0, 0] = dq
    grad_ref[1, 0] = dk
    grad_ref[2, 0] = dv
    term = dot(n_ref[0], jnp.concatenate([dq, dk, dv], axis=1), TN)
    half = kept_ref.shape[0]
    last = pl.num_programs(1) - 1

    @pl.when(strip == 0)
    def begin():
        total_ref[...] = term

    @pl.when(strip > 0)
    def more():
        total_ref[...] += term

    @pl.when(strip == last)
    def finish():
        kept_ref[...] = low(total_ref[pl.ds(pl.multiple_of(info_ref[0] * half, 8), half), :])
        sent_ref[...] = low(total_ref[pl.ds(pl.multiple_of((1 - info_ref[0]) * half, 8), half), :])


def attend_back_call(packed, dmixed, normed, info, heads, live, part, parts, after, name):
    strips, length, triple = packed.shape
    width = triple // 3
    heads_here = GROUP // (width // heads)
    groups = width // GROUP
    here = groups // parts
    third = lambda j: pl.BlockSpec(
        (1, length, GROUP), lambda g, s, _: (s, 0, g + part * here + j * groups)
    )
    product = pl.BlockSpec((width // 2, 3 * GROUP), lambda g, s, _: (0, g))
    return call(
        functools.partial(attend_back_kernel, heads_here=heads_here, live=live),
        (
            sds((3, strips, length, here * GROUP)),
            sds((width // 2, here * 3 * GROUP)),
            sds((width // 2, here * 3 * GROUP)),
        ),
        (here, strips),
        [
            third(0),
            third(1),
            third(2),
            third(0),
            pl.BlockSpec((1, length, width), lambda g, s, _: (s, 0, 0)),
        ],
        (pl.BlockSpec((3, 1, length, GROUP), lambda g, s, _: (0, s, 0, g)), product, product),
        (strips * heads * length * length * GROUP * 12 + 6 * strips * length * width * width) // parts,
        strips * length * width * 14 // parts,
        exps=strips * heads * length * length // parts,
        after=after,
        name=name,
        scratch=[pltpu.VMEM((width, 3 * GROUP), jnp.float32)],
    )(info, packed, packed, packed, dmixed, normed)


def encoder_ff_kernel(
    info_ref,
    x_ref,
    mixed_ref,
    gain_ref,
    shift_ref,
    w_out_ref,
    bias_out_ref,
    w_up_ref,
    bias_up_ref,
    w_down_ref,
    w_proj_ref,
    bias_proj_ref,
    mid_ref,
    n_ref,
    act_ref,
    slope_ref,
    y_ref,
    encoded_ref,
    projected_ref,
    *,
    chunk,
    length
):
    x = live_rows(x_ref[...], pl.program_id(1) * x_ref.shape[0], length)
    mid = x + dot(mixed_ref[...], w_out_ref[...], NN) + row_of(bias_out_ref, 0)
    mid_ref[...] = mid
    normed, _, _ = norm(mid, row_of(gain_ref, 1), row_of(shift_ref, 1))
    normed = low(normed)
    n_ref[...] = normed
    bias_up = vector_of(bias_up_ref)
    y = mid + row_of(bias_out_ref, 1)
    for start in range(0, w_up_ref.shape[1], chunk):
        part = slice(start, start + chunk)
        hidden = dot(normed, w_up_ref[:, part], NN) + bias_up[:, part]
        act, slope = gelu_parts(hidden)
        act = low(act)
        act_ref[:, part] = act
        slope_ref[:, part] = low(slope)
        y = y + dot(act, w_down_ref[part, :], NN)
    y_ref[...] = y
    encoded, _, _ = norm(y, row_of(gain_ref, 2), row_of(shift_ref, 2))
    encoded = low(encoded)
    encoded_ref[...] = encoded
    projected_ref[...] = low(dot(encoded, w_proj_ref[...], NN) + vector_of(bias_proj_ref))


def encoder_ff_call(
    sizes, info, x, mixed, gains, shifts, w_out, bias_out, w_up, bias_up, w_down, w_proj, bias_proj
):
    rows, width = sizes.rows, x.shape[2]
    units = w_up.shape[1]
    narrow = w_proj.shape[1]
    flat = sizes.flat
    weights = (gains, shifts, w_out, bias_out, w_up, bias_up, w_down, w_proj, bias_proj)
    return call(
        functools.partial(encoder_ff_kernel, chunk=units // 4, length=sizes.length),
        (
            sds((rows, width), jnp.float32),
            sds((rows, width)),
            sds((rows, units)),
            sds((rows, units)),
            sds((rows, width), jnp.float32),
            sds((rows, width)),
            sds((rows, narrow)),
        ),
        sizes.grid,
        [sizes.raw(width), flat(width)] + [whole(w) for w in weights],
        (flat(width), flat(width), flat(units), flat(units), flat(width), flat(width), flat(narrow)),
        2 * rows * width * (width + 2 * units + narrow),
        rows * (width * 16 + units * 4) + 2 * width * (width + 2 * units + narrow),
        exps=rows * units,
        name="encoder_feed_forward",
    )(info, x, mixed, *weights)


def decoder_ff_kernel(
    info_ref,
    x_ref,
    mixed_ref,
    cot_ref,
    gain_ref,
    shift_ref,
    w_out_ref,
    bias_out_ref,
    w_up_ref,
    bias_up_ref,
    w_down_ref,
    kept_ref,
    sent_ref,
    cot_low_ref,
    n_ref,
    act_ref,
    dhidden_ref,
    gm_ref,
    gb_ref,
    dmixed_ref,
    sums_ref,
    up_sums_ref,
    *,
    chunk,
    length
):
    mid = x_ref[...] + dot(mixed_ref[...], w_out_ref[...], NN) + row_of(bias_out_ref, 0)
    gain = row_of(gain_ref, 1)
    normed, unit, inverse = norm(mid, gain, row_of(shift_ref, 1))
    normed = low(normed)
    n_ref[...] = normed
    grad = live_rows(cot_ref[...], pl.program_id(1) * cot_ref.shape[0], length)
    cot = low(grad)
    cot_low_ref[...] = cot
    bias_up = vector_of(bias_up_ref)
    y = mid + row_of(bias_out_ref, 1)
    dnormed = jnp.zeros(y.shape, jnp.float32)
    up_sums = []
    for start in range(0, w_up_ref.shape[1], chunk):
        part = slice(start, start + chunk)
        hidden = dot(normed, w_up_ref[:, part], NN) + bias_up[:, part]
        act, slope = gelu_parts(hidden)
        act = low(act)
        act_ref[:, part] = act
        y = y + dot(act, w_down_ref[part, :], NN)
        dhidden = low(dot(cot, w_down_ref[part, :], NT) * slope)
        dhidden_ref[:, part] = dhidden
        up_sums.append(col_sum(dhidden.astype(jnp.float32)))
        dnormed = dnormed + dot(dhidden, w_up_ref[:, part], NT)
    store_halves(info_ref, kept_ref, sent_ref, y)
    gm = grad + norm_back(dnormed, unit, inverse, gain)
    gm_ref[...] = gm
    gb = low(gm)
    gb_ref[...] = gb
    dmixed_ref[...] = low(dot(gb, w_out_ref[...], NT))
    add_rows(
        sums_ref,
        (col_sum(dnormed * unit), col_sum(dnormed), col_sum(gb.astype(jnp.float32)), col_sum(grad)),
    )
    add_rows(up_sums_ref, (jnp.concatenate(up_sums, axis=1),))


def decoder_ff_call(
    sizes, info, x, mixed, cot, gains, shifts, w_out, bias_out, w_up, bias_up, w_down
):
    rows, width = x.shape
    units = w_up.shape[1]
    flat = sizes.flat
    weights = (gains, shifts, w_out, bias_out, w_up, bias_up, w_down)
    half = sds((sizes.strips, sizes.length, width // 2))
    return call(
        functools.partial(decoder_ff_kernel, chunk=units // 4, length=sizes.length),
        (
            half,
            half,
            sds((rows, width)),
            sds((rows, width)),
            sds((rows, units)),
            sds((rows, units)),
            sds((rows, width), jnp.float32),
            sds((rows, width)),
            sds((rows, width)),
            sds((8, width), jnp.float32),
            sds((8, units), jnp.float32),
        ),
        sizes.grid,
        [flat(width), flat(width), sizes.raw(width)] + [whole(w) for w in weights],
        (
            sizes.half(width // 2),
            sizes.half(width // 2),
            flat(width),
            flat(width),
            flat(units),
            flat(units),
            flat(width),
            flat(width),
            flat(width),
            sizes.sums(width),
            sizes.sums(units),
        ),
        2 * rows * width * (2 * width + 4 * units),
        rows * (width * 22 + units * 4) + 2 * width * (width + 2 * units),
        exps=rows * units,
        name="decoder_feed_forward",
    )(info, x, mixed, cot, *weights)


def encoder_ff_back_kernel(
    info_ref,
    grad_ref,
    mid_ref,
    slope_ref,
    gain_ref,
    shift_ref,
    w_out_ref,
    w_up_ref,
    w_down_ref,
    dhidden_ref,
    gm_ref,
    gb_ref,
    dmixed_ref,
    sums_ref,
    up_sums_ref,
    *,
    chunk
):
    gain = row_of(gain_ref, 1)
    _, unit, inverse = norm(mid_ref[...], gain, row_of(shift_ref, 1))
    grad = grad_ref[...]
    grad_low = low(grad)
    dnormed = jnp.zeros(grad.shape, jnp.float32)
    up_sums = []
    for start in range(0, w_up_ref.shape[1], chunk):
        part = slice(start, start + chunk)
        slope = slope_ref[:, part].astype(jnp.float32)
        dhidden = low(dot(grad_low, w_down_ref[part, :], NT) * slope)
        dhidden_ref[:, part] = dhidden
        up_sums.append(col_sum(dhidden.astype(jnp.float32)))
        dnormed = dnormed + dot(dhidden, w_up_ref[:, part], NT)
    gm = grad + norm_back(dnormed, unit, inverse, gain)
    gm_ref[...] = gm
    gb = low(gm)
    gb_ref[...] = gb
    dmixed_ref[...] = low(dot(gb, w_out_ref[...], NT))
    add_rows(
        sums_ref,
        (
            col_sum(dnormed * unit),
            col_sum(dnormed),
            col_sum(gb.astype(jnp.float32)),
            col_sum(grad_low.astype(jnp.float32)),
        ),
    )
    add_rows(up_sums_ref, (jnp.concatenate(up_sums, axis=1),))


def encoder_ff_back_call(sizes, info, grad, mid, slope, gains, shifts, w_out, w_up, w_down, after):
    rows, width = grad.shape
    units = w_up.shape[1]
    flat = sizes.flat
    weights = (gains, shifts, w_out, w_up, w_down)
    return call(
        functools.partial(encoder_ff_back_kernel, chunk=units // 4),
        (
            sds((rows, units)),
            sds((rows, width), jnp.float32),
            sds((rows, width)),
            sds((rows, width)),
            sds((8, width), jnp.float32),
            sds((8, units), jnp.float32),
        ),
        sizes.grid,
        [flat(width), flat(width), flat(units)] + [whole(w) for w in weights],
        (flat(units), flat(width), flat(width), flat(width), sizes.sums(width), sizes.sums(units)),
        2 * rows * width * (width + 2 * units),
        rows * (width * 16 + units * 4) + 2 * width * (width + 2 * units),
        after=after,
        name="encoder_feed_forward_back",
    )(info, grad, mid, slope, *weights)


def packed_back(grad_refs, w_ref):
    width = w_ref.shape[0]
    total = None
    for part, grad_ref in enumerate(grad_refs):
        here = grad_ref.shape[-1]
        for j in range(3):
            start = j * width + part * here
            term = dot(grad_ref[j], w_ref[:, start : start + here], NT)
            total = term if total is None else total + term
    return total


def decoder_back_kernel(
    info_ref,
    dpacked_ref,
    gm_ref,
    x_ref,
    source_ref,
    y_ref,
    encoded_ref,
    gain_ref,
    shift_ref,
    w_ref,
    w_proj_ref,
    enc_gain_ref,
    enc_shift_ref,
    grad_ref,
    grad_low_ref,
    sums_ref,
    enc_sums_ref,
    kept_ref,
    sent_ref,
    total_ref,
):
    dnormed = packed_back((dpacked_ref,), w_ref)
    gain = row_of(gain_ref, 0)
    _, unit, inverse = norm(x_ref[...], gain, row_of(shift_ref, 0))
    dx = gm_ref[...] + norm_back(dnormed, unit, inverse, gain)
    picker = picker_of(source_ref, info_ref[STRIP + pl.program_id(0)])
    taken = dot(picker, low(dx), NN)
    last = taken.shape[0] - 1
    dproj = low(jnp.where(last_row(taken.shape[0]), 0.0, taken))
    term = dot(encoded_ref[...], dproj, TN)
    half = kept_ref.shape[0]

    @pl.when(pl.program_id(0) == 0)
    def begin():
        total_ref[...] = term

    @pl.when(pl.program_id(0) > 0)
    def more():
        total_ref[...] += term

    @pl.when(pl.program_id(0) == pl.num_programs(0) - 1)
    def finish():
        kept_ref[...] = low(total_ref[pl.ds(pl.multiple_of(info_ref[0] * half, 8), half), :])
        sent_ref[...] = low(total_ref[pl.ds(pl.multiple_of((1 - info_ref[0]) * half, 8), half), :])

    dencoded = low(dot(dproj, w_proj_ref[...], NT)).astype(jnp.float32)
    enc_gain = row_of(enc_gain_ref, 2)
    _, unit_final, inverse_final = norm(y_ref[...], enc_gain, row_of(enc_shift_ref, 2))
    grad = norm_back(dencoded, unit_final, inverse_final, enc_gain)
    grad_ref[...] = grad
    grad_low_ref[...] = low(grad)
    add_rows(
        sums_ref,
        (
            col_sum(dnormed * unit),
            col_sum(dnormed),
            taken[last : last + 1],
            col_sum(dproj.astype(jnp.float32)),
        ),
    )
    add_rows(enc_sums_ref, (col_sum(dencoded * unit_final), col_sum(dencoded)))


def decoder_back_call(
    sizes,
    info,
    dpacked,
    gm,
    x,
    source,
    y,
    encoded,
    gains,
    shifts,
    w_qkv,
    w_proj,
    enc_gains,
    enc_shifts,
    after,
):
    strips, padded, rows = sizes.strips, sizes.padded, sizes.rows
    width = x.shape[2]
    wide = y.shape[2]
    weights = (gains, shifts, w_qkv, w_proj, enc_gains, enc_shifts)
    strip = sizes.strip
    return call(
        decoder_back_kernel,
        (
            sds((strips, padded, wide), jnp.float32),
            sds((strips, padded, wide)),
            sds((8, width), jnp.float32),
            sds((8, wide), jnp.float32),
            sds((wide // 2, width)),
            sds((wide // 2, width)),
        ),
        (strips, 1),
        [
            pl.BlockSpec((3, None, padded, width), lambda s, i, info: (0, s, 0, 0)),
            strip(width),
            strip(width),
            whole(source),
            strip(wide),
            strip(wide),
        ]
        + [whole(w) for w in weights],
        (
            strip(wide),
            strip(wide),
            sizes.sums(width),
            sizes.sums(wide),
            pl.BlockSpec((wide // 2, width), lambda s, i, info: (0, 0)),
            pl.BlockSpec((wide // 2, width), lambda s, i, info: (0, 0)),
        ),
        2 * rows * width * (3 * width + padded + 2 * wide),
        rows * (width * 16 + wide * 8) + 2 * width * (3 * width + wide),
        after=after,
        name="decoder_packed_back",
        scratch=[pltpu.VMEM((wide, width), jnp.float32)],
    )(info, dpacked, gm, x, source, y, encoded, *weights)


def encoder_back_kernel(
    info_ref, first_ref, second_ref, gm_ref, x_ref, gain_ref, shift_ref, w_ref, kept_ref, sent_ref, sums_ref, *, length
):
    dnormed = packed_back((first_ref, second_ref), w_ref)
    gain = row_of(gain_ref, 0)
    x = live_rows(x_ref[...], pl.program_id(1) * x_ref.shape[0], length)
    _, unit, inverse = norm(x, gain, row_of(shift_ref, 0))
    store_halves(
        info_ref, kept_ref, sent_ref, gm_ref[...] + norm_back(dnormed, unit, inverse, gain)
    )
    add_rows(sums_ref, (col_sum(dnormed * unit), col_sum(dnormed)))


def encoder_back_call(sizes, info, dpacked, gm, x, gains, shifts, w_qkv, after):
    rows, width = gm.shape
    weights = (gains, shifts, w_qkv)
    half = sds((1, sizes.length, width // 2))
    three = [part.reshape(3, rows, part.shape[-1]) for part in dpacked]
    return call(
        functools.partial(encoder_back_kernel, length=sizes.length),
        (half, half, sds((8, width), jnp.float32)),
        sizes.grid,
        [sizes.flat_three(part.shape[-1]) for part in three]
        + [sizes.flat(width), sizes.raw(width)]
        + [whole(w) for w in weights],
        (sizes.half(width // 2), sizes.half(width // 2), sizes.sums(width)),
        6 * rows * width * width,
        rows * width * 14 + 6 * width * width,
        after=after,
        name=f"encoder_packed_back_{sizes.at}",
    )(info, *three, gm, x, *weights)


class Job:
    def __init__(self, left, right, row_step, col_step, offset):
        self.half = left.shape[1] // 2
        self.width = right.shape[1]
        self.rows = left.shape[0]
        self.row_step, self.col_step, self.offset = row_step, col_step, offset
        self.down = self.half // row_step
        self.across = self.width // col_step
        self.count = self.down * self.across

    def at(self, step):
        here = jnp.clip(step - self.offset, 0, self.count - 1)
        if self.across == 1:
            return here, 0
        if self.down == 1:
            return 0, here
        return here // self.across, here % self.across

    def left(self, pick):
        return pl.BlockSpec(
            (self.rows, self.row_step),
            lambda step, info: (0, pick(info[0]) * self.down + self.at(step)[0]),
        )

    def right(self):
        return pl.BlockSpec((self.rows, self.col_step), lambda step, info: (0, self.at(step)[1]))

    def out(self):
        return pl.BlockSpec((self.row_step, self.col_step), lambda step, info: self.at(step))


def product_kernel(info_ref, *refs, jobs):
    step = pl.program_id(0)
    out = 3 * len(jobs)
    for place, (offset, count) in enumerate(jobs):
        mine_ref, other_ref, right_ref = refs[3 * place : 3 * place + 3]
        kept_ref, sent_ref = refs[out + 2 * place : out + 2 * place + 2]

        @pl.when((step >= offset) & (step < offset + count))
        def product():
            right = right_ref[...]
            sent_ref[...] = low(dot(other_ref[...], right, TN))
            kept_ref[...] = low(dot(mine_ref[...], right, TN))


def product_call(info, products, name, after=()):
    jobs, operands, in_specs, out_specs, out_shape = [], [], [], [], []
    offset = flops = moved = 0
    for left, right, row_step, col_step in products:
        job = Job(left, right, row_step, col_step, offset)
        offset += job.count
        jobs.append(job)
        operands += [left, left, right]
        in_specs += [job.left(lambda own: own), job.left(lambda own: 1 - own), job.right()]
        out_specs += [job.out(), job.out()]
        out_shape += [sds((job.half, job.width))] * 2
        flops += 4 * job.rows * job.half * job.width
        moved += 2 * job.rows * (2 * job.half + job.width) + 4 * job.half * job.width
    outs = call(
        functools.partial(product_kernel, jobs=[(job.offset, job.count) for job in jobs]),
        tuple(out_shape),
        (offset,),
        in_specs,
        tuple(out_specs),
        flops,
        moved,
        after=after,
        name=name,
    )(info, *operands)
    return [outs[2 * place : 2 * place + 2] for place in range(len(jobs))]


def decoder_products_kernel(
    info_ref, n_ref, dhid_ref, act_ref, cot_ref, mixed_ref, gb_ref, out_ref, *, steps, col_step, row_step, share
):
    step = pl.program_id(0)
    width = cot_ref.shape[1]
    folds = steps

    @pl.when(step < steps)
    def up():
        start = pl.multiple_of(step * col_step, GROUP)
        out_ref[:, pl.ds(start, col_step)] = low(dot(n_ref[...], dhid_ref[...], TN))

    @pl.when((step >= steps) & (step < 2 * steps))
    def down():
        product = dot(act_ref[...], cot_ref[...], TN).reshape(-1, folds, share, width)
        here = row_step // folds
        start = pl.multiple_of((step - steps) * here, share)
        for fold in range(folds):
            place = width * (folds + 1 + fold)
            out_ref[pl.ds(start, here), place : place + width] = low(
                product[:, fold].reshape(here, width)
            )

    @pl.when(step == 2 * steps)
    def out():
        out_ref[:, width * folds : width * (folds + 1)] = low(dot(mixed_ref[...], gb_ref[...], TN))


def decoder_products_call(info, n, dhid, act, cot, mixed, gb, share, name):
    rows, width = cot.shape
    units = dhid.shape[1]
    steps = units // width
    shape = (width, 2 * units + width)
    at = lambda first: lambda step, info: (0, jnp.clip(step - first, 0, steps - 1))
    return call(
        functools.partial(
            decoder_products_kernel, steps=steps, col_step=width, row_step=width, share=share
        ),
        sds(shape),
        (2 * steps + 1,),
        [
            whole(n),
            pl.BlockSpec((rows, width), at(0)),
            pl.BlockSpec((rows, width), at(steps)),
            whole(cot),
            whole(mixed),
            whole(gb),
        ],
        pl.BlockSpec(shape, lambda step, info: (0, 0)),
        2 * rows * width * (2 * units + width),
        2 * rows * (2 * units + 4 * width) + 2 * shape[0] * shape[1],
        name=name,
    )(info, n, dhid, act, cot, mixed, gb)


class Chain:
    def __init__(self, pairs, order, parts):
        self.pairs = pairs
        self.bits = list(range(pairs.bit_length() - 1))
        self.order = [bit for bit in order if bit < len(self.bits)]
        self.order += [bit for bit in self.bits if bit not in self.order]
        self.widths = [kept.shape[1] for kept, _ in parts]
        self.parts = [
            (kept.reshape(pairs, -1, kept.shape[1]), arrived.reshape(pairs, -1, kept.shape[1]))
            for kept, arrived in parts
        ]
        self.done = None

    def item(self):
        kept = self.parts[0][0]
        if not self.order:
            return ("last", self.parts, self.widths, None)
        bit = self.order[0]
        lower = sum(1 for other in self.bits if other < bit)
        return ("halve", self.parts, (kept.shape[0] >> (lower + 1), 1 << lower), bit)

    def take(self, outs):
        if not self.order:
            self.done = outs
            return []
        bit = self.order.pop(0)
        self.bits.remove(bit)
        kept, sent = outs
        route = [(place, place ^ (1 << bit)) for place in range(self.pairs)]
        self.parts = [(kept, lax.ppermute(sent, "dp", route))]
        return [sent]


class Total:
    def __init__(self, pairs, values):
        self.pairs = pairs
        bits = [1 << bit for bit in range((2 * pairs).bit_length() - 1)]
        bits = bits[-1:] + bits[:-1]
        self.left = [bits[place : place + 2] for place in range(0, len(bits), 2)]
        self.done = None
        self.launch(values)

    def launch(self, values):
        group = self.left.pop(0)
        masks = group + [sum(group)] if len(group) > 1 else group
        count = 2 * self.pairs
        arrived = [
            lax.ppermute(values, ("section", "dp"), [(place, place ^ mask) for place in range(count)])
            for mask in masks
        ]
        self.parts = [(values, *arrived)]
        self.sent = values

    def item(self):
        return ("add", self.parts, None, None)

    def take(self, outs):
        (values,) = outs
        if not self.left:
            self.done = values
            return []
        self.launch(values)
        return [values]


def round_kernel(info_ref, *refs, items, counts):
    place = 0
    out = sum(sum(widths) for _, widths, _, _ in items)
    for (kind, widths, how, bit), count in zip(items, counts):
        pairs = []
        for width in widths:
            pairs.append(refs[place : place + width])
            place += width
        outs = refs[out : out + count]
        out += count
        if kind == "add":
            outs[0][...] = sum(ref[...] for ref in pairs[0])
            continue

        def total(pair, index):
            return pair[0][index].astype(jnp.float32) + pair[1][index].astype(jnp.float32)

        if kind == "last":
            start = 0
            values = [total(pair, 0) for pair in pairs]
            whole_row = values[0] if len(values) == 1 else jnp.concatenate(values, axis=1)
            for ref, width in zip(outs, how):
                ref[...] = whole_row[:, start : start + width]
                start += width
            continue
        high, lower = how
        mine = (info_ref[BLOCK] >> bit) & 1
        for h in range(high):
            for l in range(lower):
                start = 0
                for pair in pairs:
                    width = pair[0].shape[-1]
                    for ref, chosen in zip(outs, (mine, 1 - mine)):
                        index = (h * 2 + chosen) * lower + l
                        ref[h * lower + l, :, start : start + width] = low(total(pair, index))
                    start += width


def round_call(info, chains, name, after=()):
    items = [chain.item() for chain in chains]
    operands, out_shape, counts, moved = [], [], [], 0
    for kind, parts, how, _ in items:
        for part in parts:
            operands += part
            moved += len(part) * part[0].size * part[0].dtype.itemsize
        shape = parts[0][0].shape
        if kind == "add":
            out_shape.append(sds(shape, jnp.float32))
            counts.append(1)
        elif kind == "last":
            out_shape += [sds((shape[1], width), jnp.float32) for width in how]
            counts.append(len(how))
        else:
            width = sum(part[0].shape[-1] for part in parts)
            out_shape += [sds((shape[0] // 2, shape[1], width))] * 2
            counts.append(2)
    plain = [(kind, [len(part) for part in parts], how, bit) for kind, parts, how, bit in items]
    outs = call(
        functools.partial(round_kernel, items=plain, counts=counts),
        tuple(out_shape),
        (1,),
        [whole(operand) for operand in operands],
        tuple(whole(shape) for shape in out_shape),
        moved,
        2 * moved,
        after=after,
        name=name,
    )(info, *operands)
    sent, start = [], 0
    for chain, count in zip(chains, counts):
        sent += chain.take(outs[start : start + count])
        start += count
    return sent


def across(values):
    return lax.ppermute(values, "section", [(0, 1), (1, 0)])


def arrange_kernel(info_ref, *refs, strips):
    *sources, out_ref = refs
    holder = info_ref[STRIP + 2 * strips + pl.program_id(0)]
    slot = info_ref[STRIP + 4 * strips + pl.program_id(0)]
    per = len(sources) // 2
    values = None
    for place in range(strips):
        kept, arrived = (
            (sources[place][0], sources[per + place][0])
            if per == strips
            else (sources[0][place], sources[1][place])
        )
        chosen = jnp.where(holder == info_ref[0], kept, arrived)
        values = chosen if values is None else jnp.where(slot == place, chosen, values)
    out_ref[0] = values


def arrange_call(info, kept, arrived, strips, name, after=()):
    _, length, half = kept[0].shape
    return call(
        functools.partial(arrange_kernel, strips=strips),
        sds((2 * strips, length, half)),
        (2 * strips,),
        [whole(array) for array in (*kept, *arrived)],
        pl.BlockSpec((1, length, half), lambda k, info: (k, 0, 0)),
        1,
        strips * length * half * 12,
        name=name,
        after=after,
    )(info, *kept, *arrived)


def gather_small_kernel(
    info_ref, up_enc, up_dec, enc, dec, dec_in, final, *rest
):
    *enc_in, out_ref = rest
    out_ref[...] = jnp.zeros_like(out_ref)
    wide, narrow = enc.shape[1], dec.shape[1]
    out_ref[0:1, : up_enc.shape[1]] = up_enc[0:1, :]
    out_ref[1:2, : up_dec.shape[1]] = up_dec[0:1, :]
    out_ref[2:6, :wide] = enc[0:4, :]
    out_ref[2:6, wide : wide + narrow] = dec[0:4, :]
    out_ref[2:6, wide + narrow : wide + 2 * narrow] = dec_in[0:4, :]
    out_ref[6:8, :wide] = final[0:2, :]
    out_ref[6:8, wide : 2 * wide] = sum(ref[0:2, :] for ref in enc_in)


def gather_small_call(info, values):
    shape = (8, values[0].shape[1])
    return call(
        gather_small_kernel,
        sds(shape, jnp.float32),
        (1,),
        [whole(value) for value in values],
        pl.BlockSpec(shape, lambda i, info: (0, 0)),
        shape[1],
        shape[1] * 64,
        name="small_rows",
    )(info, *values)


def unshuffled(parts):
    return jnp.concatenate(
        [
            part[:, (3 * group + j) * GROUP : (3 * group + j + 1) * GROUP]
            for j in range(3)
            for part in parts
            for group in range(part.shape[1] // (3 * GROUP))
        ],
        axis=1,
    )


def shares_kernel(info_ref, rows_ref, dec_qkv_ref, *refs, parts, wide, narrow, units, dec_units, count):
    block = info_ref[BLOCK]

    def share(first, last, start, width):
        values = rows_ref[first:last, start : start + width]
        part = width // count
        return pltpu.roll(values, width - block * part, 1)[:, :part]

    enc_qkv = [ref[...] for ref in refs[:parts]]
    outs = refs[parts:]
    bias_up_enc = share(0, 1, 0, units)
    bias_up_dec = share(1, 2, 0, dec_units)
    enc = share(2, 6, 0, wide)
    dec = share(2, 6, wide, narrow)
    dec_in = share(2, 6, wide + narrow, narrow)
    final = share(6, 8, 0, wide)
    enc_in = share(6, 8, wide, wide)
    for ref, value in zip(
        outs,
        (
            jnp.concatenate([enc_in[0:1], enc[0:1], final[0:1]], axis=0),
            jnp.concatenate([enc_in[1:2], enc[1:2], final[1:2]], axis=0),
            enc[2:4],
            bias_up_enc,
            dec_in[3:4],
            dec_in[2:3],
            jnp.concatenate([dec_in[0:1], dec[0:1]], axis=0),
            jnp.concatenate([dec_in[1:2], dec[1:2]], axis=0),
            dec[2:4],
            bias_up_dec,
            unshuffled([dec_qkv_ref[...]]),
            unshuffled(enc_qkv),
        ),
    ):
        ref[...] = value


def shares_call(info, rows, dec_qkv, enc_qkv, wide, narrow, units, dec_units, count):
    shapes = [
        (height, width // count)
        for height, width in (
            (3, wide),
            (3, wide),
            (2, wide),
            (1, units),
            (1, narrow),
            (1, narrow),
            (2, narrow),
            (2, narrow),
            (2, narrow),
            (1, dec_units),
        )
    ] + [dec_qkv.shape, (wide // count, 3 * wide)]
    return call(
        functools.partial(
            shares_kernel,
            parts=len(enc_qkv),
            wide=wide,
            narrow=narrow,
            units=units,
            dec_units=dec_units,
            count=count,
        ),
        tuple(sds(shape, jnp.float32) for shape in shapes),
        (1,),
        [whole(array) for array in (rows, dec_qkv, *enc_qkv)],
        tuple(pl.BlockSpec(shape, lambda i, info: (0, 0)) for shape in shapes),
        rows.size,
        rows.size * 4,
        name="shares",
    )(info, rows, dec_qkv, *enc_qkv)


def decoder_shares_kernel(info_ref, rows_ref, up_ref, out_ref, down_ref):
    width = out_ref.shape[1]
    units = up_ref.shape[1]
    share = up_ref.shape[0]
    rows = rows_ref[...].astype(jnp.float32)
    up_ref[...] = rows[:, :units]
    out_ref[...] = rows[:, units : units + width]
    for fold in range(units // width):
        start = units + (fold + 1) * width
        down_ref[fold * share : (fold + 1) * share, :] = rows[:, start : start + width]


def decoder_shares_call(info, rows, width, units, after):
    share = rows.shape[0]
    shapes = ((share, units), (share, width), (share * units // width, width))
    return call(
        decoder_shares_kernel,
        tuple(sds(shape, jnp.float32) for shape in shapes),
        (1,),
        [whole(rows)],
        tuple(pl.BlockSpec(shape, lambda i, info: (0, 0)) for shape in shapes),
        rows.size,
        rows.size * 6,
        name="decoder_shares",
        after=after,
    )(info, rows)


def place_table(length_rows, model_width):
    halfway = model_width // 2
    places = np.arange(length_rows, dtype=np.float64)[:, None]
    rates = np.exp(np.arange(halfway, dtype=np.float64) * (-math.log(10000.0) / halfway))[None, :]
    return np.concatenate([np.sin(places * rates), np.cos(places * rates)], axis=1).astype(
        np.float32
    )


def local(
    patches,
    visible,
    source,
    enc_gains,
    enc_shifts,
    enc_qkv,
    enc_out,
    enc_bias_out,
    enc_up,
    enc_bias_up,
    enc_down,
    enc_proj,
    proj_bias,
    mask_token,
    dec_gains,
    dec_shifts,
    dec_qkv,
    dec_out,
    dec_bias_out,
    dec_up,
    dec_bias_up,
    dec_down,
    cotangent,
):
    pairs = lax.axis_size("dp")
    count = 2 * pairs
    length = patches.shape[1]
    wide = patches.shape[2]
    narrow = dec_qkv.shape[0]
    strips = patches.shape[0] // 2
    padded = -(-(length + 1) // ROW_STEP) * ROW_STEP
    sizes = Sizes(strips, length, padded)
    rows = sizes.rows
    info = place_info(visible, strips)
    taken = jnp.pad(
        jnp.where(source < 0, padded - 1, source),
        ((0, 0), (0, padded - length)),
        constant_values=padded - 1,
    )
    places = jnp.asarray(place_table(padded, narrow))
    strip_form = lambda array: array.reshape(strips, padded, array.shape[-1])
    row_form = lambda array: array.reshape(rows, array.shape[-1])

    n1_enc, packed_enc = packed_call(sizes, info, patches, enc_gains, enc_shifts, enc_qkv)
    packed_enc = strip_form(packed_enc)
    enc_live = visible_live(strips)
    mixed_enc = row_form(attend_call(packed_enc, info, HEADS_ENC, enc_live, "encoder_attention"))
    mid_enc, n2_enc, act_enc, slope_enc, y_enc, encoded, projected = encoder_ff_call(
        sizes,
        info,
        patches,
        mixed_enc,
        enc_gains,
        enc_shifts,
        enc_out,
        enc_bias_out,
        enc_up,
        enc_bias_up,
        enc_down,
        enc_proj,
        proj_bias,
    )
    x_dec, n1_dec, packed_dec = decoder_in_call(
        sizes, info, projected, taken, mask_token, places, dec_gains, dec_shifts, dec_qkv
    )
    dec_live = all_live(length)
    mixed_dec = row_form(attend_call(packed_dec, info, HEADS_DEC, dec_live, "decoder_attention"))
    (
        kept_dec,
        sent_dec,
        cot,
        n2_dec,
        act_dec,
        dhid_dec,
        gm_dec,
        gb_dec,
        dmixed_dec,
        sums_dec,
        up_sums_dec,
    ) = decoder_ff_call(
        sizes,
        info,
        row_form(x_dec),
        mixed_dec,
        cotangent,
        dec_gains,
        dec_shifts,
        dec_out,
        dec_bias_out,
        dec_up,
        dec_bias_up,
        dec_down,
    )
    dec_half, enc_half = narrow // 2, wide // 2
    share = narrow // count
    folded = share % 8 == 0
    if folded:
        beside = decoder_products_call(
            info, n2_dec, dhid_dec, act_dec, cot, mixed_dec, gb_dec, share, "grad_dec_weights"
        )
        summed = lax.psum_scatter(
            beside.reshape(count, share, -1), ("section", "dp"), scatter_dimension=0, tiled=True
        )[0]
        first_sent = (beside,)
    else:
        pieces = product_call(
            info,
            [
                (act_dec, cot, narrow, narrow),
                (n2_dec, dhid_dec, dec_half, narrow),
                (mixed_dec, gb_dec, dec_half, narrow),
            ],
            "grad_dec_weights",
        )
        first_sent = tuple(sent for _, sent in pieces)
        dec_chains = [
            Chain(pairs, (1, 0, 2, 3), ((kept, across(sent)),)) for kept, sent in pieces
        ]
    arrived_dec = across(sent_dec)
    dpacked_dec, kept_dqkv, sent_dqkv = attend_back_call(
        packed_dec,
        strip_form(dmixed_dec),
        n1_dec,
        info,
        HEADS_DEC,
        dec_live,
        0,
        1,
        (*first_sent, sent_dec),
        "decoder_attention_back",
    )
    arrived_dqkv = across(sent_dqkv)
    grad_enc, grad_enc_low, sums_dec_in, sums_final, kept_proj, sent_proj = decoder_back_call(
        sizes,
        info,
        dpacked_dec,
        strip_form(gm_dec),
        x_dec,
        taken,
        strip_form(y_enc),
        strip_form(encoded),
        dec_gains,
        dec_shifts,
        dec_qkv,
        enc_proj,
        enc_gains,
        enc_shifts,
        (sent_dqkv,),
    )
    grad_enc, grad_enc_low = map(row_form, (grad_enc, grad_enc_low))
    arrived_proj = across(sent_proj)
    qkv_dec = Chain(pairs, (0, 1, 2, 3), ((kept_dqkv, arrived_dqkv),))
    sent = round_call(info, [qkv_dec], "round_1", (grad_enc_low,))
    ((kept_edown, sent_edown),) = product_call(
        info, [(act_enc, grad_enc_low, enc_half, wide)], "grad_enc_down", (*sent, sent_proj)
    )
    arrived_edown = across(sent_edown)
    sent = round_call(info, [qkv_dec], "round_2", (kept_edown,))
    dhid_enc, gm_enc, gb_enc, dmixed_enc, sums_enc, up_sums_enc = encoder_ff_back_call(
        sizes,
        info,
        grad_enc,
        mid_enc,
        slope_enc,
        enc_gains,
        enc_shifts,
        enc_out,
        enc_up,
        enc_down,
        (*sent, sent_edown),
    )
    down_enc = Chain(pairs, (1, 2, 0, 3), ((kept_edown, arrived_edown),))
    sent = round_call(info, [qkv_dec], "round_3", (gb_enc,))
    (kept_eup, sent_eup), (kept_eout, sent_eout) = product_call(
        info,
        [(n2_enc, dhid_enc, enc_half, wide), (mixed_enc, gb_enc, enc_half, wide)],
        "grad_enc_up_out",
        sent,
    )
    arrived_eup, arrived_eout = map(across, (sent_eup, sent_eout))
    sent = round_call(info, [down_enc, qkv_dec], "round_4", (kept_eout,))
    half_back = lambda part, after: attend_back_call(
        packed_enc,
        strip_form(dmixed_enc),
        strip_form(n1_enc),
        info,
        HEADS_ENC,
        enc_live,
        part,
        2,
        after,
        f"encoder_attention_back_{part}",
    )
    dpacked_one, kept_one, sent_one = half_back(0, (*sent, sent_eup, sent_eout))
    arrived_one = across(sent_one)
    up_enc = Chain(pairs, (0, 1, 2, 3), ((kept_eup, arrived_eup),))
    out_enc = Chain(pairs, (2, 0, 1, 3), ((kept_eout, arrived_eout), (kept_proj, arrived_proj)))
    chains = [up_enc, down_enc, out_enc]
    sent = round_call(info, [*chains, qkv_dec], "round_5", (kept_one,))
    dpacked_two, kept_two, sent_two = half_back(1, (*sent, sent_one))
    arrived_two = across(sent_two)
    one_chain = Chain(pairs, (2, 0, 1, 3), ((kept_one, arrived_one),))
    chains += [one_chain]
    sent = round_call(info, chains, "round_6", (kept_two,))
    decoded = arrange_call(info, [kept_dec], [arrived_dec], strips, "decoded_strips", (kept_two,))
    back = lambda strip, after: encoder_back_call(
        OneStrip(sizes, strip),
        info,
        (dpacked_one, dpacked_two),
        gm_enc,
        patches,
        enc_gains,
        enc_shifts,
        enc_qkv,
        after,
    )
    kept_enc, arrived_enc, sums_enc_in = [], [], []
    after = (*sent, sent_two)
    for strip in range(strips):
        kept, sent_here, sums = back(strip, after)
        kept_enc.append(kept)
        arrived_enc.append(across(sent_here))
        sums_enc_in.append(sums)
        if strip == 0:
            two_chain = Chain(pairs, (1, 0, 2, 3), ((kept_two, arrived_two),))
            chains = [two_chain, *chains]
            sent = round_call(info, chains, "round_7", (sums,))
            after = (*sent, sent_here)
    small = Total(
        pairs,
        gather_small_call(
            info,
            (up_sums_enc, up_sums_dec, sums_enc, sums_dec, sums_dec_in, sums_final, *sums_enc_in),
        ),
    )
    after = (small.sent, sent_here)
    if not folded:
        chains += dec_chains
    number = 8
    every = [*chains, qkv_dec, small]
    while any(chain.done is None for chain in every):
        active = [chain for chain in every if chain.done is None]
        sent = round_call(info, active, f"round_{number}", after)
        if number == 8:
            patch_grad = arrange_call(
                info, kept_enc, arrived_enc, strips, "patch_grad_strips", tuple(sent)
            )
            after = (patch_grad,)
        else:
            after = ()
        number += 1
    (g_dqkv,), (g_one,), (g_two,) = qkv_dec.done, one_chain.done, two_chain.done
    shares = shares_call(
        info, small.done, g_dqkv, (g_one, g_two), wide, narrow, enc_up.shape[1], dec_up.shape[1], count
    )
    if folded:
        g_dup, g_dout, g_ddown = decoder_shares_call(
            info, summed, narrow, dec_up.shape[1], (kept_two,)
        )
    else:
        (g_ddown,), (g_dup,), (g_dout,) = [chain.done for chain in dec_chains]
    (g_edown,), (g_eup,), (g_eout, g_proj) = down_enc.done, up_enc.done, out_enc.done
    return (
        decoded,
        patch_grad,
        shares[0],
        shares[1],
        shares[11],
        g_eout,
        shares[2],
        g_eup,
        shares[3].reshape(-1),
        g_edown,
        g_proj,
        shares[4].reshape(-1),
        shares[5].reshape(-1),
        shares[6],
        shares[7],
        shares[10],
        g_dout,
        shares[8],
        g_dup,
        shares[9].reshape(-1),
        g_ddown,
    )


def solution(mesh):
    return jax.shard_map(
        local,
        mesh=mesh,
        in_specs=(
            P("dp", None, None),
            P("dp"),
            P("dp", None),
            P(),
            P(),
            P(),
            P(),
            P(),
            P(),
            P(),
            P(),
            P(),
            P(),
            P(),
            P(),
            P(),
            P(),
            P(),
            P(),
            P(),
            P(),
            P(),
            P("dp", None, None),
        ),
        out_specs=(
            P("dp", None, "section"),
            P("dp", None, "section"),
            P(None, ("section", "dp")),
            P(None, ("section", "dp")),
            P(("section", "dp"), None),
            P(("section", "dp"), None),
            P(None, ("section", "dp")),
            P(("section", "dp"), None),
            P(("section", "dp")),
            P(("section", "dp"), None),
            P(("section", "dp"), None),
            P(("section", "dp")),
            P(("section", "dp")),
            P(None, ("section", "dp")),
            P(None, ("section", "dp")),
            P(("section", "dp"), None),
            P(("section", "dp"), None),
            P(None, ("section", "dp")),
            P(("section", "dp"), None),
            P(("section", "dp")),
            P(("section", "dp"), None),
        ),
        check_vma=False,
    )
```

time: 1340 us -> 505 us (0.38)
  waiting for transfers between devices: 583 us -> 43.9 us
  matrix products: 409 us -> 0 us
  Pallas kernels: 0 us -> 379 us
  other arithmetic: 167 us -> 0.01 us
  local copies, waits for them, and re-layouts: 113 us -> 24.5 us
  blocking collectives: 43 us -> 0 us
  starting transfers between devices: 1.28 us -> 34.2 us
    reduce_scatter x9 -> x1, waiting for transfers between devices: 583 us -> 0.01 us  [local(): lax.psum_scatter(beside.reshape(count, share, -1), ('section', 'dp'), sca...]
    pallas_call x0 -> x32, Pallas kernels: none -> 379 us  [call(): return lambda *operands: made(*operands, *after)]
    dot_general x38 -> x0, matrix products: 370 us -> none  [the longest x9 74.2 us: backward_product(): jnp.einsum('blf,df->bld', left_side, right_side, preferred_element_type=j...]
    convert_element_type x22 -> x0, other arithmetic: 142 us -> none  [the longest x2 63.7 us: attend_grad(): grad_scores = (weights_full * (grad_weights - jnp.sum(weights_full * grad...]
    ppermute x2 -> x41, waiting for transfers between devices: 0.01 us -> 43.8 us  [the longest x24 41.1 us: take(): self.parts = [(kept, lax.ppermute(sent, 'dp', route))]]
    unnamed x1 -> x0, blocking collectives: 43 us -> none
    sub x2 -> x0, matrix products: 39.1 us -> none  [attend(): exp_terms = jnp.exp(scores - highest)]
    reshape x22 -> x0, local copies, waits for them, and re-layouts: 36 us -> none  [the longest x10 14.5 us: small_scatter(): jnp.moveaxis(grad_value, axis_dim, 0).reshape(count, -1)]
  transfers between devices with their start and end apart: 11 -> 42, of which waited for: 5 -> 11; matrix products, arithmetic and copies ran while one was open for 32% -> 1% of each run, Pallas kernels for 0% -> 37%
where the time goes in v2:
time: 505 us; the launch traced here: 496 us
  Pallas kernels  379 us (75%)
  waiting for transfers between devices  43.9 us (9%)
  starting transfers between devices  34.2 us (7%)
  local copies, waits for them, and re-layouts  24.5 us (5%)
  between operations  15.1 us (3%)
    pallas_call x32, Pallas kernels, call(): return lambda *operands: made(*operands, *after)  379 us
    ppermute x24, waiting for transfers between devices, take(): self.parts = [(kept, lax.ppermute(sent, 'dp', route))]  41.1 us
    ppermute x24, starting transfers between devices, take(): self.parts = [(kept, lax.ppermute(sent, 'dp', route))]  22.1 us
    unnamed x116, local copies, waits for them, and re-layouts  21.9 us
  transfers between devices with their start and end apart: 42, of which 11 were waited for; matrix products, arithmetic and copies ran while one was open for 1% of the time, Pallas kernels for 37%

profile of v2, /device:TPU:0, one launch (start us, length us, event | category | flops | bytes accessed | tf_op | source)
XLA Modules:
  0.0 496.3 jit_solution(5607764479627021009)
XLA Ops:
  7.3 4.1 copy.53.refs_1_.refs_4_
  12.1 9.5 %encoder_packed.1 = (bf16[1088,768]{1,0:T(8,128)(2,1)}, bf16[1088,2304]{1,0:T(8,128)(2,1)}) custom-call(s32[14]{0:T(128)} %concatenate.3.refs_0_, bf16[4,529,768]{2,1,0:T(8,128)(2,1)} %copy.53.refs_1_.refs_4_, bf16[3,768]{1,0:T(4,128)(2,1)} %refs_5_.11, bf16[3,768]{1,0:T(4,128)(2,1)} %refs_6_.11, bf16[768,2304]{1,0:T(8,128)(2,1)} %refs_7_.13), custom_call_target="tpu_custom_call" | custom-call | flops 15040512 | bytes 46464 | tf_op jit(solution)/shard_map/encoder_packed/pallas_call | solution.py:58
  21.6 22.3 %encoder_attention.1 = bf16[2,544,768]{2,1,0:T(8,128)(2,1)} custom-call(s32[14]{0:T(128)} %concatenate.3.refs_0_, bf16[2,544,2304]{2,1,0:T(8,128)(2,1)} %bitcast.37, bf16[2,544,2304]{2,1,0:T(8,128)(2,1)} %bitcast.38, bf16[2,544,2304]{2,1,0:T(8,128)(2,1)} %bitcast.39), custom_call_target="tpu_custom_call" | custom-call | flops 21307392 | bytes 26112 | tf_op jit(solution)/shard_map/encoder_attention/pallas_call | solution.py:58
  44.5 30.4 %encoder_feed_forward.1 = (f32[1088,768]{1,0:T(8,128)}, bf16[1088,768]{1,0:T(8,128)(2,1)}, bf16[1088,3072]{1,0:T(8,128)(2,1)}, bf16[1088,3072]{1,0:T(8,128)(2,1)...) custom-call(s32[14]{0:T(128)} %concatenate.3.refs_0_, ...), custom_call_target="tpu_custom_call" | custom-call | flops 48463872 | bytes 148992 | tf_op jit(solution)/shard_map/encoder_feed_forward/pallas_call | solution.py:58
  74.9 7.6 %decoder_packed.1 = (f32[2,544,512]{2,1,0:T(8,128)}, bf16[2,544,512]{2,1,0:T(8,128)(2,1)}, bf16[2,544,1536]{2,1,0:T(8,128)(2,1)}) custom-call(s32[14]{0:T(128)} %concatenate.3.refs_0_, bf16[2,544,512]{2,1,0:T(8,128)(2,1)} %bitcast.75, s32[4,544]{1,0:T(4,128)} %pad.4.refs_2_.refs_4_, bf16[512]{0:T(512)(128)(2,1)} %refs_3_.6, ...), custom_call_target="tpu_custom_call" | custom-call | flops 9052160 | bytes 45312 | tf_op jit(solution)/shard_map/decoder_packed/pallas_call | solution.py:58
  82.5 25.1 %decoder_attention.1 = bf16[2,544,512]{2,1,0:T(8,128)(2,1)} custom-call(s32[14]{0:T(128)} %concatenate.3.refs_0_, bf16[2,544,1536]{2,1,0:T(8,128)(2,1)} %get-tuple-element.152.refs_1_.refs_2_.refs_3_, bf16[2,544,1536]{2,1,0:T(8,128)(2,1)} %get-tuple-element.152.refs_1_.refs_2_.refs_3_, bf16[2,544,1536]{2,1,0:T(8,128)(2,1)} %get-tuple-element.152.refs_1_.refs_2_.refs_3_), custom_call_target="tpu_custom_call" | custom-call | flops 28409856 | bytes 17408 | tf_op jit(solution)/shard_map/decoder_attention/pallas_call | solution.py:58
  109.4 26.7 %decoder_feed_forward.1 = (bf16[2,529,256]{2,1,0:T(8,128)(2,1)}, bf16[2,529,256]{2,1,0:T(8,128)(2,1)}, bf16[1088,512]{1,0:T(8,128)(2,1)}, bf16[1088,512]{1,0:T(8...) custom-call(s32[14]{0:T(128)} %concatenate.3.refs_0_, ...), custom_call_target="tpu_custom_call" | custom-call | flops 40108032 | bytes 101120 | tf_op jit(solution)/shard_map/decoder_feed_forward/pallas_call | solution.py:58
  136.1 15.0 %grad_dec_weights.1.refs_6_ = bf16[512,4608]{1,0:T(8,128)(2,1)} custom-call(s32[14]{0:T(128)} %concatenate.3.refs_0_, bf16[1088,512]{1,0:T(8,128)(2,1)} %get-tuple-element.157.refs_1_, bf16[1088,2048]{1,0:T(8,128)(2,1)} %get-tuple-element.158.refs_2_, bf16[1088,2048]{1,0:T(8,128)(2,1)} %get-tuple-element.159.refs_3_, ...), custom_call_target="tpu_custom_call" | custom-call | flops 20054016 | bytes 70656 | tf_op jit(solution)/shard_map/grad_dec_weights/pallas_call | solution.py:58
  151.1 52.4 %decoder_attention_back.1 = (bf16[3,2,544,512]{3,2,1,0:T(8,128)(2,1)}, bf16[256,1536]{1,0:T(8,128)(2,1)}, bf16[256,1536]{1,0:T(8,128)(2,1)}) custom-call(s32[14]{0:T(128)} %concatenate.3.refs_0_, bf16[2,544,1536]{2,1,0:T(8,128)(2,1)} %get-tuple-element.152.refs_1_.refs_2_.refs_3_, bf16[2,544,1536]{2,1,0:T(8,128)(2,1)} %get-tuple-element.152.refs_1_.refs_2_.refs_3_, ...), custom_call_target="tpu_custom_call" | custom-call | flops 63504384 | bytes 30464 | tf_op jit(solution)/shard_map/decoder_attention_back/pallas_call | solution.py:58
  204.0 15.6 %decoder_packed_back.1 = (f32[2,544,768]{2,1,0:T(8,128)}, bf16[2,544,768]{2,1,0:T(8,128)(2,1)}, f32[8,512]{1,0:T(8,128)}, f32[8,768]{1,0:T(8,128)}, bf16[384,512]{1,0:T(8,128)(2,1)}, /*index=5*/bf16[384,512]{1,0:T(8,128)(2,1)}) custom-call(s32[14]{0:T(128)} %concatenate.3.refs_0_, bf16[3,2,544,512]{3,2,1,0:T(8,128)(2,1)} %get-tuple-element.162.refs_1_, ...), custom_call_target="tpu_custom_call" | custom-call | flops 15736832 | bytes 70144 | tf_op jit(solution)/shard_map/decoder_packed_back/pallas_call | solution.py:58
  220.5 3.2 round_1.1
  223.6 11.2 %grad_enc_down.1 = (bf16[1536,768]{1,0:T(8,128)(2,1)}, bf16[1536,768]{1,0:T(8,128)(2,1)}) custom-call(s32[14]{0:T(128)} %concatenate.3.refs_0_, bf16[1088,3072]{1,0:T(8,128)(2,1)} %get-tuple-element.174.refs_1_.refs_2_, bf16[1088,3072]{1,0:T(8,128)(2,1)} %get-tuple-element.174.refs_1_.refs_2_, bf16[1088,768]{1,0:T(8,128)(2,1)} %bitcast.60, ...), custom_call_target="tpu_custom_call" | custom-call | flops 20054016 | bytes 51072 | tf_op jit(solution)/shard_map/grad_enc_down/pallas_call | solution.py:58
  237.9 9.4 %collective-permute-done.2.refs_2_ = bf16[8,16,1536]{2,1,0:T(8,128)(2,1)S(1)} collective-permute-done((bf16[8,16,1536]{2,1,0:T(8,128)(2,1)S(1)}, bf16[8,16,1536]{2,1,0:T(8,128)(2,1)S(1)}, u32[]{:S(2)}, u32[]{:S(2)}) %collective-permute-start.2) | collective-permute-done | bytes 393248 | tf_op jit(solution)/shard_map/ppermute | solution.py:1020
  252.4 23.4 %encoder_feed_forward_back.1 = (bf16[1088,3072]{1,0:T(8,128)(2,1)}, f32[1088,768]{1,0:T(8,128)}, bf16[1088,768]{1,0:T(8,128)(2,1)}, bf16[1088,768]{1,0:T(8,128)(...) custom-call(s32[14]{0:T(128)} %concatenate.3.refs_0_, f32[1088,768]{1,0:T(8,128)} %bitcast.66, ...), custom_call_target="tpu_custom_call" | custom-call | flops 45121536 | bytes 145920 | tf_op jit(solution)/shard_map/encoder_feed_forward_back/pallas_call | solution.py:58
  278.9 14.2 %grad_enc_up_out.1 = (bf16[384,3072]{1,0:T(8,128)(2,1)}, bf16[384,3072]{1,0:T(8,128)(2,1)}, bf16[384,768]{1,0:T(8,128)(2,1)}, bf16[384,768]{1,0:T(8,128)(2,1)}) custom-call(s32[14]{0:T(128)} %concatenate.3.refs_0_, bf16[1088,768]{1,0:T(8,128)(2,1)} %get-tuple-element.181.refs_1_.refs_2_, bf16[1088,768]{1,0:T(8,128)(2,1)} %get-tuple-element.181.refs_1_.refs_2_, ...), custom_call_target="tpu_custom_call" | custom-call | flops 25067520 | bytes 68736 | tf_op jit(solution)/shard_map/grad_enc_up_out/pallas_call | solution.py:58
  294.4 4.4 collective-permute-done.6.refs_4_
  300.2 5.2 %round_4.1 = (bf16[8,96,768]{2,1,0:T(8,128)(2,1)}, bf16[8,96,768]{2,1,0:T(8,128)(2,1)}, bf16[1,16,1536]{2,1,0:T(8,128)(2,1)}, bf16[1,16,1536]{2,1,0:T(8,128)(2,1)}) custom-call(s32[14]{0:T(128)} %concatenate.3.refs_0_, bf16[16,96,768]{2,1,0:T(8,128)(2,1)} %bitcast.57, bf16[16,96,768]{2,1,0:T(8,128)(2,1)} %bitcast.71, ...), custom_call_target="tpu_custom_call" | custom-call | flops 19200 | bytes 38400 | tf_op jit(solution)/shard_map/round_4/pallas_call | solution.py:58
  308.1 26.0 %encoder_attention_back_0.1 = (bf16[3,2,544,384]{3,2,1,0:T(8,128)(2,1)}, bf16[384,1152]{1,0:T(8,128)(2,1)}, bf16[384,1152]{1,0:T(8,128)(2,1)}) custom-call(s32[14]{0:T(128)} %concatenate.3.refs_0_, bf16[2,544,2304]{2,1,0:T(8,128)(2,1)} %bitcast.40, bf16[2,544,2304]{2,1,0:T(8,128)(2,1)} %bitcast.41, bf16[2,544,2304]{2,1,0:T(8,128)(2,1)} %bitcast.42, ...), custom_call_target="tpu_custom_call" | custom-call | flops 28827648 | bytes 22848 | tf_op jit(solution)/shard_map/encoder_attention_back_0/pallas_call | solution.py:58
  336.3 7.4 %round_5.1 = (bf16[8,24,3072]{2,1,0:T(8,128)(2,1)}, bf16[8,24,3072]{2,1,0:T(8,128)(2,1)}, bf16[4,96,768]{2,1,0:T(8,128)(2,1)}, bf16[4,96,768]{2,1,0:T(8,128)(2,1...) custom-call(s32[14]{0:T(128)} %concatenate.3.refs_0_, ...), custom_call_target="tpu_custom_call" | custom-call | flops 35712 | bytes 71424 | tf_op jit(solution)/shard_map/round_5/pallas_call | solution.py:58
  347.2 25.9 %encoder_attention_back_1.1 = (bf16[3,2,544,384]{3,2,1,0:T(8,128)(2,1)}, bf16[384,1152]{1,0:T(8,128)(2,1)}, bf16[384,1152]{1,0:T(8,128)(2,1)}) custom-call(s32[14]{0:T(128)} %concatenate.3.refs_0_, bf16[2,544,2304]{2,1,0:T(8,128)(2,1)} %bitcast.43, bf16[2,544,2304]{2,1,0:T(8,128)(2,1)} %bitcast.44, bf16[2,544,2304]{2,1,0:T(8,128)(2,1)} %bitcast.45, ...), custom_call_target="tpu_custom_call" | custom-call | flops 28827648 | bytes 22848 | tf_op jit(solution)/shard_map/encoder_attention_back_1/pallas_call | solution.py:58
  374.8 5.6 %round_6.1 = (bf16[4,24,3072]{2,1,0:T(8,128)(2,1)}, bf16[4,24,3072]{2,1,0:T(8,128)(2,1)}, bf16[2,96,768]{2,1,0:T(8,128)(2,1)}, bf16[2,96,768]{2,1,0:T(8,128)(2,1...) custom-call(s32[14]{0:T(128)} %concatenate.3.refs_0_, ...), custom_call_target="tpu_custom_call" | custom-call | flops 24576 | bytes 49152 | tf_op jit(solution)/shard_map/round_6/pallas_call | solution.py:58
  385.8 8.0 %encoder_packed_back_0.1 = (bf16[1,529,384]{2,1,0:T(8,128)(2,1)}, bf16[1,529,384]{2,1,0:T(8,128)(2,1)}, f32[8,768]{1,0:T(8,128)}) custom-call(s32[14]{0:T(128)} %concatenate.3.refs_0_, bf16[3,1088,384]{2,1,0:T(8,128)(2,1)} %bitcast.51, bf16[3,1088,384]{2,1,0:T(8,128)(2,1)} %bitcast.53, f32[1088,768]{1,0:T(8,128)} %get-tuple-element.204.refs_3_, ...), custom_call_target="tpu_custom_call" | custom-call | flops 15040512 | bytes 59520 | tf_op jit(solution)/shard_map/encoder_packed_back_0/pallas_call | solution.py:58
  393.8 4.3 collective-permute-done.18.refs_8_
  399.3 4.9 round_7.1
  404.3 8.3 %encoder_packed_back_1.1 = (bf16[1,529,384]{2,1,0:T(8,128)(2,1)}, bf16[1,529,384]{2,1,0:T(8,128)(2,1)}, f32[8,768]{1,0:T(8,128)}) custom-call(s32[14]{0:T(128)} %concatenate.3.refs_0_, bf16[3,1088,384]{2,1,0:T(8,128)(2,1)} %bitcast.52, bf16[3,1088,384]{2,1,0:T(8,128)(2,1)} %bitcast.54, f32[1088,768]{1,0:T(8,128)} %get-tuple-element.204.refs_3_, ...), custom_call_target="tpu_custom_call" | custom-call | flops 15040512 | bytes 59520 | tf_op jit(solution)/shard_map/encoder_packed_back_1/pallas_call | solution.py:58
  423.2 4.1 collective-permute-done.24.refs_6_
  430.0 5.9 %collective-permute-done.23.refs_4_ = bf16[2,24,3072]{2,1,0:T(8,128)(2,1)S(1)} collective-permute-done((bf16[2,24,3072]{2,1,0:T(8,128)(2,1)S(1)}, bf16[2,24,3072]{2,1,0:T(8,128)(2,1)S(1)}, u32[]{:S(2)}, u32[]{:S(2)}) %collective-permute-start.23) | collective-permute-done | bytes 294944 | tf_op jit(solution)/shard_map/ppermute | solution.py:1020
  436.8 3.6 round_8.1
  444.1 4.4 collective-permute-done.32.refs_6_
  451.6 3.9 patch_grad_strips.1.refs_13_
  463.0 5.6 %collective-permute-done.38.refs_4_ = bf16[1,24,1152]{2,1,0:T(8,128)(2,1)S(1)} collective-permute-done((bf16[1,24,1152]{2,1,0:T(8,128)(2,1)}, bf16[1,24,1152]{2,1,0:T(8,128)(2,1)S(1)}, u32[]{:S(2)}, u32[]{:S(2)}) %collective-permute-start.38) | collective-permute-done | bytes 55328 | tf_op jit(solution)/shard_map/ppermute | solution.py:1020
  473.3 3.5 decoded_strips.1
  (209 shorter events, 80.1 us)
Async XLA Ops:
  7.2 472.4 %reduce-scatter.2.cloned.1.call-start = ((), (), s32[]{:S(2)}) async-start(), calls=%async_computation.1 | async-start | bytes 4866048 | tf_op jit(solution)/shard_map/reduce_scatter | solution.py:1419
  203.5 16.1 %collective-permute-start.1 = (bf16[256,1536]{1,0:T(8,128)(2,1)}, bf16[256,1536]{1,0:T(8,128)(2,1)S(1)}, u32[]{:S(2)}, u32[]{:S(2)}) collective-permute-start(bf16[256,1536]{1,0:T(8,128)(2,1)} %get-tuple-element.166.refs_13_), channel_id=1, source_target_pairs={{0,16},{16,0},{1,17},{17,1},{2,18},{18,2},{3,19},{19,3},{4,20},{20... | collective-permute-start | bytes 2359304 | tf_op jit(solution)/shard_map/ppermute | solution.py:1132
  234.8 64.0 %collective-permute-start.5 = (bf16[1536,768]{1,0:T(8,128)(2,1)}, bf16[1536,768]{1,0:T(8,128)(2,1)S(1)}, u32[]{:S(2)}, u32[]{:S(2)}) collective-permute-start(bf16[1536,768]{1,0:T(8,128)(2,1)} %get-tuple-element.178.refs_10_), channel_id=1, source_target_pairs={{0,16},{16,0},{1,17},{17,1},{2,18},{18,2},{3,19},{19,3},{4,20},{20... | collective-permute-start | bytes 7077896 | tf_op jit(solution)/shard_map/ppermute | solution.py:1132
  234.9 12.3 %collective-permute-start.2 = (bf16[8,16,1536]{2,1,0:T(8,128)(2,1)S(1)}, bf16[8,16,1536]{2,1,0:T(8,128)(2,1)S(1)}, u32[]{:S(2)}, u32[]{:S(2)}) collective-permute-start(bf16[8,16,1536]{2,1,0:T(8,128)(2,1)S(1)} %copy-done.25), channel_id=1, source_target_pairs={{0,1},{1,0},{2,3},{3,2},{4,5},{5,4},{6,7},{7,6},{8,9},{9,8},{10,11... | collective-permute-start | bytes 1179656 | tf_op jit(solution)/shard_map/ppermute | solution.py:1020
  250.6 25.2 %collective-permute-start.3 = (bf16[4,16,1536]{2,1,0:T(8,128)(2,1)}, bf16[4,16,1536]{2,1,0:T(8,128)(2,1)S(1)}, u32[]{:S(2)}, u32[]{:S(2)}) collective-permute-start(bf16[4,16,1536]{2,1,0:T(8,128)(2,1)} %get-tuple-element.177.refs_9_), channel_id=1, source_target_pairs={{0,2},{1,3},{2,0},{3,1},{4,6},{5,7},{6,4},{7,5},{8,10},{9,11},{10,... | collective-permute-start | bytes 589832 | tf_op jit(solution)/shard_map/ppermute | solution.py:1020
  293.0 41.1 %collective-permute-start.4 = (bf16[384,3072]{1,0:T(8,128)(2,1)}, bf16[384,3072]{1,0:T(8,128)(2,1)S(1)}, u32[]{:S(2)}, u32[]{:S(2)}) collective-permute-start(bf16[384,3072]{1,0:T(8,128)(2,1)} %get-tuple-element.187.refs_8_), channel_id=1, source_target_pairs={{0,16},{16,0},{1,17},{17,1},{2,18},{18,2},{3,19},{19,3},{4,20},{20... | collective-permute-start | bytes 7077896 | tf_op jit(solution)/shard_map/ppermute | solution.py:1132
  305.4 28.8 %collective-permute-start.7 = (bf16[8,96,768]{2,1,0:T(8,128)(2,1)}, bf16[8,96,768]{2,1,0:T(8,128)(2,1)S(1)}, u32[]{:S(2)}, u32[]{:S(2)}) collective-permute-start(bf16[8,96,768]{2,1,0:T(8,128)(2,1)} %get-tuple-element.191.refs_6_), channel_id=1, source_target_pairs={{0,2},{1,3},{2,0},{3,1},{4,6},{5,7},{6,4},{7,5},{8,10},{9,11},{10,... | collective-permute-start | bytes 3538952 | tf_op jit(solution)/shard_map/ppermute | solution.py:1020
  305.6 28.5 %collective-permute-start.8 = (bf16[384,768]{1,0:T(8,128)(2,1)S(1)}, bf16[384,768]{1,0:T(8,128)(2,1)S(1)}, u32[]{:S(2)}, u32[]{:S(2)}) collective-permute-start(bf16[384,768]{1,0:T(8,128)(2,1)S(1)} %copy-done.12), channel_id=1, source_target_pairs={{0,16},{16,0},{1,17},{17,1},{2,18},{18,2},{3,19},{19,3},{4,20},{20... | collective-permute-start | bytes 1769480 | tf_op jit(solution)/shard_map/ppermute | solution.py:1132
  305.6 28.5 %collective-permute-start.9 = (bf16[384,512]{1,0:T(8,128)(2,1)S(1)}, bf16[384,512]{1,0:T(8,128)(2,1)S(1)}, u32[]{:S(2)}, u32[]{:S(2)}) collective-permute-start(bf16[384,512]{1,0:T(8,128)(2,1)S(1)} %copy-done.24), channel_id=1, source_target_pairs={{0,16},{16,0},{1,17},{17,1},{2,18},{18,2},{3,19},{19,3},{4,20},{20... | collective-permute-start | bytes 1179656 | tf_op jit(solution)/shard_map/ppermute | solution.py:1132
  306.1 28.0 %collective-permute-start.10 = (bf16[1,16,1536]{2,1,0:T(8,128)(2,1)}, bf16[1,16,1536]{2,1,0:T(8,128)(2,1)S(1)}, u32[]{:S(2)}, u32[]{:S(2)}) collective-permute-start(bf16[1,16,1536]{2,1,0:T(8,128)(2,1)} %get-tuple-element.195.refs_7_), channel_id=1, source_target_pairs={{0,8},{1,9},{2,10},{3,11},{4,12},{5,13},{6,14},{7,15},{8,0},{9,1},... | collective-permute-start | bytes 147464 | tf_op jit(solution)/shard_map/ppermute | solution.py:1020
  343.8 29.4 %collective-permute-start.11 = (bf16[8,24,3072]{2,1,0:T(8,128)(2,1)}, bf16[8,24,3072]{2,1,0:T(8,128)(2,1)S(1)}, u32[]{:S(2)}, u32[]{:S(2)}) collective-permute-start(bf16[8,24,3072]{2,1,0:T(8,128)(2,1)} %get-tuple-element.197.refs_6_), channel_id=1, source_target_pairs={{0,1},{1,0},{2,3},{3,2},{4,5},{5,4},{6,7},{7,6},{8,9},{9,8},{10,11... | collective-permute-start | bytes 3538952 | tf_op jit(solution)/shard_map/ppermute | solution.py:1020
  345.2 27.9 %collective-permute-start.14 = (bf16[384,1152]{1,0:T(8,128)(2,1)S(1)}, bf16[384,1152]{1,0:T(8,128)(2,1)S(1)}, u32[]{:S(2)}, u32[]{:S(2)}) collective-permute-start(bf16[384,1152]{1,0:T(8,128)(2,1)S(1)} %copy-done.9), channel_id=1, source_target_pairs={{0,16},{16,0},{1,17},{17,1},{2,18},{18,2},{3,19},{19,3},{4,20},{20... | collective-permute-start | bytes 2654216 | tf_op jit(solution)/shard_map/ppermute | solution.py:1132
  345.2 28.0 %collective-permute-start.12 = (bf16[4,96,768]{2,1,0:T(8,128)(2,1)}, bf16[4,96,768]{2,1,0:T(8,128)(2,1)S(1)}, u32[]{:S(2)}, u32[]{:S(2)}) collective-permute-start(bf16[4,96,768]{2,1,0:T(8,128)(2,1)} %get-tuple-element.198.refs_7_), channel_id=1, source_target_pairs={{0,4},{1,5},{2,6},{3,7},{4,0},{5,1},{6,2},{7,3},{8,12},{9,13},{10,... | collective-permute-start | bytes 1769480 | tf_op jit(solution)/shard_map/ppermute | solution.py:1020
  346.8 26.3 %collective-permute-start.13 = (bf16[8,24,1280]{2,1,0:T(8,128)(2,1)}, bf16[8,24,1280]{2,1,0:T(8,128)(2,1)S(1)}, u32[]{:S(2)}, u32[]{:S(2)}) collective-permute-start(bf16[8,24,1280]{2,1,0:T(8,128)(2,1)} %get-tuple-element.199.refs_8_), channel_id=1, source_target_pairs={{0,4},{1,5},{2,6},{3,7},{4,0},{5,1},{6,2},{7,3},{8,12},{9,13},{10,... | collective-permute-start | bytes 1474568 | tf_op jit(solution)/shard_map/ppermute | solution.py:1020
  373.1 20.7 %collective-permute-start.15 = (bf16[384,1152]{1,0:T(8,128)(2,1)}, bf16[384,1152]{1,0:T(8,128)(2,1)S(1)}, u32[]{:S(2)}, u32[]{:S(2)}) collective-permute-start(bf16[384,1152]{1,0:T(8,128)(2,1)} %get-tuple-element.212.refs_12_), channel_id=1, source_target_pairs={{0,16},{16,0},{1,17},{17,1},{2,18},{18,2},{3,19},{19,3},{4,20},{20... | collective-permute-start | bytes 2654216 | tf_op jit(solution)/shard_map/ppermute | solution.py:1132
  380.4 17.7 %collective-permute-start.16 = (bf16[4,24,3072]{2,1,0:T(8,128)(2,1)}, bf16[4,24,3072]{2,1,0:T(8,128)(2,1)S(1)}, u32[]{:S(2)}, u32[]{:S(2)}) collective-permute-start(bf16[4,24,3072]{2,1,0:T(8,128)(2,1)} %get-tuple-element.208.refs_8_), channel_id=1, source_target_pairs={{0,2},{1,3},{2,0},{3,1},{4,6},{5,7},{6,4},{7,5},{8,10},{9,11},{10,... | collective-permute-start | bytes 1769480 | tf_op jit(solution)/shard_map/ppermute | solution.py:1020
  382.1 16.0 %collective-permute-start.19 = (bf16[8,24,1152]{2,1,0:T(8,128)(2,1)}, bf16[8,24,1152]{2,1,0:T(8,128)(2,1)S(1)}, u32[]{:S(2)}, u32[]{:S(2)}) collective-permute-start(bf16[8,24,1152]{2,1,0:T(8,128)(2,1)} %get-tuple-element.211.refs_11_), channel_id=1, source_target_pairs={{0,4},{1,5},{2,6},{3,7},{4,0},{5,1},{6,2},{7,3},{8,12},{9,13},{10,... | collective-permute-start | bytes 1327112 | tf_op jit(solution)/shard_map/ppermute | solution.py:1020
  383.8 14.3 %collective-permute-start.17 = (bf16[2,96,768]{2,1,0:T(8,128)(2,1)}, bf16[2,96,768]{2,1,0:T(8,128)(2,1)S(1)}, u32[]{:S(2)}, u32[]{:S(2)}) collective-permute-start(bf16[2,96,768]{2,1,0:T(8,128)(2,1)} %get-tuple-element.209.refs_9_), channel_id=1, source_target_pairs={{0,1},{1,0},{2,3},{3,2},{4,5},{5,4},{6,7},{7,6},{8,9},{9,8},{10,11... | collective-permute-start | bytes 884744 | tf_op jit(solution)/shard_map/ppermute | solution.py:1020
  384.3 13.8 %collective-permute-start.18 = (bf16[4,24,1280]{2,1,0:T(8,128)(2,1)}, bf16[4,24,1280]{2,1,0:T(8,128)(2,1)S(1)}, u32[]{:S(2)}, u32[]{:S(2)}) collective-permute-start(bf16[4,24,1280]{2,1,0:T(8,128)(2,1)} %get-tuple-element.210.refs_10_), channel_id=1, source_target_pairs={{0,1},{1,0},{2,3},{3,2},{4,5},{5,4},{6,7},{7,6},{8,9},{9,8},{10,11... | collective-permute-start | bytes 737288 | tf_op jit(solution)/shard_map/ppermute | solution.py:1020
  414.9 7.7 %collective-permute-start.25 = (bf16[2,24,1280]{2,1,0:T(8,128)(2,1)S(1)}, bf16[2,24,1280]{2,1,0:T(8,128)(2,1)S(1)}, u32[]{:S(2)}, u32[]{:S(2)}) collective-permute-start(bf16[2,24,1280]{2,1,0:T(8,128)(2,1)S(1)} %copy-done.37), channel_id=1, source_target_pairs={{0,2},{1,3},{2,0},{3,1},{4,6},{5,7},{6,4},{7,5},{8,10},{9,11},{10,... | collective-permute-start | bytes 368648 | tf_op jit(solution)/shard_map/ppermute | solution.py:1020
  416.8 10.5 %collective-permute-start.24 = (bf16[1,96,768]{2,1,0:T(8,128)(2,1)S(1)}, bf16[1,96,768]{2,1,0:T(8,128)(2,1)S(1)}, u32[]{:S(2)}, u32[]{:S(2)}) collective-permute-start(bf16[1,96,768]{2,1,0:T(8,128)(2,1)S(1)} %copy-done.34), channel_id=1, source_target_pairs={{0,8},{1,9},{2,10},{3,11},{4,12},{5,13},{6,14},{7,15},{8,0},{9,1},... | collective-permute-start | bytes 442376 | tf_op jit(solution)/shard_map/ppermute | solution.py:1020
  417.3 18.7 %collective-permute-start.22 = (bf16[8,24,1152]{2,1,0:T(8,128)(2,1)S(1)}, bf16[8,24,1152]{2,1,0:T(8,128)(2,1)S(1)}, u32[]{:S(2)}, u32[]{:S(2)}) collective-permute-start(bf16[8,24,1152]{2,1,0:T(8,128)(2,1)S(1)} %copy-done.16), channel_id=1, source_target_pairs={{0,2},{1,3},{2,0},{3,1},{4,6},{5,7},{6,4},{7,5},{8,10},{9,11},{10,... | collective-permute-start | bytes 1327112 | tf_op jit(solution)/shard_map/ppermute | solution.py:1020
  421.2 21.6 %collective-permute-start.20 = (bf16[1,529,384]{2,1,0:T(8,128)(2,1)S(1)}, bf16[1,529,384]{2,1,0:T(8,128)(2,1)S(1)}, u32[]{:S(2)}, u32[]{:S(2)}) collective-permute-start(bf16[1,529,384]{2,1,0:T(8,128)(2,1)S(1)} %copy-done.21), channel_id=1, source_target_pairs={{0,16},{16,0},{1,17},{17,1},{2,18},{18,2},{3,19},{19,3},{4,20},{20... | collective-permute-start | bytes 1218824 | tf_op jit(solution)/shard_map/ppermute | solution.py:1132
  421.7 21.1 %collective-permute-start.21 = (bf16[1,529,384]{2,1,0:T(8,128)(2,1)}, bf16[1,529,384]{2,1,0:T(8,128)(2,1)S(1)}, u32[]{:S(2)}, u32[]{:S(2)}) collective-permute-start(bf16[1,529,384]{2,1,0:T(8,128)(2,1)} %get-tuple-element.226.refs_16_), channel_id=1, source_target_pairs={{0,16},{16,0},{1,17},{17,1},{2,18},{18,2},{3,19},{19,3},{4,20},{20... | collective-permute-start | bytes 1218824 | tf_op jit(solution)/shard_map/ppermute | solution.py:1132
  427.3 8.7 %collective-permute-start.23 = (bf16[2,24,3072]{2,1,0:T(8,128)(2,1)S(1)}, bf16[2,24,3072]{2,1,0:T(8,128)(2,1)S(1)}, u32[]{:S(2)}, u32[]{:S(2)}) collective-permute-start(bf16[2,24,3072]{2,1,0:T(8,128)(2,1)S(1)} %copy-done.28), channel_id=1, source_target_pairs={{0,4},{1,5},{2,6},{3,7},{4,0},{5,1},{6,2},{7,3},{8,12},{9,13},{10,... | collective-permute-start | bytes 884744 | tf_op jit(solution)/shard_map/ppermute | solution.py:1020
  430.0 42.4 %collective-permute-start = (bf16[2,529,256]{2,0,1:T(2,128)(2,1)S(1)}, bf16[2,529,256]{2,0,1:T(2,128)(2,1)S(1)}, u32[]{:S(2)}, u32[]{:S(2)}) collective-permute-start(bf16[2,529,256]{2,0,1:T(2,128)(2,1)S(1)} %copy.55), channel_id=1, source_target_pairs={{0,16},{16,0},{1,17},{17,1},{2,18},{18,2},{3,19},{19,3},{4,20},{20... | collective-permute-start | bytes 1625096 | tf_op jit(solution)/shard_map/ppermute | solution.py:1132
  440.4 15.8 %collective-permute-start.30 = (bf16[4,24,1152]{2,1,0:T(8,128)(2,1)}, bf16[4,24,1152]{2,1,0:T(8,128)(2,1)S(1)}, u32[]{:S(2)}, u32[]{:S(2)}) collective-permute-start(bf16[4,24,1152]{2,1,0:T(8,128)(2,1)} %get-tuple-element.239.refs_5_), channel_id=1, source_target_pairs={{0,1},{1,0},{2,3},{3,2},{4,5},{5,4},{6,7},{7,6},{8,9},{9,8},{10,11... | collective-permute-start | bytes 663560 | tf_op jit(solution)/shard_map/ppermute | solution.py:1020
  441.0 7.6 %collective-permute-start.34 = (f32[8,3072]{1,0:T(8,128)}, f32[8,3072]{1,0:T(8,128)S(1)}, u32[]{:S(2)}, u32[]{:S(2)}) collective-permute-start(f32[8,3072]{1,0:T(8,128)} %get-tuple-element.243.refs_9_), channel_id=1, source_target_pairs={{0,2},{1,3},{2,0},{3,1},{4,6},{5,7},{6,4},{7,5},{8,10},{9,11},{10,... | collective-permute-start | bytes 294920 | tf_op jit(solution)/shard_map/ppermute | solution.py:1038
  448.6 7.6 %collective-permute-start.31 = (bf16[1,24,3072]{2,1,0:T(8,128)(2,1)}, bf16[1,24,3072]{2,1,0:T(8,128)(2,1)S(1)}, u32[]{:S(2)}, u32[]{:S(2)}) collective-permute-start(bf16[1,24,3072]{2,1,0:T(8,128)(2,1)} %get-tuple-element.240.refs_6_), channel_id=1, source_target_pairs={{0,8},{1,9},{2,10},{3,11},{4,12},{5,13},{6,14},{7,15},{8,0},{9,1},... | collective-permute-start | bytes 442376 | tf_op jit(solution)/shard_map/ppermute | solution.py:1020
  459.9 8.7 %collective-permute-start.37 = (bf16[2,24,1152]{2,1,0:T(8,128)(2,1)}, bf16[2,24,1152]{2,1,0:T(8,128)(2,1)S(1)}, u32[]{:S(2)}, u32[]{:S(2)}) collective-permute-start(bf16[2,24,1152]{2,1,0:T(8,128)(2,1)} %get-tuple-element.249), channel_id=1, source_target_pairs={{0,4},{1,5},{2,6},{3,7},{4,0},{5,1},{6,2},{7,3},{8,12},{9,13},{10,... | collective-permute-start | bytes 331784 | tf_op jit(solution)/shard_map/ppermute | solution.py:1020
  460.1 8.6 %collective-permute-start.39 = (f32[8,3072]{1,0:T(8,128)}, f32[8,3072]{1,0:T(8,128)S(1)}, u32[]{:S(2)}, u32[]{:S(2)}) collective-permute-start(f32[8,3072]{1,0:T(8,128)} %get-tuple-element.252.refs_5_), channel_id=1, source_target_pairs={{0,8},{1,9},{2,10},{3,11},{4,12},{5,13},{6,14},{7,15},{8,0},{9,1},... | collective-permute-start | bytes 294920 | tf_op jit(solution)/shard_map/ppermute | solution.py:1038
  471.9 11.8 %collective-permute-start.40 = (bf16[1,24,1152]{2,1,0:T(8,128)(2,1)}, bf16[1,24,1152]{2,1,0:T(8,128)(2,1)S(1)}, u32[]{:S(2)}, u32[]{:S(2)}) collective-permute-start(bf16[1,24,1152]{2,1,0:T(8,128)(2,1)} %get-tuple-element.257), channel_id=1, source_target_pairs={{0,8},{1,9},{2,10},{3,11},{4,12},{5,13},{6,14},{7,15},{8,0},{9,1},... | collective-permute-start | bytes 165896 | tf_op jit(solution)/shard_map/ppermute | solution.py:1020
  (66 other events, 425.5 us)
Sparse Core Ops, SparseCore 0:
  204.1 112.0 reduce-scatter.1

commit v3 on v2

v3 whole, which is shorter than its diff:
```python
import functools
import math

import jax
import jax.numpy as jnp
import numpy as np
from jax import lax
from jax.experimental import pallas as pl
from jax.experimental.pallas import tpu as pltpu
from jax.sharding import PartitionSpec as P

HEADS_ENC = 12
HEADS_DEC = 16
ROW_STEP = 32
GROUP = 128
PARTS = 2
VMEM_BYTES = 56 * 1024 * 1024
MASKED = -1e30
LOG2E = math.log2(math.e)

epsilon = 1e-06

NN = (((1,), (0,)), ((), ()))
NT = (((1,), (1,)), ((), ()))
TN = (((0,), (0,)), ((), ()))


def dot(left_side, right_side, dims):
    return lax.dot_general(left_side, right_side, dims, preferred_element_type=jnp.float32)


def low(values):
    return values.astype(jnp.bfloat16)


def call(
    kernel, out_shape, grid, in_specs, out_specs, flops, moved, scalars=1, exps=0, after=(), name=None, scratch=(), through=()
):
    count = scalars + len(in_specs)
    ordered = [pl.BlockSpec(memory_space=pl.ANY)] * (len(after) + len(through))
    aliases = {}
    if through:
        outs = len(out_shape)
        aliases = {count + len(after) + place: outs + place for place in range(len(through))}
        out_shape = tuple(out_shape) + tuple(sds(array.shape, array.dtype) for array in through)
        out_specs = tuple(out_specs) + (pl.BlockSpec(memory_space=pl.ANY),) * len(through)

    def body(*refs):
        ins, rest = refs[:count], refs[count + len(after) + len(through) :]
        if through:
            rest = rest[:outs] + rest[outs + len(through) :]
        kernel(*ins, *rest)

    made = pl.pallas_call(
        body,
        out_shape=out_shape,
        grid_spec=pltpu.PrefetchScalarGridSpec(
            num_scalar_prefetch=scalars,
            grid=grid,
            in_specs=list(in_specs) + ordered,
            out_specs=out_specs,
            scratch_shapes=list(scratch),
        ),
        input_output_aliases=aliases,
        compiler_params=pltpu.CompilerParams(vmem_limit_bytes=VMEM_BYTES),
        cost_estimate=pl.CostEstimate(flops=flops // 256, bytes_accessed=moved // 256, transcendentals=0),
        name=name,
    )
    return lambda *operands: made(*operands, *after, *through)


def whole(array):
    rank = array.ndim
    return pl.BlockSpec(array.shape, lambda *unused: (0,) * rank)


def row_of(ref, place):
    return ref[place : place + 1, :].astype(jnp.float32)


def vector_of(ref):
    return ref[...].astype(jnp.float32).reshape(1, -1)


def live_rows(values, start, count):
    row = lax.broadcasted_iota(jnp.int32, (values.shape[0], 1), 0) + start
    return jnp.where(row < count, values.astype(jnp.float32), 0.0)


def sds(shape, kind=jnp.bfloat16):
    return jax.ShapeDtypeStruct(shape, kind)


def norm(values, gain_row, shift_row):
    center = values - jnp.mean(values, axis=-1, keepdims=True)
    inverse = lax.rsqrt(jnp.mean(center * center, axis=-1, keepdims=True) + epsilon)
    unit = center * inverse
    return unit * gain_row + shift_row, unit, inverse


def norm_back(grad_out, unit, inverse, gain_row):
    scaled = grad_out * gain_row
    return inverse * (
        scaled
        - jnp.mean(scaled, axis=-1, keepdims=True)
        - unit * jnp.mean(scaled * unit, axis=-1, keepdims=True)
    )


def col_sum(values):
    return jnp.sum(values, axis=0, keepdims=True)


def gelu_parts(values):
    share = 0.5 + 0.5 * lax.erf(values * math.sqrt(0.5))
    bell = jnp.exp2(values * values * (-0.5 * LOG2E)) * (1.0 / math.sqrt(2.0 * math.pi))
    return values * share, share + values * bell


def add_rows(ref, rows):
    @pl.when((pl.program_id(0) == 0) & (pl.program_id(1) == 0))
    def start():
        ref[...] = jnp.zeros_like(ref)

    for place, row in enumerate(rows):
        ref[place : place + 1, :] += row


BLOCK = 1
STRIP = 2


def place_info(visible, strips):
    section_index = lax.axis_index("section")
    block = section_index * lax.axis_size("dp") + lax.axis_index("dp")
    mine = section_index * strips + jnp.arange(strips, dtype=jnp.int32)
    every = jnp.arange(2 * strips, dtype=jnp.int32)
    return jnp.concatenate(
        [
            jnp.stack([section_index, block]),
            mine,
            lax.dynamic_slice_in_dim(visible, section_index * strips, strips, 0),
            every // strips,
            every % strips,
        ]
    ).astype(jnp.int32)


class Sizes:
    def __init__(self, strips, length, padded):
        self.strips, self.length, self.padded = strips, length, padded
        self.rows = strips * padded

    def place(self, strip):
        return slice(strip * self.padded, (strip + 1) * self.padded)

    def raw(self, width):
        return [
            pl.BlockSpec(
                (None, self.padded, width), lambda *step, s=s: (step[-1][STRIP + s], 0, 0)
            )
            for s in range(self.strips)
        ]

    def all(self, width):
        return pl.BlockSpec((self.rows, width), lambda *step: (0, 0))

    def cols(self, width):
        return pl.BlockSpec((self.rows, width), lambda i, info: (0, i))

    def half(self, width):
        return pl.BlockSpec((self.strips, self.padded, width), lambda *step: (0, 0, 0))

    def sums(self, width):
        return pl.BlockSpec((8, width), lambda *step: (0, 0))

    def strip(self, width):
        return pl.BlockSpec((None, self.padded, width), lambda s, i, info: (s, 0, 0))


def first_step(run):
    pl.when(pl.program_id(0) == 0)(run)


def last_step(run):
    pl.when(pl.program_id(0) == pl.num_programs(0) - 1)(run)


def store_halves(info_ref, kept_ref, sent_ref, values):
    half = kept_ref.shape[-1]
    first = info_ref[0] == 0
    kept_ref[...] = low(jnp.where(first, values[:, :half], values[:, half:]))
    sent_ref[...] = low(jnp.where(first, values[:, half:], values[:, :half]))


def set_rows(ref, rows):
    for place, row in enumerate(rows):
        ref[place : place + 1, :] = row


def packed_kernel(info_ref, *refs, sizes):
    x_refs = refs[: sizes.strips]
    gain_ref, shift_ref, w_ref, n_ref, packed_ref = refs[sizes.strips :]

    @first_step
    def normalize():
        for strip, x_ref in enumerate(x_refs):
            x = live_rows(x_ref[...], 0, sizes.length)
            normed, _, _ = norm(x, row_of(gain_ref, 0), row_of(shift_ref, 0))
            n_ref[sizes.place(strip), :] = low(normed)

    packed_ref[...] = low(dot(n_ref[...], w_ref[...], NN))


def packed_call(sizes, info, x, gains, shifts, w_qkv):
    rows, width = sizes.rows, x.shape[2]
    return call(
        functools.partial(packed_kernel, sizes=sizes),
        (sds((rows, width)), sds((rows, 3 * width))),
        (3,),
        sizes.raw(width)
        + [whole(gains), whole(shifts), pl.BlockSpec((width, width), lambda i, info: (0, i))],
        (sizes.all(width), sizes.cols(width)),
        6 * rows * width * width,
        rows * width * 10 + 6 * width * width,
        name="encoder_packed",
    )(info, *[x] * sizes.strips, gains, shifts, w_qkv)


def picker_of(source_ref, strip):
    taken = source_ref[pl.ds(strip, 1), :]
    length = taken.shape[1]
    return low(jnp.where(taken == lax.broadcasted_iota(jnp.int32, (length, length), 0), 1.0, 0.0))


def last_row(length):
    return lax.broadcasted_iota(jnp.int32, (length, 1), 0) == length - 1


def decoder_in_kernel(
    info_ref,
    rows_ref,
    source_ref,
    mask_ref,
    places_ref,
    gain_ref,
    shift_ref,
    w_ref,
    x_ref,
    n_ref,
    packed_ref,
    *,
    sizes
):
    @first_step
    def gather():
        for strip in range(sizes.strips):
            place = sizes.place(strip)
            picker = picker_of(source_ref, info_ref[STRIP + strip])
            rows = jnp.where(
                last_row(sizes.padded), vector_of(mask_ref), rows_ref[place, :].astype(jnp.float32)
            )
            x = dot(picker, low(rows), TN) + places_ref[...]
            x_ref[place, :] = x
            normed, _, _ = norm(x, row_of(gain_ref, 0), row_of(shift_ref, 0))
            n_ref[place, :] = low(normed)

    packed_ref[...] = low(dot(n_ref[...], w_ref[...], NN))


def decoder_in_call(sizes, info, projected, source, mask_row, places, gains, shifts, w_qkv):
    width = projected.shape[1]
    rows = sizes.rows
    return call(
        functools.partial(decoder_in_kernel, sizes=sizes),
        (sds((rows, width), jnp.float32), sds((rows, width)), sds((rows, 3 * width))),
        (3,),
        [sizes.all(width), whole(source), whole(mask_row), whole(places), whole(gains), whole(shifts)]
        + [pl.BlockSpec((width, width), lambda i, info: (0, i))],
        (sizes.all(width), sizes.all(width), sizes.cols(width)),
        6 * rows * width * width + 2 * rows * sizes.padded * width,
        rows * width * 18 + 6 * width * width,
        name="decoder_packed",
    )(info, projected, source, mask_row, places, gains, shifts, w_qkv)


def head_parts(head, heads_here):
    lane = lax.broadcasted_iota(jnp.int32, (1, GROUP), 1)
    size = GROUP // heads_here
    mine = (lane >= head * size) & (lane < (head + 1) * size)
    spare = ((head + 1) % heads_here) * size
    return mine, lane == spare, spare


def key_bias(live, length):
    row = lax.broadcasted_iota(jnp.int32, (length, 1), 0)
    return low(jnp.where(row < live, 0.0, MASKED))


def attend_kernel(info_ref, q_ref, k_ref, v_ref, out_ref, *, heads_here, live):
    length = q_ref.shape[1]
    rate = (GROUP // heads_here) ** -0.5 * LOG2E
    bias = key_bias(live(info_ref, pl.program_id(0)), length)
    one = jnp.bfloat16(1.0)
    half = length // 2
    for start in range(0, q_ref.shape[2], GROUP):
        group = slice(start, start + GROUP)
        k, v = k_ref[0, :, group], v_ref[0, :, group]
        for begin in range(0, length, half):
            q = q_ref[0, begin : begin + half, group]
            mixed = jnp.zeros((half, GROUP), jnp.float32)
            for head in range(heads_here):
                mine, at_spare, spare = head_parts(head, heads_here)
                head_q = jnp.where(mine, q, low(jnp.where(at_spare, 1.0, 0.0)))
                scores = dot(head_q, jnp.where(at_spare, bias, k), NT)
                highest = jnp.max(scores, axis=1, keepdims=True)
                terms = low(jnp.exp2((scores - highest) * rate))
                product = dot(terms, jnp.where(at_spare, one, v), NN)
                total = product[:, spare : spare + 1]
                mixed = jnp.where(mine, product * (1.0 / total), mixed)
            out_ref[0, begin : begin + half, group] = low(mixed)


def all_live(length):
    return lambda info_ref, strip: length


def visible_live(strips):
    return lambda info_ref, strip: info_ref[STRIP + strips + strip]


def attend_call(packed, info, heads, live, name):
    strips, length, triple = packed.shape
    width = triple // 3
    heads_here = GROUP // (width // heads)
    groups = 2
    part = width // groups
    third = lambda j: pl.BlockSpec((1, length, part), lambda s, g, _: (s, 0, g + j * groups))
    return call(
        functools.partial(attend_kernel, heads_here=heads_here, live=live),
        sds((strips, length, width)),
        (strips, groups),
        [third(0), third(1), third(2)],
        third(0),
        strips * heads * length * length * GROUP * 6,
        strips * length * width * 8,
        exps=strips * heads * length * length,
        name=name,
    )(info, packed, packed, packed)


def attend_back_kernel(
    info_ref,
    q_ref,
    k_ref,
    v_ref,
    dout_ref,
    n_ref,
    grad_ref,
    kept_ref,
    sent_ref,
    total_ref,
    *,
    heads_here,
    live
):
    length = q_ref.shape[1]
    factor = (GROUP // heads_here) ** -0.5
    rate = factor * LOG2E
    strip = pl.program_id(1)
    q, k, v, dout = q_ref[0], k_ref[0], v_ref[0], dout_ref[0]
    bias = key_bias(live(info_ref, strip), length)
    k_turned = k.T
    dq_turned = []
    dk = jnp.zeros((length, GROUP), jnp.float32)
    dv = jnp.zeros((length, GROUP), jnp.float32)
    size = GROUP // heads_here
    for head in range(heads_here):
        mine, at_spare, _ = head_parts(head, heads_here)
        head_q = jnp.where(mine, q, low(jnp.where(at_spare, 1.0, 0.0)))
        head_dout = jnp.where(mine, dout, jnp.bfloat16(0.0))
        scores = dot(jnp.where(at_spare, bias, k), head_q, NT)
        highest = jnp.max(scores, axis=0, keepdims=True)
        terms = jnp.exp2((scores - highest) * rate)
        probs = terms * (1.0 / jnp.sum(terms, axis=0, keepdims=True))
        weighted = probs * dot(v, head_dout, NT)
        dscores = low(weighted - probs * jnp.sum(weighted, axis=0, keepdims=True))
        dk = jnp.where(mine, dot(dscores, q, NN), dk)
        dv = jnp.where(mine, dot(low(probs), dout, NN), dv)
        dq_turned.append(dot(k_turned[head * size : (head + 1) * size], dscores, NN))
    dq = low(jnp.concatenate(dq_turned, axis=0).T * factor)
    dk, dv = low(dk * factor), low(dv)
    grad_ref[0, 0] = dq
    grad_ref[1, 0] = dk
    grad_ref[2, 0] = dv
    term = dot(n_ref[0], jnp.concatenate([dq, dk, dv], axis=1), TN)
    half = kept_ref.shape[0]
    last = pl.num_programs(1) - 1

    @pl.when(strip == 0)
    def begin():
        total_ref[...] = term

    @pl.when(strip > 0)
    def more():
        total_ref[...] += term

    @pl.when(strip == last)
    def finish():
        kept_ref[...] = low(total_ref[pl.ds(pl.multiple_of(info_ref[0] * half, 8), half), :])
        sent_ref[...] = low(total_ref[pl.ds(pl.multiple_of((1 - info_ref[0]) * half, 8), half), :])


def attend_back_call(packed, dmixed, normed, info, heads, live, part, parts, after, name):
    strips, length, triple = packed.shape
    width = triple // 3
    heads_here = GROUP // (width // heads)
    groups = width // GROUP
    here = groups // parts
    third = lambda j: pl.BlockSpec(
        (1, length, GROUP), lambda g, s, _: (s, 0, g + part * here + j * groups)
    )
    product = pl.BlockSpec((width // 2, 3 * GROUP), lambda g, s, _: (0, g))
    return call(
        functools.partial(attend_back_kernel, heads_here=heads_here, live=live),
        (
            sds((3, strips, length, here * GROUP)),
            sds((width // 2, here * 3 * GROUP)),
            sds((width // 2, here * 3 * GROUP)),
        ),
        (here, strips),
        [
            third(0),
            third(1),
            third(2),
            third(0),
            pl.BlockSpec((1, length, width), lambda g, s, _: (s, 0, 0)),
        ],
        (pl.BlockSpec((3, 1, length, GROUP), lambda g, s, _: (0, s, 0, g)), product, product),
        (strips * heads * length * length * GROUP * 12 + 6 * strips * length * width * width) // parts,
        strips * length * width * 14 // parts,
        exps=strips * heads * length * length // parts,
        after=after,
        name=name,
        scratch=[pltpu.VMEM((width, 3 * GROUP), jnp.float32)],
    )(info, packed, packed, packed, dmixed, normed)


def encoder_ff_kernel(info_ref, *refs, sizes):
    x_refs = refs[: sizes.strips]
    (
        mixed_ref,
        gain_ref,
        shift_ref,
        w_out_ref,
        bias_out_ref,
        w_up_ref,
        bias_up_ref,
        w_down_ref,
        w_proj_ref,
        bias_proj_ref,
        mid_ref,
        n_ref,
        act_ref,
        slope_ref,
        y_low_ref,
        encoded_ref,
        projected_ref,
        y_ref,
        bias_ref,
    ) = refs[sizes.strips :]
    places = [sizes.place(strip) for strip in range(sizes.strips)]

    @first_step
    def middle():
        bias_ref[...] = vector_of(bias_up_ref)
        for place, x_ref in zip(places, x_refs):
            x = live_rows(x_ref[...], 0, sizes.length)
            mid = x + dot(mixed_ref[place, :], w_out_ref[...], NN) + row_of(bias_out_ref, 0)
            mid_ref[place, :] = low(mid)
            normed, _, _ = norm(mid, row_of(gain_ref, 1), row_of(shift_ref, 1))
            n_ref[place, :] = low(normed)
            y_ref[place, :] = mid + row_of(bias_out_ref, 1)

    chunk = w_up_ref.shape[1]
    bias = bias_ref[:, pl.ds(pl.multiple_of(pl.program_id(0) * chunk, GROUP), chunk)]
    hidden = [dot(n_ref[place, :], w_up_ref[...], NN) + bias for place in places]
    for place, values in zip(places, hidden):
        act, slope = gelu_parts(values)
        act = low(act)
        act_ref[place, :] = act
        slope_ref[place, :] = low(slope)
        y_ref[place, :] += dot(act, w_down_ref[...], NN)

    @last_step
    def finish():
        for place in places:
            y = y_ref[place, :]
            y_low_ref[place, :] = low(y)
            encoded, _, _ = norm(y, row_of(gain_ref, 2), row_of(shift_ref, 2))
            encoded = low(encoded)
            encoded_ref[place, :] = encoded
            projected_ref[place, :] = low(
                dot(encoded, w_proj_ref[...], NN) + vector_of(bias_proj_ref)
            )


def encoder_ff_call(
    sizes, info, x, mixed, gains, shifts, w_out, bias_out, w_up, bias_up, w_down, w_proj, bias_proj
):
    rows, width = sizes.rows, x.shape[2]
    units = w_up.shape[1]
    narrow = w_proj.shape[1]
    chunk = units // 4
    return call(
        functools.partial(encoder_ff_kernel, sizes=sizes),
        (
            sds((rows, width)),
            sds((rows, width)),
            sds((rows, units)),
            sds((rows, units)),
            sds((rows, width)),
            sds((rows, width)),
            sds((rows, narrow)),
        ),
        (4,),
        sizes.raw(width)
        + [sizes.all(width)]
        + [whole(w) for w in (gains, shifts, w_out, bias_out)]
        + [
            pl.BlockSpec((width, chunk), lambda i, info: (0, i)),
            whole(bias_up),
            pl.BlockSpec((chunk, width), lambda i, info: (i, 0)),
            whole(w_proj),
            whole(bias_proj),
        ],
        (
            sizes.all(width),
            sizes.all(width),
            sizes.cols(chunk),
            sizes.cols(chunk),
            sizes.all(width),
            sizes.all(width),
            sizes.all(narrow),
        ),
        2 * rows * width * (width + 2 * units + narrow),
        rows * (width * 16 + units * 4) + 2 * width * (width + 2 * units + narrow),
        exps=rows * units,
        name="encoder_feed_forward",
        scratch=[pltpu.VMEM((rows, width), jnp.float32), pltpu.VMEM((1, units), jnp.float32)],
    )(
        info,
        *[x] * sizes.strips,
        mixed,
        gains,
        shifts,
        w_out,
        bias_out,
        w_up,
        bias_up,
        w_down,
        w_proj,
        bias_proj,
    )


def decoder_ff_kernel(info_ref, *refs, sizes, folds, share, units):
    cot_refs = refs[: sizes.strips]
    (
        x_ref,
        mixed_ref,
        gain_ref,
        shift_ref,
        w_out_ref,
        bias_out_ref,
        w_up_ref,
        bias_up_ref,
        w_down_ref,
        kept_ref,
        sent_ref,
        gb_ref,
        dmixed_ref,
        sums_ref,
        up_sums_ref,
        kept_up_ref,
        sent_up_ref,
        *down_refs,
        cot_ref,
        n_ref,
        act_ref,
        dhidden_ref,
        mid_ref,
        y_ref,
        dnormed_ref,
        bias_ref,
        beside_ref,
        down_ref,
    ) = refs[sizes.strips :]
    places = [sizes.place(strip) for strip in range(sizes.strips)]
    gain, shift = row_of(gain_ref, 1), row_of(shift_ref, 1)

    @first_step
    def middle():
        bias_ref[...] = vector_of(bias_up_ref)
        dnormed_ref[...] = jnp.zeros_like(dnormed_ref)
        for place, cot_here in zip(places, cot_refs):
            mid = x_ref[place, :] + dot(mixed_ref[place, :], w_out_ref[...], NN) + row_of(bias_out_ref, 0)
            mid_ref[place, :] = mid
            normed, _, _ = norm(mid, gain, shift)
            n_ref[place, :] = low(normed)
            y_ref[place, :] = mid + row_of(bias_out_ref, 1)
            cot_ref[place, :] = low(live_rows(cot_here[...], 0, sizes.length))

    chunk = w_up_ref.shape[1]
    bias = bias_ref[:, pl.ds(pl.multiple_of(pl.program_id(0) * chunk, GROUP), chunk)]
    hidden = [dot(n_ref[place, :], w_up_ref[...], NN) + bias for place in places]
    dact = [dot(cot_ref[place, :], w_down_ref[...], NT) for place in places]
    up_sums = jnp.zeros((1, chunk), jnp.float32)
    for place, values, grads in zip(places, hidden, dact):
        act, slope = gelu_parts(values)
        act = low(act)
        act_ref[place, :] = act
        y_ref[place, :] += dot(act, w_down_ref[...], NN)
        dhidden = low(grads * slope)
        dhidden_ref[place, :] = dhidden
        up_sums = up_sums + col_sum(dhidden.astype(jnp.float32))
        dnormed_ref[place, :] += dot(dhidden, w_up_ref[...], NT)
    up_sums_ref[0:1, :] = up_sums
    step, width = pl.program_id(0), n_ref.shape[1]
    beside_ref[:, pl.ds(pl.multiple_of(step * chunk, GROUP), chunk)] = low(
        dot(n_ref[...], dhidden_ref[...], TN)
    )
    down = dot(act_ref[...], cot_ref[...], TN)
    if folds:
        down = down.reshape(-1, folds, share, width)
        here = chunk // folds
        rows = pl.ds(pl.multiple_of(step * here, share), here)
        for fold in range(folds):
            start = (folds + 1 + fold) * width
            beside_ref[rows, start : start + width] = low(down[:, fold].reshape(here, width))
    else:
        down_ref[pl.ds(pl.multiple_of(step * chunk, GROUP), chunk), :] = low(down)

    @last_step
    def finish():
        totals = []
        for strip, place in enumerate(places):
            store_halves(info_ref, kept_ref.at[strip], sent_ref.at[strip], y_ref[place, :])
            _, unit, inverse = norm(mid_ref[place, :], gain, shift)
            grad = cot_ref[place, :].astype(jnp.float32)
            dnormed = dnormed_ref[place, :]
            gb = low(grad + norm_back(dnormed, unit, inverse, gain))
            gb_ref[place, :] = gb
            dmixed_ref[place, :] = low(dot(gb, w_out_ref[...], NT))
            totals.append(
                (
                    col_sum(dnormed * unit),
                    col_sum(dnormed),
                    col_sum(gb.astype(jnp.float32)),
                    col_sum(grad),
                )
            )
        set_rows(sums_ref, [sum(rows) for rows in zip(*totals)])
        beside_ref[:, units : units + width] = low(dot(mixed_ref[...], gb_ref[...], TN))
        for kept, sent, whole_ref in zip(
            (kept_up_ref, *down_refs[:1]), (sent_up_ref, *down_refs[1:]), (beside_ref, down_ref)
        ):
            half = kept.shape[0]
            kept[...] = whole_ref[pl.ds(pl.multiple_of(info_ref[0] * half, 16), half), :]
            sent[...] = whole_ref[pl.ds(pl.multiple_of((1 - info_ref[0]) * half, 16), half), :]


def decoder_ff_call(
    sizes, info, x, mixed, cot, gains, shifts, w_out, bias_out, w_up, bias_up, w_down, share
):
    rows, width = x.shape
    units = w_up.shape[1]
    chunk = units // 4
    all_rows = sizes.all(width)
    half = sds((sizes.strips, sizes.length, width // 2))
    up_sums = pl.BlockSpec((8, chunk), lambda i, info: (0, i))
    folds = units // width if share % 8 == 0 else 0
    beside = units + width + (units if folds else 0)
    halves = [(width // 2, beside)] * 2 + ([] if folds else [(units // 2, width)] * 2)
    return call(
        functools.partial(decoder_ff_kernel, sizes=sizes, folds=folds, share=share, units=units),
        (
            half,
            half,
            sds((rows, width)),
            sds((rows, width)),
            sds((8, width), jnp.float32),
            sds((8, units), jnp.float32),
            *[sds(shape) for shape in halves],
        ),
        (4,),
        sizes.raw(width)
        + [all_rows, all_rows]
        + [whole(w) for w in (gains, shifts, w_out, bias_out)]
        + [
            pl.BlockSpec((width, chunk), lambda i, info: (0, i)),
            whole(bias_up),
            pl.BlockSpec((chunk, width), lambda i, info: (i, 0)),
        ],
        (
            sizes.half(width // 2),
            sizes.half(width // 2),
            all_rows,
            all_rows,
            sizes.sums(width),
            up_sums,
            *[pl.BlockSpec(shape, lambda i, info: (0, 0)) for shape in halves],
        ),
        2 * rows * width * (3 * width + 6 * units),
        rows * width * 16 + 4 * width * (width + 2 * units),
        exps=rows * units,
        name="decoder_feed_forward",
        scratch=[
            pltpu.VMEM((rows, width), jnp.bfloat16),
            pltpu.VMEM((rows, width), jnp.bfloat16),
            pltpu.VMEM((rows, chunk), jnp.bfloat16),
            pltpu.VMEM((rows, chunk), jnp.bfloat16),
            pltpu.VMEM((rows, width), jnp.float32),
            pltpu.VMEM((rows, width), jnp.float32),
            pltpu.VMEM((rows, width), jnp.float32),
            pltpu.VMEM((1, units), jnp.float32),
            pltpu.VMEM((width, beside), jnp.bfloat16),
            pltpu.VMEM((16 if folds else units, width), jnp.bfloat16),
        ],
    )(info, *[cot] * sizes.strips, x, mixed, gains, shifts, w_out, bias_out, w_up, bias_up, w_down)


def encoder_ff_back_kernel(
    info_ref,
    grad_ref,
    mid_ref,
    slope_ref,
    gain_ref,
    shift_ref,
    w_out_ref,
    w_up_ref,
    w_down_ref,
    dhidden_ref,
    gb_ref,
    dmixed_ref,
    sums_ref,
    up_sums_ref,
    dnormed_ref,
    *,
    sizes
):
    places = [sizes.place(strip) for strip in range(sizes.strips)]

    @first_step
    def begin():
        dnormed_ref[...] = jnp.zeros_like(dnormed_ref)

    dact = [dot(grad_ref[place, :], w_down_ref[...], NT) for place in places]
    up_sums = jnp.zeros((1, w_up_ref.shape[1]), jnp.float32)
    for place, values in zip(places, dact):
        dhidden = low(values * slope_ref[place, :].astype(jnp.float32))
        dhidden_ref[place, :] = dhidden
        up_sums = up_sums + col_sum(dhidden.astype(jnp.float32))
        dnormed_ref[place, :] += dot(dhidden, w_up_ref[...], NT)
    up_sums_ref[0:1, :] = up_sums

    @last_step
    def finish():
        gain, shift = row_of(gain_ref, 1), row_of(shift_ref, 1)
        totals = []
        for place in places:
            _, unit, inverse = norm(mid_ref[place, :].astype(jnp.float32), gain, shift)
            grad = grad_ref[place, :].astype(jnp.float32)
            dnormed = dnormed_ref[place, :]
            gb = low(grad + norm_back(dnormed, unit, inverse, gain))
            gb_ref[place, :] = gb
            dmixed_ref[place, :] = low(dot(gb, w_out_ref[...], NT))
            totals.append(
                (
                    col_sum(dnormed * unit),
                    col_sum(dnormed),
                    col_sum(gb.astype(jnp.float32)),
                    col_sum(grad),
                )
            )
        set_rows(sums_ref, [sum(rows) for rows in zip(*totals)])


def encoder_ff_back_call(sizes, info, grad, mid, slope, gains, shifts, w_out, w_up, w_down, after):
    rows, width = grad.shape
    units = w_up.shape[1]
    chunk = units // 4
    all_rows, cols = sizes.all(width), sizes.cols(chunk)
    return call(
        functools.partial(encoder_ff_back_kernel, sizes=sizes),
        (
            sds((rows, units)),
            sds((rows, width)),
            sds((rows, width)),
            sds((8, width), jnp.float32),
            sds((8, units), jnp.float32),
        ),
        (4,),
        [all_rows, all_rows, cols, whole(gains), whole(shifts), whole(w_out)]
        + [
            pl.BlockSpec((width, chunk), lambda i, info: (0, i)),
            pl.BlockSpec((chunk, width), lambda i, info: (i, 0)),
        ],
        (
            cols,
            all_rows,
            all_rows,
            sizes.sums(width),
            pl.BlockSpec((8, chunk), lambda i, info: (0, i)),
        ),
        2 * rows * width * (width + 2 * units),
        rows * (width * 16 + units * 4) + 2 * width * (width + 2 * units),
        after=after,
        name="encoder_feed_forward_back",
        scratch=[pltpu.VMEM((rows, width), jnp.float32)],
    )(info, grad, mid, slope, gains, shifts, w_out, w_up, w_down)


def packed_back(grad_ref, w_ref):
    width = w_ref.shape[0]
    return sum(dot(grad_ref[j], w_ref[:, j * width : (j + 1) * width], NT) for j in range(3))


def decoder_back_kernel(
    info_ref,
    dpacked_ref,
    gm_ref,
    x_ref,
    source_ref,
    y_ref,
    encoded_ref,
    gain_ref,
    shift_ref,
    w_ref,
    w_proj_ref,
    enc_gain_ref,
    enc_shift_ref,
    grad_ref,
    sums_ref,
    enc_sums_ref,
    kept_ref,
    sent_ref,
    total_ref,
):
    dnormed = packed_back(dpacked_ref, w_ref)
    gain = row_of(gain_ref, 0)
    _, unit, inverse = norm(x_ref[...], gain, row_of(shift_ref, 0))
    dx = gm_ref[...].astype(jnp.float32) + norm_back(dnormed, unit, inverse, gain)
    picker = picker_of(source_ref, info_ref[STRIP + pl.program_id(0)])
    taken = dot(picker, low(dx), NN)
    last = taken.shape[0] - 1
    dproj = low(jnp.where(last_row(taken.shape[0]), 0.0, taken))
    term = dot(encoded_ref[...], dproj, TN)
    half = kept_ref.shape[0]

    @pl.when(pl.program_id(0) == 0)
    def begin():
        total_ref[...] = term

    @pl.when(pl.program_id(0) > 0)
    def more():
        total_ref[...] += term

    @pl.when(pl.program_id(0) == pl.num_programs(0) - 1)
    def finish():
        kept_ref[...] = low(total_ref[pl.ds(pl.multiple_of(info_ref[0] * half, 8), half), :])
        sent_ref[...] = low(total_ref[pl.ds(pl.multiple_of((1 - info_ref[0]) * half, 8), half), :])

    dencoded = low(dot(dproj, w_proj_ref[...], NT)).astype(jnp.float32)
    enc_gain = row_of(enc_gain_ref, 2)
    _, unit_final, inverse_final = norm(
        y_ref[...].astype(jnp.float32), enc_gain, row_of(enc_shift_ref, 2)
    )
    grad_ref[...] = low(norm_back(dencoded, unit_final, inverse_final, enc_gain))
    add_rows(
        sums_ref,
        (
            col_sum(dnormed * unit),
            col_sum(dnormed),
            taken[last : last + 1],
            col_sum(dproj.astype(jnp.float32)),
        ),
    )
    add_rows(enc_sums_ref, (col_sum(dencoded * unit_final), col_sum(dencoded)))


def decoder_back_call(
    sizes,
    info,
    dpacked,
    gm,
    x,
    source,
    y,
    encoded,
    gains,
    shifts,
    w_qkv,
    w_proj,
    enc_gains,
    enc_shifts,
    after,
):
    strips, padded, rows = sizes.strips, sizes.padded, sizes.rows
    width = x.shape[2]
    wide = y.shape[2]
    weights = (gains, shifts, w_qkv, w_proj, enc_gains, enc_shifts)
    strip = sizes.strip
    return call(
        decoder_back_kernel,
        (
            sds((strips, padded, wide)),
            sds((8, width), jnp.float32),
            sds((8, wide), jnp.float32),
            sds((wide // 2, width)),
            sds((wide // 2, width)),
        ),
        (strips, 1),
        [
            pl.BlockSpec((3, None, padded, width), lambda s, i, info: (0, s, 0, 0)),
            strip(width),
            strip(width),
            whole(source),
            strip(wide),
            strip(wide),
        ]
        + [whole(w) for w in weights],
        (
            strip(wide),
            sizes.sums(width),
            sizes.sums(wide),
            pl.BlockSpec((wide // 2, width), lambda s, i, info: (0, 0)),
            pl.BlockSpec((wide // 2, width), lambda s, i, info: (0, 0)),
        ),
        2 * rows * width * (3 * width + padded + 2 * wide),
        rows * (width * 16 + wide * 8) + 2 * width * (3 * width + wide),
        after=after,
        name="decoder_packed_back",
        scratch=[pltpu.VMEM((wide, width), jnp.float32)],
    )(info, dpacked, gm, x, source, y, encoded, *weights)


def encoder_back_kernel(info_ref, *refs, parts, length):
    grad_refs, w_refs = refs[:parts], refs[parts : 2 * parts]
    gb_ref, x_ref, gain_ref, shift_ref, kept_ref, sent_ref, sums_ref, dnormed_ref = refs[2 * parts :]
    term = sum(dot(grad_ref[...], w_ref[...], NT) for grad_ref, w_ref in zip(grad_refs, w_refs))

    @first_step
    def begin():
        dnormed_ref[...] = term

    @pl.when(pl.program_id(0) > 0)
    def more():
        dnormed_ref[...] += term

    @last_step
    def finish():
        dnormed = dnormed_ref[...]
        gain = row_of(gain_ref, 0)
        x = live_rows(x_ref[...], 0, length)
        _, unit, inverse = norm(x, gain, row_of(shift_ref, 0))
        dx = gb_ref[...].astype(jnp.float32) + norm_back(dnormed, unit, inverse, gain)
        store_halves(info_ref, kept_ref, sent_ref, dx)
        set_rows(sums_ref, (col_sum(dnormed * unit), col_sum(dnormed)))


def encoder_back_call(sizes, info, dpacked, gb, x, gains, shifts, w_qkv, strip, after):
    rows, width = gb.shape
    padded = sizes.padded
    half = sds((1, sizes.length, width // 2))
    parts = len(dpacked)
    here = width // parts
    half_spec = pl.BlockSpec((None, padded, width // 2), lambda j, info: (0, 0, 0))
    return call(
        functools.partial(encoder_back_kernel, parts=parts, length=sizes.length),
        (half, half, sds((8, width), jnp.float32)),
        (3,),
        [pl.BlockSpec((None, None, padded, here), lambda j, info: (j, strip, 0, 0))] * parts
        + [
            pl.BlockSpec((width, here), lambda j, info, part=part: (0, j * parts + part))
            for part in range(parts)
        ]
        + [
            pl.BlockSpec((padded, width), lambda j, info: (strip, 0)),
            sizes.raw(width)[strip],
            whole(gains),
            whole(shifts),
        ],
        (half_spec, half_spec, sizes.sums(width)),
        6 * rows * width * width // sizes.strips,
        rows * width * 12 // sizes.strips + 6 * width * width,
        after=after,
        name=f"encoder_packed_back_{strip}",
        scratch=[pltpu.VMEM((padded, width), jnp.float32)],
    )(info, *dpacked, *[w_qkv] * parts, gb, x, gains, shifts)


class Job:
    def __init__(self, left, right, row_step, col_step, offset):
        self.half = left.shape[1] // 2
        self.width = right.shape[1]
        self.rows = left.shape[0]
        self.row_step, self.col_step, self.offset = row_step, col_step, offset
        self.down = self.half // row_step
        self.across = self.width // col_step
        self.count = self.down * self.across

    def at(self, step):
        here = jnp.clip(step - self.offset, 0, self.count - 1)
        if self.across == 1:
            return here, 0
        if self.down == 1:
            return 0, here
        return here // self.across, here % self.across

    def left(self, pick):
        return pl.BlockSpec(
            (self.rows, self.row_step),
            lambda step, info: (0, pick(info[0]) * self.down + self.at(step)[0]),
        )

    def right(self):
        return pl.BlockSpec((self.rows, self.col_step), lambda step, info: (0, self.at(step)[1]))

    def out(self):
        return pl.BlockSpec((self.row_step, self.col_step), lambda step, info: self.at(step))


def product_kernel(info_ref, *refs, jobs):
    step = pl.program_id(0)
    out = 3 * len(jobs)
    for place, (offset, count) in enumerate(jobs):
        mine_ref, other_ref, right_ref = refs[3 * place : 3 * place + 3]
        kept_ref, sent_ref = refs[out + 2 * place : out + 2 * place + 2]

        @pl.when((step >= offset) & (step < offset + count))
        def product():
            right = right_ref[...]
            sent_ref[...] = low(dot(other_ref[...], right, TN))
            kept_ref[...] = low(dot(mine_ref[...], right, TN))


def product_call(info, products, name, after=()):
    jobs, operands, in_specs, out_specs, out_shape = [], [], [], [], []
    offset = flops = moved = 0
    for left, right, row_step, col_step in products:
        job = Job(left, right, row_step, col_step, offset)
        offset += job.count
        jobs.append(job)
        operands += [left, left, right]
        in_specs += [job.left(lambda own: own), job.left(lambda own: 1 - own), job.right()]
        out_specs += [job.out(), job.out()]
        out_shape += [sds((job.half, job.width))] * 2
        flops += 4 * job.rows * job.half * job.width
        moved += 2 * job.rows * (2 * job.half + job.width) + 4 * job.half * job.width
    outs = call(
        functools.partial(product_kernel, jobs=[(job.offset, job.count) for job in jobs]),
        tuple(out_shape),
        (offset,),
        in_specs,
        tuple(out_specs),
        flops,
        moved,
        after=after,
        name=name,
    )(info, *operands)
    return [outs[2 * place : 2 * place + 2] for place in range(len(jobs))]


class Chain:
    def __init__(self, pairs, order, parts):
        self.pairs = pairs
        self.bits = list(range(pairs.bit_length() - 1))
        self.order = [bit for bit in order if bit < len(self.bits)]
        self.order += [bit for bit in self.bits if bit not in self.order]
        self.parts, self.widths = [], []
        for kept, arrived in parts:
            width = kept.shape[1]
            self.widths.append(width)
            self.parts.append(tuple(array.reshape(pairs, -1, width) for array in (kept, arrived)))
        self.done = None

    def item(self):
        kept = self.parts[0][0]
        if not self.order:
            return ("last", self.parts, self.widths, None)
        bit = self.order[0]
        lower = sum(1 for other in self.bits if other < bit)
        return ("halve", self.parts, (kept.shape[0] >> (lower + 1), 1 << lower), bit)

    def take(self, outs):
        if not self.order:
            self.done = outs
            return []
        bit = self.order.pop(0)
        self.bits.remove(bit)
        kept, sent = outs
        route = [(place, place ^ (1 << bit)) for place in range(self.pairs)]
        self.parts = [(kept, lax.ppermute(sent, "dp", route))]
        return [sent]


class Total:
    def __init__(self, pairs, values):
        self.pairs = pairs
        bits = [1 << bit for bit in range((2 * pairs).bit_length() - 1)]
        self.left = [bits[-1:]] + [bits[place : place + 2] for place in range(0, len(bits) - 1, 2)]
        self.done = None
        self.launch(values)

    def launch(self, values):
        group = self.left.pop(0)
        masks = group + [sum(group)] if len(group) > 1 else group
        count = 2 * self.pairs
        arrived = [
            lax.ppermute(values, ("section", "dp"), [(place, place ^ mask) for place in range(count)])
            for mask in masks
        ]
        self.parts = [(values, *arrived)]
        self.sent = values

    def item(self):
        return ("add", self.parts, None, None)

    def take(self, outs):
        (values,) = outs
        if not self.left:
            self.done = values
            return []
        self.launch(values)
        return [values]


def in_thirds(kind, parts):
    return kind == "halve" and len(parts) == 1 and parts[0][0].shape[-1] % (3 * GROUP) == 0


def round_kernel(info_ref, *refs, items):
    place = 0
    out = sum(sum(widths) for _, widths, _, _, _, _ in items)
    for kind, widths, how, bit, count, split in items:
        pairs = []
        for width in widths:
            pairs.append(refs[place : place + width])
            place += width
        outs = refs[out : out + count]
        out += count
        run = functools.partial(round_item, info_ref, kind, pairs, how, bit, outs)
        if split:
            run()
        else:
            first_step(run)


def round_item(info_ref, kind, pairs, how, bit, outs):
    if kind == "add":
        outs[0][...] = sum(ref[...] for ref in pairs[0])
        return

    def total(pair, index):
        return pair[0][index].astype(jnp.float32) + pair[1][index].astype(jnp.float32)

    if kind == "last":
        start = 0
        values = [total(pair, 0) for pair in pairs]
        whole_row = values[0] if len(values) == 1 else jnp.concatenate(values, axis=1)
        for ref, width in zip(outs, how):
            ref[...] = whole_row[:, start : start + width]
            start += width
        return
    high, lower = how
    mine = (info_ref[BLOCK] >> bit) & 1
    for h in range(high):
        for l in range(lower):
            start = 0
            for pair in pairs:
                width = pair[0].shape[-1]
                for ref, chosen in zip(outs, (mine, 1 - mine)):
                    index = (h * 2 + chosen) * lower + l
                    ref[h * lower + l, :, start : start + width] = low(total(pair, index))
                start += width


def round_call(info, chains, name, after=(), through=()):
    items = [chain.item() for chain in chains]
    operands, specs, out_shape, out_specs, plain, counts, moved = [], [], [], [], [], [], 0
    for kind, parts, how, bit in items:
        split = in_thirds(kind, parts)
        for part in parts:
            operands += part
            moved += len(part) * part[0].size * part[0].dtype.itemsize
            if split:
                block = (*part[0].shape[:-1], part[0].shape[-1] // 3)
                specs += [pl.BlockSpec(block, lambda i, info: (0, 0, i))] * len(part)
            else:
                specs += [whole(array) for array in part]
        shape = parts[0][0].shape
        if kind == "add":
            shapes = [sds(shape, jnp.float32)]
        elif kind == "last":
            shapes = [sds((shape[1], width), jnp.float32) for width in how]
        else:
            width = sum(part[0].shape[-1] for part in parts)
            shapes = [sds((shape[0] // 2, shape[1], width))] * 2
        out_shape += shapes
        if split:
            out_specs += [
                pl.BlockSpec((*shape.shape[:-1], shape.shape[-1] // 3), lambda i, info: (0, 0, i))
                for shape in shapes
            ]
        else:
            out_specs += [whole(shape) for shape in shapes]
        counts.append(len(shapes))
        plain.append((kind, [len(part) for part in parts], how, bit, len(shapes), split))
    outs = call(
        functools.partial(round_kernel, items=plain),
        tuple(out_shape),
        (3 if any(item[-1] for item in plain) else 1,),
        specs,
        tuple(out_specs),
        moved,
        2 * moved,
        after=after,
        through=through,
        name=name,
    )(info, *operands)
    sent, start = [], 0
    for chain, count in zip(chains, counts):
        sent += chain.take(outs[start : start + count])
        start += count
    return sent, outs[start:]


def across(values):
    return lax.ppermute(values, "section", [(0, 1), (1, 0)])


def arrange_kernel(info_ref, *refs, strips):
    *sources, out_ref = refs
    holder = info_ref[STRIP + 2 * strips + pl.program_id(0)]
    slot = info_ref[STRIP + 4 * strips + pl.program_id(0)]
    per = len(sources) // 2
    values = None
    for place in range(strips):
        kept, arrived = (
            (sources[place][0], sources[per + place][0])
            if per == strips
            else (sources[0][place], sources[1][place])
        )
        chosen = jnp.where(holder == info_ref[0], kept, arrived)
        values = chosen if values is None else jnp.where(slot == place, chosen, values)
    out_ref[0] = values


def arrange_call(info, kept, arrived, strips, name, after=()):
    _, length, half = kept[0].shape
    return call(
        functools.partial(arrange_kernel, strips=strips),
        sds((2 * strips, length, half)),
        (2 * strips,),
        [whole(array) for array in (*kept, *arrived)],
        pl.BlockSpec((1, length, half), lambda k, info: (k, 0, 0)),
        1,
        strips * length * half * 12,
        name=name,
        after=after,
    )(info, *kept, *arrived)


def gather_small_kernel(
    info_ref, up_enc, up_dec, enc, dec, dec_in, final, *rest
):
    *enc_in, out_ref = rest
    out_ref[...] = jnp.zeros_like(out_ref)
    wide, narrow = enc.shape[1], dec.shape[1]
    out_ref[0:1, : up_enc.shape[1]] = up_enc[0:1, :]
    out_ref[1:2, : up_dec.shape[1]] = up_dec[0:1, :]
    out_ref[2:6, :wide] = enc[0:4, :]
    out_ref[2:6, wide : wide + narrow] = dec[0:4, :]
    out_ref[2:6, wide + narrow : wide + 2 * narrow] = dec_in[0:4, :]
    out_ref[6:8, :wide] = final[0:2, :]
    out_ref[6:8, wide : 2 * wide] = sum(ref[0:2, :] for ref in enc_in)


def gather_small_call(info, values):
    shape = (8, values[0].shape[1])
    return call(
        gather_small_kernel,
        sds(shape, jnp.float32),
        (1,),
        [whole(value) for value in values],
        pl.BlockSpec(shape, lambda i, info: (0, 0)),
        shape[1],
        shape[1] * 64,
        name="small_rows",
    )(info, *values)


def unshuffled(parts):
    return jnp.concatenate(
        [
            part[:, (3 * group + j) * GROUP : (3 * group + j + 1) * GROUP]
            for j in range(3)
            for part in parts
            for group in range(part.shape[1] // (3 * GROUP))
        ],
        axis=1,
    )


def shares_kernel(info_ref, rows_ref, dec_qkv_ref, *refs, parts, wide, narrow, units, dec_units, count):
    block = info_ref[BLOCK]

    def share(first, last, start, width):
        values = rows_ref[first:last, start : start + width]
        part = width // count
        return pltpu.roll(values, width - block * part, 1)[:, :part]

    enc_qkv = [ref[...] for ref in refs[:parts]]
    outs = refs[parts:]
    bias_up_enc = share(0, 1, 0, units)
    bias_up_dec = share(1, 2, 0, dec_units)
    enc = share(2, 6, 0, wide)
    dec = share(2, 6, wide, narrow)
    dec_in = share(2, 6, wide + narrow, narrow)
    final = share(6, 8, 0, wide)
    enc_in = share(6, 8, wide, wide)
    for ref, value in zip(
        outs,
        (
            jnp.concatenate([enc_in[0:1], enc[0:1], final[0:1]], axis=0),
            jnp.concatenate([enc_in[1:2], enc[1:2], final[1:2]], axis=0),
            enc[2:4],
            bias_up_enc,
            dec_in[3:4],
            dec_in[2:3],
            jnp.concatenate([dec_in[0:1], dec[0:1]], axis=0),
            jnp.concatenate([dec_in[1:2], dec[1:2]], axis=0),
            dec[2:4],
            bias_up_dec,
            unshuffled([dec_qkv_ref[...]]),
            unshuffled(enc_qkv),
        ),
    ):
        ref[...] = value


def shares_call(info, rows, dec_qkv, enc_qkv, wide, narrow, units, dec_units, count):
    shapes = [
        (height, width // count)
        for height, width in (
            (3, wide),
            (3, wide),
            (2, wide),
            (1, units),
            (1, narrow),
            (1, narrow),
            (2, narrow),
            (2, narrow),
            (2, narrow),
            (1, dec_units),
        )
    ] + [dec_qkv.shape, (wide // count, 3 * wide)]
    return call(
        functools.partial(
            shares_kernel,
            parts=len(enc_qkv),
            wide=wide,
            narrow=narrow,
            units=units,
            dec_units=dec_units,
            count=count,
        ),
        tuple(sds(shape, jnp.float32) for shape in shapes),
        (1,),
        [whole(array) for array in (rows, dec_qkv, *enc_qkv)],
        tuple(pl.BlockSpec(shape, lambda i, info: (0, 0)) for shape in shapes),
        rows.size,
        rows.size * 4,
        name="shares",
    )(info, rows, dec_qkv, *enc_qkv)


def decoder_shares_kernel(info_ref, rows_ref, up_ref, out_ref, down_ref):
    width = out_ref.shape[1]
    units = up_ref.shape[1]
    share = up_ref.shape[0]
    rows = rows_ref[...]
    up_ref[...] = rows[:, :units]
    out_ref[...] = rows[:, units : units + width]
    for fold in range(units // width):
        start = units + (fold + 1) * width
        down_ref[fold * share : (fold + 1) * share, :] = rows[:, start : start + width]


def decoder_shares_call(info, rows, width, units, after):
    share = rows.shape[0]
    shapes = ((share, units), (share, width), (share * units // width, width))
    return call(
        decoder_shares_kernel,
        tuple(sds(shape, jnp.float32) for shape in shapes),
        (1,),
        [whole(rows)],
        tuple(pl.BlockSpec(shape, lambda i, info: (0, 0)) for shape in shapes),
        rows.size,
        rows.size * 6,
        name="decoder_shares",
        after=after,
    )(info, rows)


def place_table(length_rows, model_width):
    halfway = model_width // 2
    places = np.arange(length_rows, dtype=np.float64)[:, None]
    rates = np.exp(np.arange(halfway, dtype=np.float64) * (-math.log(10000.0) / halfway))[None, :]
    return np.concatenate([np.sin(places * rates), np.cos(places * rates)], axis=1).astype(
        np.float32
    )


def local(
    patches,
    visible,
    source,
    enc_gains,
    enc_shifts,
    enc_qkv,
    enc_out,
    enc_bias_out,
    enc_up,
    enc_bias_up,
    enc_down,
    enc_proj,
    proj_bias,
    mask_token,
    dec_gains,
    dec_shifts,
    dec_qkv,
    dec_out,
    dec_bias_out,
    dec_up,
    dec_bias_up,
    dec_down,
    cotangent,
):
    pairs = lax.axis_size("dp")
    count = 2 * pairs
    length = patches.shape[1]
    wide = patches.shape[2]
    narrow = dec_qkv.shape[0]
    strips = patches.shape[0] // 2
    padded = -(-(length + 1) // ROW_STEP) * ROW_STEP
    sizes = Sizes(strips, length, padded)
    rows = sizes.rows
    info = place_info(visible, strips)
    taken = jnp.pad(
        jnp.where(source < 0, padded - 1, source),
        ((0, 0), (0, padded - length)),
        constant_values=padded - 1,
    )
    places = jnp.asarray(place_table(padded, narrow))
    strip_form = lambda array: array.reshape(strips, padded, array.shape[-1])
    row_form = lambda array: array.reshape(rows, array.shape[-1])

    n1_enc, packed_enc = packed_call(sizes, info, patches, enc_gains, enc_shifts, enc_qkv)
    packed_enc = strip_form(packed_enc)
    enc_live = visible_live(strips)
    mixed_enc = row_form(attend_call(packed_enc, info, HEADS_ENC, enc_live, "encoder_attention"))
    mid_enc, n2_enc, act_enc, slope_enc, y_enc, encoded, projected = encoder_ff_call(
        sizes,
        info,
        patches,
        mixed_enc,
        enc_gains,
        enc_shifts,
        enc_out,
        enc_bias_out,
        enc_up,
        enc_bias_up,
        enc_down,
        enc_proj,
        proj_bias,
    )
    x_dec, n1_dec, packed_dec = decoder_in_call(
        sizes, info, projected, taken, mask_token, places, dec_gains, dec_shifts, dec_qkv
    )
    x_dec, n1_dec, packed_dec = map(strip_form, (x_dec, n1_dec, packed_dec))
    dec_live = all_live(length)
    mixed_dec = row_form(attend_call(packed_dec, info, HEADS_DEC, dec_live, "decoder_attention"))
    share = narrow // count
    (
        kept_dec,
        sent_dec,
        gb_dec,
        dmixed_dec,
        sums_dec,
        up_sums_dec,
        kept_beside,
        sent_beside,
        *apart,
    ) = decoder_ff_call(
        sizes,
        info,
        row_form(x_dec),
        mixed_dec,
        cotangent,
        dec_gains,
        dec_shifts,
        dec_out,
        dec_bias_out,
        dec_up,
        dec_bias_up,
        dec_down,
        share,
    )
    arrived_beside, arrived_dec = map(across, (sent_beside, sent_dec))
    enc_half = wide // 2
    dpacked_dec, kept_dqkv, sent_dqkv = attend_back_call(
        packed_dec,
        strip_form(dmixed_dec),
        n1_dec,
        info,
        HEADS_DEC,
        dec_live,
        0,
        1,
        (sent_beside, sent_dec),
        "decoder_attention_back",
    )
    arrived_dqkv = across(sent_dqkv)
    decoded = arrange_call(info, [kept_dec], [arrived_dec], strips, "decoded_strips", (dpacked_dec,))
    grad_enc, sums_dec_in, sums_final, kept_proj, sent_proj = decoder_back_call(
        sizes,
        info,
        dpacked_dec,
        strip_form(gb_dec),
        x_dec,
        taken,
        strip_form(y_enc),
        strip_form(encoded),
        dec_gains,
        dec_shifts,
        dec_qkv,
        enc_proj,
        enc_gains,
        enc_shifts,
        (sent_dqkv, decoded),
    )
    grad_enc = row_form(grad_enc)
    arrived_proj = across(sent_proj)
    ((kept_edown, sent_edown),) = product_call(
        info, [(act_enc, grad_enc, enc_half, wide)], "grad_enc_down", (sent_proj,)
    )
    grads_dec = Chain(
        pairs, (0, 1, 2, 3), ((kept_beside, arrived_beside), (kept_dqkv, arrived_dqkv))
    )
    sent, (sent_edown,) = round_call(
        info, [grads_dec], "round_1", (kept_edown, arrived_proj), (sent_edown,)
    )
    arrived_edown = across(sent_edown)
    dhid_enc, gb_enc, dmixed_enc, sums_enc, up_sums_enc = encoder_ff_back_call(
        sizes,
        info,
        grad_enc,
        mid_enc,
        slope_enc,
        enc_gains,
        enc_shifts,
        enc_out,
        enc_up,
        enc_down,
        (*sent, sent_edown),
    )
    (kept_eup, sent_eup), (kept_eout, sent_eout) = product_call(
        info,
        [(n2_enc, dhid_enc, enc_half, wide), (mixed_enc, gb_enc, enc_half, wide)],
        "grad_enc_up_out",
        sent,
    )
    down_enc = Chain(pairs, (0, 2, 1, 3), ((kept_edown, arrived_edown),))
    sent, (sent_eup, sent_eout) = round_call(
        info, [down_enc, grads_dec], "round_2", (kept_eout,), (sent_eup, sent_eout)
    )
    arrived_eup, arrived_eout = map(across, (sent_eup, sent_eout))
    up_enc = Chain(pairs, (1, 0, 2, 3), ((kept_eup, arrived_eup),))
    out_enc = Chain(pairs, (0, 1, 2, 3), ((kept_eout, arrived_eout), (kept_proj, arrived_proj)))
    every = [up_enc, down_enc, grads_dec, out_enc]
    active = lambda: [chain for chain in every if chain.done is None]
    after = (*sent, sent_eup, sent_eout)
    number, dpacked_enc, qkv_enc = 3, [], []
    by_y, by_z = (1, 0, 2, 3), (2, 0, 1, 3)
    for part in range(PARTS):
        dpacked, kept, sent_here = attend_back_call(
            packed_enc,
            strip_form(dmixed_enc),
            strip_form(n1_enc),
            info,
            HEADS_ENC,
            enc_live,
            part,
            PARTS,
            after,
            f"encoder_attention_back_{part}",
        )
        dpacked_enc.append(dpacked)
        sent, (sent_here,) = round_call(info, active(), f"round_{number}", (dpacked,), (sent_here,))
        chain = Chain(pairs, (by_z, by_y)[part % 2], ((kept, across(sent_here)),))
        number += 1
        qkv_enc.append(chain)
        every.append(chain)
        after = (*sent, sent_here)
    kept_enc, sent_enc, sums_enc_in = [], [], []
    for strip in range(strips):
        kept, sent_here, sums = encoder_back_call(
            sizes, info, dpacked_enc, gb_enc, patches, enc_gains, enc_shifts, enc_qkv, strip, after
        )
        kept_enc.append(kept)
        sums_enc_in.append(sums)
        sent_enc.append(sent_here)
        through = ()
        if strip == strips - 1:
            through = tuple(sent_enc)
            if apart:
                down_dec = Chain(pairs, by_y, ((apart[0], across(apart[1])),))
                every.append(down_dec)
            small = gather_small_call(
                info,
                (
                    up_sums_enc,
                    up_sums_dec,
                    sums_enc,
                    sums_dec,
                    sums_dec_in,
                    sums_final,
                    *sums_enc_in,
                ),
            )
            through += (small,)
        sent, through = round_call(info, active(), f"round_{number}", (sums,), through)
        number += 1
        after = (*sent,)
    *sent_enc, small = through
    arrived_enc = [across(array) for array in sent_enc]
    small = Total(pairs, small)
    every.append(small)
    patch_grad = arrange_call(info, kept_enc, arrived_enc, strips, "patch_grad_strips", after)
    after = (patch_grad,)
    while active():
        round_call(info, active(), f"round_{number}", after)
        after = ()
        number += 1
    g_beside, g_dqkv = grads_dec.done
    shares = shares_call(
        info,
        small.done,
        g_dqkv,
        [chain.done[0] for chain in qkv_enc],
        wide,
        narrow,
        enc_up.shape[1],
        dec_up.shape[1],
        count,
    )
    if apart:
        g_dup, g_dout = g_beside[:, : dec_up.shape[1]], g_beside[:, dec_up.shape[1] :]
        (g_ddown,) = down_dec.done
    else:
        g_dup, g_dout, g_ddown = decoder_shares_call(info, g_beside, narrow, dec_up.shape[1], ())
    (g_edown,), (g_eup,) = down_enc.done, up_enc.done
    g_eout, g_proj = out_enc.done
    return (
        decoded,
        patch_grad,
        shares[0],
        shares[1],
        shares[11],
        g_eout,
        shares[2],
        g_eup,
        shares[3].reshape(-1),
        g_edown,
        g_proj,
        shares[4].reshape(-1),
        shares[5].reshape(-1),
        shares[6],
        shares[7],
        shares[10],
        g_dout,
        shares[8],
        g_dup,
        shares[9].reshape(-1),
        g_ddown,
    )


def solution(mesh):
    return jax.shard_map(
        local,
        mesh=mesh,
        in_specs=(
            P("dp", None, None),
            P("dp"),
            P("dp", None),
            P(),
            P(),
            P(),
            P(),
            P(),
            P(),
            P(),
            P(),
            P(),
            P(),
            P(),
            P(),
            P(),
            P(),
            P(),
            P(),
            P(),
            P(),
            P(),
            P("dp", None, None),
        ),
        out_specs=(
            P("dp", None, "section"),
            P("dp", None, "section"),
            P(None, ("section", "dp")),
            P(None, ("section", "dp")),
            P(("section", "dp"), None),
            P(("section", "dp"), None),
            P(None, ("section", "dp")),
            P(("section", "dp"), None),
            P(("section", "dp")),
            P(("section", "dp"), None),
            P(("section", "dp"), None),
            P(("section", "dp")),
            P(("section", "dp")),
            P(None, ("section", "dp")),
            P(None, ("section", "dp")),
            P(("section", "dp"), None),
            P(("section", "dp"), None),
            P(None, ("section", "dp")),
            P(("section", "dp"), None),
            P(("section", "dp")),
            P(("section", "dp"), None),
        ),
        check_vma=False,
    )
```

time: 505 us -> 444 us (0.88)
  Pallas kernels: 379 us -> 352 us
  waiting for transfers between devices: 43.9 us -> 17.5 us
  between operations: 15.1 us -> 1.45 us
  starting transfers between devices: 34.2 us -> 41.4 us
    pallas_call x32 -> x29, Pallas kernels: 379 us -> 352 us  [call(): return lambda *operands: made(*operands, *after, *through)]
    ppermute x24, waiting for transfers between devices: 41.1 us -> 17.4 us  [take(): self.parts = [(kept, lax.ppermute(sent, 'dp', route))]]
    ppermute x24, starting transfers between devices: 22.1 us -> 30.8 us  [take(): self.parts = [(kept, lax.ppermute(sent, 'dp', route))]]
    unnamed x116 -> x94, local copies, waits for them, and re-layouts: 21.9 us -> 20.5 us
  transfers between devices with their start and end apart: 42 -> 42, of which waited for: 11 -> 5; matrix products, arithmetic and copies ran while one was open for 1% -> 1% of each run, Pallas kernels for 37% -> 44%
where the time goes in v3:
time: 444 us; the launch traced here: 437 us
  Pallas kernels  352 us (79%)
  starting transfers between devices  41.4 us (9%)
  local copies, waits for them, and re-layouts  24.3 us (5%)
  waiting for transfers between devices  17.5 us (4%)
    pallas_call x29, Pallas kernels, call(): return lambda *operands: made(*operands, *after, *through)  352 us
    ppermute x24, starting transfers between devices, take(): self.parts = [(kept, lax.ppermute(sent, 'dp', route))]  30.8 us
    unnamed x94, local copies, waits for them, and re-layouts  20.5 us
    ppermute x24, waiting for transfers between devices, take(): self.parts = [(kept, lax.ppermute(sent, 'dp', route))]  17.4 us
  transfers between devices with their start and end apart: 42, of which 5 were waited for; matrix products, arithmetic and copies ran while one was open for 1% of the time, Pallas kernels for 44%

profile of v3, /device:TPU:0, one launch (start us, length us, event | category | flops | bytes accessed | tf_op | source)
XLA Modules:
  0.0 437.3 jit_solution(2607603968737716125)
XLA Ops:
  1.4 3.6 copy.67.refs_1_.refs_2_
  7.9 9.7 %encoder_packed.1 = (bf16[1088,768]{1,0:T(8,128)(2,1)}, bf16[1088,2304]{1,0:T(8,128)(2,1)}) custom-call(s32[14]{0:T(128)} %concatenate.3.refs_0_, bf16[4,529,768]{2,1,0:T(8,128)(2,1)} %copy.65.refs_1_.refs_2_.refs_6_, bf16[4,529,768]{2,1,0:T(8,128)(2,1)} %copy.65.refs_1_.refs_2_.refs_6_, bf16[3,768]{1,0:T(4,128)(2,1)} %refs_7_.13, bf16[3,768]{1,0:T(4,128)(2,1)} %refs_8_.11, ...), custom_call_target="tpu_custom_call" | custom-call | flops 15040512 | bytes 46464 | tf_op jit(solution)/shard_map/encoder_packed/pallas_call | solution.py:69
  17.7 16.1 %encoder_attention.1 = bf16[2,544,768]{2,1,0:T(8,128)(2,1)} custom-call(s32[14]{0:T(128)} %concatenate.3.refs_0_, bf16[2,544,2304]{2,1,0:T(8,128)(2,1)} %bitcast.35, bf16[2,544,2304]{2,1,0:T(8,128)(2,1)} %bitcast.36, bf16[2,544,2304]{2,1,0:T(8,128)(2,1)} %bitcast.37), custom_call_target="tpu_custom_call" | custom-call | flops 21307392 | bytes 26112 | tf_op jit(solution)/shard_map/encoder_attention/pallas_call | solution.py:69
  34.4 24.7 %encoder_feed_forward.1 = (bf16[1088,768]{1,0:T(8,128)(2,1)}, bf16[1088,768]{1,0:T(8,128)(2,1)}, bf16[1088,3072]{1,0:T(8,128)(2,1)}, bf16[1088,3072]{1,0:T(8,128...) custom-call(s32[14]{0:T(128)} %concatenate.3.refs_0_, ...), custom_call_target="tpu_custom_call" | custom-call | flops 48463872 | bytes 148992 | tf_op jit(solution)/shard_map/encoder_feed_forward/pallas_call | solution.py:69
  59.1 8.2 %decoder_packed.1 = (f32[1088,512]{1,0:T(8,128)}, bf16[1088,512]{1,0:T(8,128)(2,1)}, bf16[1088,1536]{1,0:T(8,128)(2,1)}) custom-call(s32[14]{0:T(128)} %concatenate.3.refs_0_, bf16[1088,512]{1,0:T(8,128)(2,1)} %get-tuple-element.155.refs_1_, s32[4,544]{1,0:T(4,128)} %pad.4.refs_2_.refs_4_, bf16[512]{0:T(512)(128)(2,1)} %refs_3_.5, ...), custom_call_target="tpu_custom_call" | custom-call | flops 9052160 | bytes 45312 | tf_op jit(solution)/shard_map/decoder_packed/pallas_call | solution.py:69
  67.2 20.5 %decoder_attention.1 = bf16[2,544,512]{2,1,0:T(8,128)(2,1)} custom-call(s32[14]{0:T(128)} %concatenate.3.refs_0_, bf16[2,544,1536]{2,1,0:T(8,128)(2,1)} %bitcast.44, bf16[2,544,1536]{2,1,0:T(8,128)(2,1)} %bitcast.45, bf16[2,544,1536]{2,1,0:T(8,128)(2,1)} %bitcast.46), custom_call_target="tpu_custom_call" | custom-call | flops 28409856 | bytes 17408 | tf_op jit(solution)/shard_map/decoder_attention/pallas_call | solution.py:69
  87.7 28.6 %decoder_feed_forward.1 = (bf16[2,529,256]{2,1,0:T(8,128)(2,1)}, bf16[2,529,256]{2,1,0:T(8,128)(2,1)}, bf16[1088,512]{1,0:T(8,128)(2,1)}, bf16[1088,512]{1,0:T(8...) custom-call(s32[14]{0:T(128)} %concatenate.3.refs_0_, ...), custom_call_target="tpu_custom_call" | custom-call | flops 60162048 | bytes 71680 | tf_op jit(solution)/shard_map/decoder_feed_forward/pallas_call | solution.py:69
  118.5 50.8 %decoder_attention_back.1 = (bf16[3,2,544,512]{3,2,1,0:T(8,128)(2,1)}, bf16[256,1536]{1,0:T(8,128)(2,1)}, bf16[256,1536]{1,0:T(8,128)(2,1)}) custom-call(s32[14]{0:T(128)} %concatenate.3.refs_0_, bf16[2,544,1536]{2,1,0:T(8,128)(2,1)} %bitcast.47, bf16[2,544,1536]{2,1,0:T(8,128)(2,1)} %bitcast.48, bf16[2,544,1536]{2,1,0:T(8,128)(2,1)} %bitcast.49, ...), custom_call_target="tpu_custom_call" | custom-call | flops 63504384 | bytes 30464 | tf_op jit(solution)/shard_map/decoder_attention_back/pallas_call | solution.py:69
  170.7 3.5 decoded_strips.1.refs_14_
  174.3 14.8 %decoder_packed_back.1 = (bf16[2,544,768]{2,1,0:T(8,128)(2,1)}, f32[8,512]{1,0:T(8,128)}, f32[8,768]{1,0:T(8,128)}, bf16[384,512]{1,0:T(8,128)(2,1)}, bf16[384,512]{1,0:T(8,128)(2,1)}) custom-call(s32[14]{0:T(128)} %concatenate.3.refs_0_, bf16[3,2,544,512]{3,2,1,0:T(8,128)(2,1)} %get-tuple-element.163.refs_3_.refs_1_, bf16[2,544,512]{2,1,0:T(8,128)(2,1)} %bitcast.73, ...), custom_call_target="tpu_custom_call" | custom-call | flops 15736832 | bytes 70144 | tf_op jit(solution)/shard_map/decoder_packed_back/pallas_call | solution.py:69
  189.1 10.9 %grad_enc_down.1 = (bf16[1536,768]{1,0:T(8,128)(2,1)}, bf16[1536,768]{1,0:T(8,128)(2,1)}) custom-call(s32[14]{0:T(128)} %concatenate.3.refs_0_, bf16[1088,3072]{1,0:T(8,128)(2,1)} %get-tuple-element.173.refs_1_.refs_2_, bf16[1088,3072]{1,0:T(8,128)(2,1)} %get-tuple-element.173.refs_1_.refs_2_, bf16[1088,768]{1,0:T(8,128)(2,1)} %bitcast.59, ...), custom_call_target="tpu_custom_call" | custom-call | flops 20054016 | bytes 51072 | tf_op jit(solution)/shard_map/grad_enc_down/pallas_call | solution.py:69
  201.8 5.8 %round_1.1 = (bf16[8,16,6144]{2,1,0:T(8,128)(2,1)}, bf16[8,16,6144]{2,1,0:T(8,128)(2,1)}, bf16[1536,768]{1,0:T(8,128)(2,1)}) custom-call(s32[14]{0:T(128)} %concatenate.3.refs_0_, bf16[16,16,4608]{2,1,0:T(8,128)(2,1)} %bitcast.64, bf16[16,16,4608]{2,1,0:T(8,128)(2,1)} %bitcast.65, bf16[16,16,1536]{2,1,0:T(8,128)(2,1)} %bitcast.78, ...), custom_call_target="tpu_custom_call", output_to_operand_aliasing={{2}: (7, {})} | custom-call | flops 24576 | bytes 49152 | tf_op jit(solution)/shard_map/round_1/pallas_call | solution.py:69
  210.5 22.1 %encoder_feed_forward_back.1 = (bf16[1088,3072]{1,0:T(8,128)(2,1)}, bf16[1088,768]{1,0:T(8,128)(2,1)}, bf16[1088,768]{1,0:T(8,128)(2,1)}, f32[8,768]{1,0:T(8,128)}, f32[8,3072]{1,0:T(8,128)}) custom-call(s32[14]{0:T(128)} %concatenate.3.refs_0_, bf16[1088,768]{1,0:T(8,128)(2,1)} %bitcast.60, bf16[1088,768]{1,0:T(8,128)(2,1)} %get-tuple-element.169.refs_2_, ...), custom_call_target="tpu_custom_call" | custom-call | flops 45121536 | bytes 145920 | tf_op jit(solution)/shard_map/encoder_feed_forward_back/pallas_call | solution.py:69
  232.6 14.0 %grad_enc_up_out.1 = (bf16[384,3072]{1,0:T(8,128)(2,1)}, bf16[384,3072]{1,0:T(8,128)(2,1)}, bf16[384,768]{1,0:T(8,128)(2,1)}, bf16[384,768]{1,0:T(8,128)(2,1)}) custom-call(s32[14]{0:T(128)} %concatenate.3.refs_0_, bf16[1088,768]{1,0:T(8,128)(2,1)} %get-tuple-element.182.refs_1_.refs_2_, bf16[1088,768]{1,0:T(8,128)(2,1)} %get-tuple-element.182.refs_1_.refs_2_, ...), custom_call_target="tpu_custom_call" | custom-call | flops 25067520 | bytes 68736 | tf_op jit(solution)/shard_map/grad_enc_up_out/pallas_call | solution.py:69
  248.5 6.8 %round_2.1 = (bf16[8,96,768]{2,1,0:T(8,128)(2,1)}, bf16[8,96,768]{2,1,0:T(8,128)(2,1)}, bf16[4,16,6144]{2,1,0:T(8,128)(2,1)}, bf16[4,16,6144]{2,1,0:T(8,128)(2,1...) custom-call(s32[14]{0:T(128)} %concatenate.3.refs_0_, ...), custom_call_target="tpu_custom_call", output_to_operand_aliasing={{4}: (6, {}), {5}: (7, {})} | custom-call | flops 30720 | bytes 61440 | tf_op jit(solution)/shard_map/round_2/pallas_call | solution.py:69
  257.8 25.6 %encoder_attention_back_0.1 = (bf16[3,2,544,384]{3,2,1,0:T(8,128)(2,1)}, bf16[384,1152]{1,0:T(8,128)(2,1)}, bf16[384,1152]{1,0:T(8,128)(2,1)}) custom-call(s32[14]{0:T(128)} %concatenate.3.refs_0_, bf16[2,544,2304]{2,1,0:T(8,128)(2,1)} %bitcast.38, bf16[2,544,2304]{2,1,0:T(8,128)(2,1)} %bitcast.39, bf16[2,544,2304]{2,1,0:T(8,128)(2,1)} %bitcast.40, ...), custom_call_target="tpu_custom_call" | custom-call | flops 28827648 | bytes 22848 | tf_op jit(solution)/shard_map/encoder_attention_back_0/pallas_call | solution.py:69
  285.7 8.6 %round_3.1 = (bf16[8,24,3072]{2,1,0:T(8,128)(2,1)}, bf16[8,24,3072]{2,1,0:T(8,128)(2,1)}, bf16[4,96,768]{2,1,0:T(8,128)(2,1)}, bf16[4,96,768]{2,1,0:T(8,128)(2,1...) custom-call(s32[14]{0:T(128)} %concatenate.3.refs_0_, ...), custom_call_target="tpu_custom_call", output_to_operand_aliasing={{8}: (12, {})} | custom-call | flops 41472 | bytes 82944 | tf_op jit(solution)/shard_map/round_3/pallas_call | solution.py:69
  298.8 25.3 %encoder_attention_back_1.1 = (bf16[3,2,544,384]{3,2,1,0:T(8,128)(2,1)}, bf16[384,1152]{1,0:T(8,128)(2,1)}, bf16[384,1152]{1,0:T(8,128)(2,1)}) custom-call(s32[14]{0:T(128)} %concatenate.3.refs_0_, bf16[2,544,2304]{2,1,0:T(8,128)(2,1)} %bitcast.41, bf16[2,544,2304]{2,1,0:T(8,128)(2,1)} %bitcast.42, bf16[2,544,2304]{2,1,0:T(8,128)(2,1)} %bitcast.43, ...), custom_call_target="tpu_custom_call" | custom-call | flops 28827648 | bytes 22848 | tf_op jit(solution)/shard_map/encoder_attention_back_1/pallas_call | solution.py:69
  325.9 6.6 %round_4.1 = (bf16[4,24,3072]{2,1,0:T(8,128)(2,1)}, bf16[4,24,3072]{2,1,0:T(8,128)(2,1)}, bf16[2,96,768]{2,1,0:T(8,128)(2,1)}, bf16[2,96,768]{2,1,0:T(8,128)(2,1...) custom-call(s32[14]{0:T(128)} %concatenate.3.refs_0_, ...), custom_call_target="tpu_custom_call", output_to_operand_aliasing={{10}: (12, {})} | custom-call | flops 27648 | bytes 55296 | tf_op jit(solution)/shard_map/round_4/pallas_call | solution.py:69
  333.7 2.6 collective-permute-start.17
  338.6 7.5 %collective-permute-done.17.refs_6_ = bf16[1,16,6144]{2,1,0:T(8,128)(2,1)S(1)} collective-permute-done((bf16[1,16,6144]{2,1,0:T(8,128)(2,1)}, bf16[1,16,6144]{2,1,0:T(8,128)(2,1)S(1)}, u32[]{:S(2)}, u32[]{:S(2)}) %collective-permute-start.17) | collective-permute-done | bytes 196640 | tf_op jit(solution)/shard_map/ppermute | solution.py:1104
  346.8 8.9 %encoder_packed_back_0.1 = (bf16[1,529,384]{2,1,0:T(8,128)(2,1)}, bf16[1,529,384]{2,1,0:T(8,128)(2,1)}, f32[8,768]{1,0:T(8,128)}) custom-call(s32[14]{0:T(128)} %concatenate.3.refs_0_, bf16[3,2,544,384]{3,2,1,0:T(8,128)(2,1)} %get-tuple-element.192.refs_11_.refs_1_, bf16[3,2,544,384]{3,2,1,0:T(8,128)(2,1)} %get-tuple-element.203.refs_11_.refs_2_, ...), custom_call_target="tpu_custom_call" | custom-call | flops 7520256 | bytes 33408 | tf_op jit(solution)/shard_map/encoder_packed_back_0/pallas_call | solution.py:69
  357.1 6.2 %round_5.1 = (bf16[2,24,3072]{2,1,0:T(8,128)(2,1)}, bf16[2,24,3072]{2,1,0:T(8,128)(2,1)}, bf16[1,96,768]{2,1,0:T(8,128)(2,1)}, bf16[1,96,768]{2,1,0:T(8,128)(2,1...) custom-call(s32[14]{0:T(128)} %concatenate.3.refs_0_, ...), custom_call_target="tpu_custom_call" | custom-call | flops 20736 | bytes 41472 | tf_op jit(solution)/shard_map/round_5/pallas_call | solution.py:69
  366.4 3.3 collective-permute-start.22
  369.7 8.8 %encoder_packed_back_1.1 = (bf16[1,529,384]{2,1,0:T(8,128)(2,1)}, bf16[1,529,384]{2,1,0:T(8,128)(2,1)}, f32[8,768]{1,0:T(8,128)}) custom-call(s32[14]{0:T(128)} %concatenate.3.refs_0_, bf16[3,2,544,384]{3,2,1,0:T(8,128)(2,1)} %get-tuple-element.192.refs_11_.refs_1_, bf16[3,2,544,384]{3,2,1,0:T(8,128)(2,1)} %get-tuple-element.203.refs_11_.refs_2_, ...), custom_call_target="tpu_custom_call" | custom-call | flops 7520256 | bytes 33408 | tf_op jit(solution)/shard_map/encoder_packed_back_1/pallas_call | solution.py:69
  381.9 4.5 %round_6.1 = (bf16[1,24,3072]{2,1,0:T(8,128)(2,1)}, bf16[1,24,3072]{2,1,0:T(8,128)(2,1)}, f32[96,768]{1,0:T(8,128)}, bf16[1,24,1280]{2,1,0:T(8,128)(2,1)}, bf16[...) custom-call(s32[14]{0:T(128)} %concatenate.3.refs_0_, ...), custom_call_target="tpu_custom_call", output_to_operand_aliasing={{9}: (12, {}), {10}: (13, {}), {11}: (14, {})} | custom-call | flops 9600 | bytes 19200 | tf_op jit(solution)/shard_map/round_6/pallas_call | solution.py:69
  391.8 3.9 patch_grad_strips.1.refs_11_
  395.7 4.8 %collective-permute-done.29.refs_4_ = bf16[1,24,1280]{2,1,0:T(8,128)(2,1)S(1)} collective-permute-done((bf16[1,24,1280]{2,1,0:T(8,128)(2,1)}, bf16[1,24,1280]{2,1,0:T(8,128)(2,1)S(1)}, u32[]{:S(2)}, u32[]{:S(2)}) %collective-permute-start.29) | collective-permute-done | bytes 61472 | tf_op jit(solution)/shard_map/ppermute | solution.py:1104
  401.3 4.1 round_7.1
  411.3 3.0 collective-permute-done.33.refs_2_
  415.1 3.4 round_8.1
  434.6 2.5 shares.1
  (183 shorter events, 66.1 us)
Async XLA Ops:
  116.3 83.8 %collective-permute-start.1 = (bf16[256,4608]{1,0:T(8,128)(2,1)}, bf16[256,4608]{1,0:T(8,128)(2,1)S(1)}, u32[]{:S(2)}, u32[]{:S(2)}) collective-permute-start(bf16[256,4608]{1,0:T(8,128)(2,1)} %get-tuple-element.162.refs_6_), channel_id=1, source_target_pairs={{0,16},{16,0},{1,17},{17,1},{2,18},{18,2},{3,19},{19,3},{4,20},{20... | collective-permute-start | bytes 7077896 | tf_op jit(solution)/shard_map/ppermute | solution.py:1240
  118.4 51.4 %collective-permute-start = (bf16[2,529,256]{2,0,1:T(2,128)(2,1)S(1)}, bf16[2,529,256]{2,0,1:T(2,128)(2,1)S(1)}, u32[]{:S(2)}, u32[]{:S(2)}) collective-permute-start(bf16[2,529,256]{2,0,1:T(2,128)(2,1)S(1)} %copy.69), channel_id=1, source_target_pairs={{0,16},{16,0},{1,17},{17,1},{2,18},{18,2},{3,19},{19,3},{4,20},{20... | collective-permute-start | bytes 1625096 | tf_op jit(solution)/shard_map/ppermute | solution.py:1240
  169.3 30.8 %collective-permute-start.2 = (bf16[256,1536]{1,0:T(8,128)(2,1)}, bf16[256,1536]{1,0:T(8,128)(2,1)S(1)}, u32[]{:S(2)}, u32[]{:S(2)}) collective-permute-start(bf16[256,1536]{1,0:T(8,128)(2,1)} %get-tuple-element.167.refs_13_), channel_id=1, source_target_pairs={{0,16},{16,0},{1,17},{17,1},{2,18},{18,2},{3,19},{19,3},{4,20},{20... | collective-permute-start | bytes 2359304 | tf_op jit(solution)/shard_map/ppermute | solution.py:1240
  189.0 11.1 %collective-permute-start.3 = (bf16[384,512]{1,0:T(8,128)(2,1)}, bf16[384,512]{1,0:T(8,128)(2,1)S(1)}, u32[]{:S(2)}, u32[]{:S(2)}) collective-permute-start(bf16[384,512]{1,0:T(8,128)(2,1)} %get-tuple-element.174.refs_4_), channel_id=1, source_target_pairs={{0,16},{16,0},{1,17},{17,1},{2,18},{18,2},{3,19},{19,3},{4,20},{20... | collective-permute-start | bytes 1179656 | tf_op jit(solution)/shard_map/ppermute | solution.py:1240
  207.6 39.0 %collective-permute-start.4 = (bf16[1536,768]{1,0:T(8,128)(2,1)}, bf16[1536,768]{1,0:T(8,128)(2,1)S(1)}, u32[]{:S(2)}, u32[]{:S(2)}) collective-permute-start(bf16[1536,768]{1,0:T(8,128)(2,1)} %get-tuple-element.178.refs_10_), channel_id=1, source_target_pairs={{0,16},{16,0},{1,17},{17,1},{2,18},{18,2},{3,19},{19,3},{4,20},{20... | collective-permute-start | bytes 7077896 | tf_op jit(solution)/shard_map/ppermute | solution.py:1240
  208.1 38.5 %collective-permute-start.5 = (bf16[8,16,6144]{2,1,0:T(8,128)(2,1)}, bf16[8,16,6144]{2,1,0:T(8,128)(2,1)S(1)}, u32[]{:S(2)}, u32[]{:S(2)}) collective-permute-start(bf16[8,16,6144]{2,1,0:T(8,128)(2,1)} %get-tuple-element.177.refs_9_.refs_7_), channel_id=1, source_target_pairs={{0,1},{1,0},{2,3},{3,2},{4,5},{5,4},{6,7},{7,6},{8,9},{9,8},{10,11... | collective-permute-start | bytes 4718600 | tf_op jit(solution)/shard_map/ppermute | solution.py:1104
  255.3 28.6 %collective-permute-start.6 = (bf16[384,3072]{1,0:T(8,128)(2,1)}, bf16[384,3072]{1,0:T(8,128)(2,1)S(1)}, u32[]{:S(2)}, u32[]{:S(2)}) collective-permute-start(bf16[384,3072]{1,0:T(8,128)(2,1)} %get-tuple-element.190.refs_8_), channel_id=1, source_target_pairs={{0,16},{16,0},{1,17},{17,1},{2,18},{18,2},{3,19},{19,3},{4,20},{20... | collective-permute-start | bytes 7077896 | tf_op jit(solution)/shard_map/ppermute | solution.py:1240
  255.5 28.4 %collective-permute-start.7 = (bf16[8,96,768]{2,1,0:T(8,128)(2,1)}, bf16[8,96,768]{2,1,0:T(8,128)(2,1)S(1)}, u32[]{:S(2)}, u32[]{:S(2)}) collective-permute-start(bf16[8,96,768]{2,1,0:T(8,128)(2,1)} %get-tuple-element.188.refs_6_), channel_id=1, source_target_pairs={{0,1},{1,0},{2,3},{3,2},{4,5},{5,4},{6,7},{7,6},{8,9},{9,8},{10,11... | collective-permute-start | bytes 3538952 | tf_op jit(solution)/shard_map/ppermute | solution.py:1104
  256.3 27.1 %collective-permute-start.8 = (bf16[4,16,6144]{2,1,0:T(8,128)(2,1)}, bf16[4,16,6144]{2,1,0:T(8,128)(2,1)S(1)}, u32[]{:S(2)}, u32[]{:S(2)}) collective-permute-start(bf16[4,16,6144]{2,1,0:T(8,128)(2,1)} %get-tuple-element.189.refs_7_), channel_id=1, source_target_pairs={{0,2},{1,3},{2,0},{3,1},{4,6},{5,7},{6,4},{7,5},{8,10},{9,11},{10,... | collective-permute-start | bytes 2359304 | tf_op jit(solution)/shard_map/ppermute | solution.py:1104
  257.8 25.6 %collective-permute-start.9 = (bf16[384,768]{1,0:T(8,128)(2,1)}, bf16[384,768]{1,0:T(8,128)(2,1)S(1)}, u32[]{:S(2)}, u32[]{:S(2)}) collective-permute-start(bf16[384,768]{1,0:T(8,128)(2,1)} %get-tuple-element.191.refs_9_), channel_id=1, source_target_pairs={{0,16},{16,0},{1,17},{17,1},{2,18},{18,2},{3,19},{19,3},{4,20},{20... | collective-permute-start | bytes 1769480 | tf_op jit(solution)/shard_map/ppermute | solution.py:1240
  294.3 29.9 %collective-permute-start.10 = (bf16[8,24,3072]{2,1,0:T(8,128)(2,1)}, bf16[8,24,3072]{2,1,0:T(8,128)(2,1)S(1)}, u32[]{:S(2)}, u32[]{:S(2)}) collective-permute-start(bf16[8,24,3072]{2,1,0:T(8,128)(2,1)} %get-tuple-element.198.refs_6_), channel_id=1, source_target_pairs={{0,2},{1,3},{2,0},{3,1},{4,6},{5,7},{6,4},{7,5},{8,10},{9,11},{10,... | collective-permute-start | bytes 3538952 | tf_op jit(solution)/shard_map/ppermute | solution.py:1104
  295.9 28.3 %collective-permute-start.14 = (bf16[384,1152]{1,0:T(8,128)(2,1)}, bf16[384,1152]{1,0:T(8,128)(2,1)S(1)}, u32[]{:S(2)}, u32[]{:S(2)}) collective-permute-start(bf16[384,1152]{1,0:T(8,128)(2,1)} %get-tuple-element.202.refs_10_), channel_id=1, source_target_pairs={{0,16},{16,0},{1,17},{17,1},{2,18},{18,2},{3,19},{19,3},{4,20},{20... | collective-permute-start | bytes 2654216 | tf_op jit(solution)/shard_map/ppermute | solution.py:1240
  295.9 28.2 %collective-permute-start.11 = (bf16[4,96,768]{2,1,0:T(8,128)(2,1)}, bf16[4,96,768]{2,1,0:T(8,128)(2,1)S(1)}, u32[]{:S(2)}, u32[]{:S(2)}) collective-permute-start(bf16[4,96,768]{2,1,0:T(8,128)(2,1)} %get-tuple-element.199.refs_7_), channel_id=1, source_target_pairs={{0,4},{1,5},{2,6},{3,7},{4,0},{5,1},{6,2},{7,3},{8,12},{9,13},{10,... | collective-permute-start | bytes 1769480 | tf_op jit(solution)/shard_map/ppermute | solution.py:1104
  297.5 26.6 %collective-permute-start.13 = (bf16[8,24,1280]{2,1,0:T(8,128)(2,1)}, bf16[8,24,1280]{2,1,0:T(8,128)(2,1)S(1)}, u32[]{:S(2)}, u32[]{:S(2)}) collective-permute-start(bf16[8,24,1280]{2,1,0:T(8,128)(2,1)} %get-tuple-element.201.refs_9_), channel_id=1, source_target_pairs={{0,1},{1,0},{2,3},{3,2},{4,5},{5,4},{6,7},{7,6},{8,9},{9,8},{10,11... | collective-permute-start | bytes 1474568 | tf_op jit(solution)/shard_map/ppermute | solution.py:1104
  298.4 25.7 %collective-permute-start.12 = (bf16[2,16,6144]{2,1,0:T(8,128)(2,1)}, bf16[2,16,6144]{2,1,0:T(8,128)(2,1)S(1)}, u32[]{:S(2)}, u32[]{:S(2)}) collective-permute-start(bf16[2,16,6144]{2,1,0:T(8,128)(2,1)} %get-tuple-element.200.refs_8_), channel_id=1, source_target_pairs={{0,4},{1,5},{2,6},{3,7},{4,0},{5,1},{6,2},{7,3},{8,12},{9,13},{10,... | collective-permute-start | bytes 1179656 | tf_op jit(solution)/shard_map/ppermute | solution.py:1104
  332.5 23.3 %collective-permute-start.20 = (bf16[384,1152]{1,0:T(8,128)(2,1)}, bf16[384,1152]{1,0:T(8,128)(2,1)S(1)}, u32[]{:S(2)}, u32[]{:S(2)}) collective-permute-start(bf16[384,1152]{1,0:T(8,128)(2,1)} %get-tuple-element.215.refs_14_), channel_id=1, source_target_pairs={{0,16},{16,0},{1,17},{17,1},{2,18},{18,2},{3,19},{19,3},{4,20},{20... | collective-permute-start | bytes 2654216 | tf_op jit(solution)/shard_map/ppermute | solution.py:1240
  332.6 23.2 %collective-permute-start.15 = (bf16[4,24,3072]{2,1,0:T(8,128)(2,1)}, bf16[4,24,3072]{2,1,0:T(8,128)(2,1)S(1)}, u32[]{:S(2)}, u32[]{:S(2)}) collective-permute-start(bf16[4,24,3072]{2,1,0:T(8,128)(2,1)} %get-tuple-element.210.refs_9_), channel_id=1, source_target_pairs={{0,1},{1,0},{2,3},{3,2},{4,5},{5,4},{6,7},{7,6},{8,9},{9,8},{10,11... | collective-permute-start | bytes 1769480 | tf_op jit(solution)/shard_map/ppermute | solution.py:1104
  333.7 12.4 %collective-permute-start.17 = (bf16[1,16,6144]{2,1,0:T(8,128)(2,1)}, bf16[1,16,6144]{2,1,0:T(8,128)(2,1)S(1)}, u32[]{:S(2)}, u32[]{:S(2)}) collective-permute-start(bf16[1,16,6144]{2,1,0:T(8,128)(2,1)} %get-tuple-element.212.refs_11_), channel_id=1, source_target_pairs={{0,8},{1,9},{2,10},{3,11},{4,12},{5,13},{6,14},{7,15},{8,0},{9,1},... | collective-permute-start | bytes 589832 | tf_op jit(solution)/shard_map/ppermute | solution.py:1104
  336.3 19.4 %collective-permute-start.19 = (bf16[8,24,1152]{2,1,0:T(8,128)(2,1)}, bf16[8,24,1152]{2,1,0:T(8,128)(2,1)S(1)}, u32[]{:S(2)}, u32[]{:S(2)}) collective-permute-start(bf16[8,24,1152]{2,1,0:T(8,128)(2,1)} %get-tuple-element.214.refs_13_), channel_id=1, source_target_pairs={{0,4},{1,5},{2,6},{3,7},{4,0},{5,1},{6,2},{7,3},{8,12},{9,13},{10,... | collective-permute-start | bytes 1327112 | tf_op jit(solution)/shard_map/ppermute | solution.py:1104
  337.9 17.8 %collective-permute-start.16 = (bf16[2,96,768]{2,1,0:T(8,128)(2,1)}, bf16[2,96,768]{2,1,0:T(8,128)(2,1)S(1)}, u32[]{:S(2)}, u32[]{:S(2)}) collective-permute-start(bf16[2,96,768]{2,1,0:T(8,128)(2,1)} %get-tuple-element.211.refs_10_), channel_id=1, source_target_pairs={{0,2},{1,3},{2,0},{3,1},{4,6},{5,7},{6,4},{7,5},{8,10},{9,11},{10,... | collective-permute-start | bytes 884744 | tf_op jit(solution)/shard_map/ppermute | solution.py:1104
  363.3 17.6 %collective-permute-start.25 = (bf16[8,24,1152]{2,1,0:T(8,128)(2,1)}, bf16[8,24,1152]{2,1,0:T(8,128)(2,1)S(1)}, u32[]{:S(2)}, u32[]{:S(2)}) collective-permute-start(bf16[8,24,1152]{2,1,0:T(8,128)(2,1)} %get-tuple-element.228.refs_13_), channel_id=1, source_target_pairs={{0,2},{1,3},{2,0},{3,1},{4,6},{5,7},{6,4},{7,5},{8,10},{9,11},{10,... | collective-permute-start | bytes 1327112 | tf_op jit(solution)/shard_map/ppermute | solution.py:1104
  364.7 16.2 %collective-permute-start.21 = (bf16[2,24,3072]{2,1,0:T(8,128)(2,1)}, bf16[2,24,3072]{2,1,0:T(8,128)(2,1)S(1)}, u32[]{:S(2)}, u32[]{:S(2)}) collective-permute-start(bf16[2,24,3072]{2,1,0:T(8,128)(2,1)} %get-tuple-element.224.refs_9_), channel_id=1, source_target_pairs={{0,4},{1,5},{2,6},{3,7},{4,0},{5,1},{6,2},{7,3},{8,12},{9,13},{10,... | collective-permute-start | bytes 884744 | tf_op jit(solution)/shard_map/ppermute | solution.py:1104
  365.4 15.4 %collective-permute-start.24 = (bf16[4,24,1152]{2,1,0:T(8,128)(2,1)}, bf16[4,24,1152]{2,1,0:T(8,128)(2,1)S(1)}, u32[]{:S(2)}, u32[]{:S(2)}) collective-permute-start(bf16[4,24,1152]{2,1,0:T(8,128)(2,1)} %get-tuple-element.227.refs_12_), channel_id=1, source_target_pairs={{0,1},{1,0},{2,3},{3,2},{4,5},{5,4},{6,7},{7,6},{8,9},{9,8},{10,11... | collective-permute-start | bytes 663560 | tf_op jit(solution)/shard_map/ppermute | solution.py:1104
  366.4 14.5 %collective-permute-start.22 = (bf16[1,96,768]{2,1,0:T(8,128)(2,1)}, bf16[1,96,768]{2,1,0:T(8,128)(2,1)S(1)}, u32[]{:S(2)}, u32[]{:S(2)}) collective-permute-start(bf16[1,96,768]{2,1,0:T(8,128)(2,1)} %get-tuple-element.225.refs_10_), channel_id=1, source_target_pairs={{0,8},{1,9},{2,10},{3,11},{4,12},{5,13},{6,14},{7,15},{8,0},{9,1},... | collective-permute-start | bytes 442376 | tf_op jit(solution)/shard_map/ppermute | solution.py:1104
  369.7 11.1 %collective-permute-start.23 = (bf16[2,24,1280]{2,1,0:T(8,128)(2,1)}, bf16[2,24,1280]{2,1,0:T(8,128)(2,1)S(1)}, u32[]{:S(2)}, u32[]{:S(2)}) collective-permute-start(bf16[2,24,1280]{2,1,0:T(8,128)(2,1)} %get-tuple-element.226.refs_11_), channel_id=1, source_target_pairs={{0,4},{1,5},{2,6},{3,7},{4,0},{5,1},{6,2},{7,3},{8,12},{9,13},{10,... | collective-permute-start | bytes 368648 | tf_op jit(solution)/shard_map/ppermute | solution.py:1104
  387.0 13.6 %collective-permute-start.31 = (bf16[4,24,1152]{2,1,0:T(8,128)(2,1)}, bf16[4,24,1152]{2,1,0:T(8,128)(2,1)S(1)}, u32[]{:S(2)}, u32[]{:S(2)}) collective-permute-start(bf16[4,24,1152]{2,1,0:T(8,128)(2,1)} %get-tuple-element.249.refs_8_), channel_id=1, source_target_pairs={{0,1},{1,0},{2,3},{3,2},{4,5},{5,4},{6,7},{7,6},{8,9},{9,8},{10,11... | collective-permute-start | bytes 663560 | tf_op jit(solution)/shard_map/ppermute | solution.py:1104
  388.1 12.5 %collective-permute-start.28 = (bf16[1,24,3072]{2,1,0:T(8,128)(2,1)}, bf16[1,24,3072]{2,1,0:T(8,128)(2,1)S(1)}, u32[]{:S(2)}, u32[]{:S(2)}) collective-permute-start(bf16[1,24,3072]{2,1,0:T(8,128)(2,1)} %get-tuple-element.246.refs_5_), channel_id=1, source_target_pairs={{0,8},{1,9},{2,10},{3,11},{4,12},{5,13},{6,14},{7,15},{8,0},{9,1},... | collective-permute-start | bytes 442376 | tf_op jit(solution)/shard_map/ppermute | solution.py:1104
  388.9 11.6 %collective-permute-start.30 = (bf16[2,24,1152]{2,1,0:T(8,128)(2,1)}, bf16[2,24,1152]{2,1,0:T(8,128)(2,1)S(1)}, u32[]{:S(2)}, u32[]{:S(2)}) collective-permute-start(bf16[2,24,1152]{2,1,0:T(8,128)(2,1)} %get-tuple-element.248.refs_7_), channel_id=1, source_target_pairs={{0,2},{1,3},{2,0},{3,1},{4,6},{5,7},{6,4},{7,5},{8,10},{9,11},{10,... | collective-permute-start | bytes 331784 | tf_op jit(solution)/shard_map/ppermute | solution.py:1104
  389.6 10.9 %collective-permute-start.32 = (f32[8,3072]{1,0:T(8,128)}, f32[8,3072]{1,0:T(8,128)S(1)}, u32[]{:S(2)}, u32[]{:S(2)}) collective-permute-start(f32[8,3072]{1,0:T(8,128)} %get-tuple-element.254.refs_9_), channel_id=1, source_target_pairs={{0,16},{1,17},{2,18},{3,19},{4,20},{5,21},{6,22},{7,23},{8,24},{9,... | collective-permute-start | bytes 294920 | tf_op jit(solution)/shard_map/ppermute | solution.py:1121
  389.7 10.8 %collective-permute-start.29 = (bf16[1,24,1280]{2,1,0:T(8,128)(2,1)}, bf16[1,24,1280]{2,1,0:T(8,128)(2,1)S(1)}, u32[]{:S(2)}, u32[]{:S(2)}) collective-permute-start(bf16[1,24,1280]{2,1,0:T(8,128)(2,1)} %get-tuple-element.247.refs_6_), channel_id=1, source_target_pairs={{0,8},{1,9},{2,10},{3,11},{4,12},{5,13},{6,14},{7,15},{8,0},{9,1},... | collective-permute-start | bytes 184328 | tf_op jit(solution)/shard_map/ppermute | solution.py:1104
  418.5 12.9 %collective-permute-start.41 = (f32[8,3072]{1,0:T(8,128)}, f32[8,3072]{1,0:T(8,128)S(1)}, u32[]{:S(2)}, u32[]{:S(2)}) collective-permute-start(f32[8,3072]{1,0:T(8,128)} %get-tuple-element.262.refs_3_), channel_id=1, source_target_pairs={{0,12},{1,13},{2,14},{3,15},{4,8},{5,9},{6,10},{7,11},{8,4},{9,5},... | collective-permute-start | bytes 294920 | tf_op jit(solution)/shard_map/ppermute | solution.py:1121
  420.3 11.1 %collective-permute-start.40 = (f32[8,3072]{1,0:T(8,128)}, f32[8,3072]{1,0:T(8,128)S(1)}, u32[]{:S(2)}, u32[]{:S(2)}) collective-permute-start(f32[8,3072]{1,0:T(8,128)} %get-tuple-element.262.refs_3_), channel_id=1, source_target_pairs={{0,8},{1,9},{2,10},{3,11},{4,12},{5,13},{6,14},{7,15},{8,0},{9,1},... | collective-permute-start | bytes 294920 | tf_op jit(solution)/shard_map/ppermute | solution.py:1121
  (55 other events, 171.1 us)

commit v4 on v3

--- a/solution.py
+++ b/solution.py
@@ -14,7 +14,7 @@
 ROW_STEP = 32
 GROUP = 128
 PARTS = 2
-VMEM_BYTES = 56 * 1024 * 1024
+VMEM_BYTES = 63 * 1024 * 1024
 MASKED = -1e30
 LOG2E = math.log2(math.e)
 
@@ -297,18 +297,20 @@
     return low(jnp.where(row < live, 0.0, MASKED))
 
 
-def attend_kernel(info_ref, q_ref, k_ref, v_ref, out_ref, *, heads_here, live):
+def attend_kernel(info_ref, q_ref, k_ref, v_ref, out_ref, scale_ref, *, heads_here, live):
     length = q_ref.shape[1]
     rate = (GROUP // heads_here) ** -0.5 * LOG2E
     bias = key_bias(live(info_ref, pl.program_id(0)), length)
     one = jnp.bfloat16(1.0)
-    half = length // 2
-    for start in range(0, q_ref.shape[2], GROUP):
-        group = slice(start, start + GROUP)
-        k, v = k_ref[0, :, group], v_ref[0, :, group]
-        for begin in range(0, length, half):
-            q = q_ref[0, begin : begin + half, group]
-            mixed = jnp.zeros((half, GROUP), jnp.float32)
+    middle = length // 2
+    for group in range(q_ref.shape[2] // GROUP):
+        columns = slice(group * GROUP, (group + 1) * GROUP)
+        k, v = k_ref[0, :, columns], v_ref[0, :, columns]
+        for rows in (slice(0, middle), slice(middle, length)):
+            q = q_ref[0, rows, columns]
+            mixed = jnp.zeros(q.shape, jnp.float32)
+            tops = jnp.zeros(q.shape, jnp.float32)
+            totals = jnp.ones(q.shape, jnp.float32)
             for head in range(heads_here):
                 mine, at_spare, spare = head_parts(head, heads_here)
                 head_q = jnp.where(mine, q, low(jnp.where(at_spare, 1.0, 0.0)))
@@ -316,9 +318,14 @@
                 highest = jnp.max(scores, axis=1, keepdims=True)
                 terms = low(jnp.exp2((scores - highest) * rate))
                 product = dot(terms, jnp.where(at_spare, one, v), NN)
-                total = product[:, spare : spare + 1]
-                mixed = jnp.where(mine, product * (1.0 / total), mixed)
-            out_ref[0, begin : begin + half, group] = low(mixed)
+                mixed = jnp.where(mine, product * (1.0 / product[:, spare : spare + 1]), mixed)
+                tops = jnp.where(at_spare, highest, tops)
+                totals = jnp.where(at_spare, product, totals)
+            out_ref[0, rows, columns] = low(mixed)
+            scales = (tops * rate + jnp.log2(totals)).T
+            for head in range(heads_here):
+                spare = head_parts(head, heads_here)[2]
+                scale_ref[0, group, head : head + 1, rows] = scales[spare : spare + 1]
 
 
 def all_live(length):
@@ -333,15 +340,16 @@
     strips, length, triple = packed.shape
     width = triple // 3
     heads_here = GROUP // (width // heads)
-    groups = 2
-    part = width // groups
-    third = lambda j: pl.BlockSpec((1, length, part), lambda s, g, _: (s, 0, g + j * groups))
+    steps = 2
+    part = width // steps
+    groups = part // GROUP
+    third = lambda j: pl.BlockSpec((1, length, part), lambda s, g, _: (s, 0, g + j * steps))
     return call(
         functools.partial(attend_kernel, heads_here=heads_here, live=live),
-        sds((strips, length, width)),
-        (strips, groups),
+        (sds((strips, length, width)), sds((strips, steps * groups, 8, length), jnp.float32)),
+        (strips, steps),
         [third(0), third(1), third(2)],
-        third(0),
+        (third(0), pl.BlockSpec((1, groups, 8, length), lambda s, g, _: (s, g, 0, 0))),
         strips * heads * length * length * GROUP * 6,
         strips * length * width * 8,
         exps=strips * heads * length * length,
@@ -355,6 +363,8 @@
     k_ref,
     v_ref,
     dout_ref,
+    mixed_ref,
+    scale_ref,
     n_ref,
     grad_ref,
     kept_ref,
@@ -371,6 +381,7 @@
     q, k, v, dout = q_ref[0], k_ref[0], v_ref[0], dout_ref[0]
     bias = key_bias(live(info_ref, strip), length)
     k_turned = k.T
+    agree = (dout.astype(jnp.float32) * mixed_ref[0].astype(jnp.float32)).T
     dq_turned = []
     dk = jnp.zeros((length, GROUP), jnp.float32)
     dv = jnp.zeros((length, GROUP), jnp.float32)
@@ -380,11 +391,9 @@
         head_q = jnp.where(mine, q, low(jnp.where(at_spare, 1.0, 0.0)))
         head_dout = jnp.where(mine, dout, jnp.bfloat16(0.0))
         scores = dot(jnp.where(at_spare, bias, k), head_q, NT)
-        highest = jnp.max(scores, axis=0, keepdims=True)
-        terms = jnp.exp2((scores - highest) * rate)
-        probs = terms * (1.0 / jnp.sum(terms, axis=0, keepdims=True))
-        weighted = probs * dot(v, head_dout, NT)
-        dscores = low(weighted - probs * jnp.sum(weighted, axis=0, keepdims=True))
+        probs = jnp.exp2(scores * rate - scale_ref[0, 0, head : head + 1, :])
+        average = jnp.sum(agree[head * size : (head + 1) * size], axis=0, keepdims=True)
+        dscores = low(probs * (dot(v, head_dout, NT) - average))
         dk = jnp.where(mine, dot(dscores, q, NN), dk)
         dv = jnp.where(mine, dot(low(probs), dout, NN), dv)
         dq_turned.append(dot(k_turned[head * size : (head + 1) * size], dscores, NN))
@@ -411,7 +420,9 @@
         sent_ref[...] = low(total_ref[pl.ds(pl.multiple_of((1 - info_ref[0]) * half, 8), half), :])
 
 
-def attend_back_call(packed, dmixed, normed, info, heads, live, part, parts, after, name):
+def attend_back_call(
+    packed, dmixed, mixed, scales, normed, info, heads, live, part, parts, after, name
+):
     strips, length, triple = packed.shape
     width = triple // 3
     heads_here = GROUP // (width // heads)
@@ -434,6 +445,8 @@
             third(1),
             third(2),
             third(0),
+            third(0),
+            pl.BlockSpec((1, 1, 8, length), lambda g, s, _: (s, g + part * here, 0, 0)),
             pl.BlockSpec((1, length, width), lambda g, s, _: (s, 0, 0)),
         ],
         (pl.BlockSpec((3, 1, length, GROUP), lambda g, s, _: (0, s, 0, g)), product, product),
@@ -443,7 +456,7 @@
         after=after,
         name=name,
         scratch=[pltpu.VMEM((width, 3 * GROUP), jnp.float32)],
-    )(info, packed, packed, packed, dmixed, normed)
+    )(info, packed, packed, packed, dmixed, mixed, scales, normed)
 
 
 def encoder_ff_kernel(info_ref, *refs, sizes):
@@ -1182,7 +1195,7 @@
                 width = pair[0].shape[-1]
                 for ref, chosen in zip(outs, (mine, 1 - mine)):
                     index = (h * 2 + chosen) * lower + l
-                    ref[h * lower + l, :, start : start + width] = low(total(pair, index))
+                    ref[h * lower + l, :, start : start + width] = pair[0][index] + pair[1][index]
                 start += width
 
 
@@ -1470,7 +1483,10 @@
     n1_enc, packed_enc = packed_call(sizes, info, patches, enc_gains, enc_shifts, enc_qkv)
     packed_enc = strip_form(packed_enc)
     enc_live = visible_live(strips)
-    mixed_enc = row_form(attend_call(packed_enc, info, HEADS_ENC, enc_live, "encoder_attention"))
+    mixed_enc, scales_enc = attend_call(
+        packed_enc, info, HEADS_ENC, enc_live, "encoder_attention"
+    )
+    mixed_enc = row_form(mixed_enc)
     mid_enc, n2_enc, act_enc, slope_enc, y_enc, encoded, projected = encoder_ff_call(
         sizes,
         info,
@@ -1491,7 +1507,10 @@
     )
     x_dec, n1_dec, packed_dec = map(strip_form, (x_dec, n1_dec, packed_dec))
     dec_live = all_live(length)
-    mixed_dec = row_form(attend_call(packed_dec, info, HEADS_DEC, dec_live, "decoder_attention"))
+    mixed_dec, scales_dec = attend_call(
+        packed_dec, info, HEADS_DEC, dec_live, "decoder_attention"
+    )
+    mixed_dec = row_form(mixed_dec)
     share = narrow // count
     (
         kept_dec,
@@ -1523,6 +1542,8 @@
     dpacked_dec, kept_dqkv, sent_dqkv = attend_back_call(
         packed_dec,
         strip_form(dmixed_dec),
+        strip_form(mixed_dec),
+        scales_dec,
         n1_dec,
         info,
         HEADS_DEC,
@@ -1598,6 +1619,8 @@
         dpacked, kept, sent_here = attend_back_call(
             packed_enc,
             strip_form(dmixed_enc),
+            strip_form(mixed_enc),
+            scales_enc,
             strip_form(n1_enc),
             info,
             HEADS_ENC,

time: 444 us -> 427 us (0.962)
  Pallas kernels: 352 us -> 333 us
  waiting for transfers between devices: 17.5 us -> 22.2 us
    pallas_call x29, Pallas kernels: 352 us -> 333 us  [call(): return lambda *operands: made(*operands, *after, *through)]
    ppermute x24, waiting for transfers between devices: 17.4 us -> 22.1 us  [take(): self.parts = [(kept, lax.ppermute(sent, 'dp', route))]]
    unnamed x94 -> x46, local copies, waits for them, and re-layouts: 20.5 us -> 16.1 us
  transfers between devices with their start and end apart: 42 -> 42, of which waited for: 5 -> 6; matrix products, arithmetic and copies ran while one was open for 1% -> 2% of each run, Pallas kernels for 44% -> 41%
where the time goes in v4:
time: 427 us; the launch traced here: 420 us
  Pallas kernels  333 us (78%)
  starting transfers between devices  42.4 us (10%)
  waiting for transfers between devices  22.2 us (5%)
  local copies, waits for them, and re-layouts  20.6 us (5%)
    pallas_call x29, Pallas kernels, call(): return lambda *operands: made(*operands, *after, *through)  333 us
    ppermute x24, starting transfers between devices, take(): self.parts = [(kept, lax.ppermute(sent, 'dp', route))]  31.9 us
    ppermute x24, waiting for transfers between devices, take(): self.parts = [(kept, lax.ppermute(sent, 'dp', route))]  22.1 us
    unnamed x46, local copies, waits for them, and re-layouts  16.1 us
  transfers between devices with their start and end apart: 42, of which 6 were waited for; matrix products, arithmetic and copies ran while one was open for 2% of the time, Pallas kernels for 41%

profile of v4, /device:TPU:0, one launch (start us, length us, event | category | flops | bytes accessed | tf_op | source)
XLA Modules:
  0.0 420.3 jit_solution(15388496672452184565)
XLA Ops:
  1.4 3.5 copy.67.refs_1_.refs_2_
  7.8 9.7 %encoder_packed.1 = (bf16[1088,768]{1,0:T(8,128)(2,1)}, bf16[1088,2304]{1,0:T(8,128)(2,1)}) custom-call(s32[14]{0:T(128)} %concatenate.3.refs_0_, bf16[4,529,768]{2,1,0:T(8,128)(2,1)} %copy.65.refs_1_.refs_2_.refs_6_, bf16[4,529,768]{2,1,0:T(8,128)(2,1)} %copy.65.refs_1_.refs_2_.refs_6_, bf16[3,768]{1,0:T(4,128)(2,1)} %refs_7_.13, bf16[3,768]{1,0:T(4,128)(2,1)} %refs_8_.11, ...), custom_call_target="tpu_custom_call" | custom-call | flops 15040512 | bytes 46464 | tf_op jit(solution)/shard_map/encoder_packed/pallas_call | solution.py:69
  17.5 18.2 %encoder_attention.1 = (bf16[2,544,768]{2,1,0:T(8,128)(2,1)}, f32[2,6,8,544]{3,2,1,0:T(8,128)}) custom-call(s32[14]{0:T(128)} %concatenate.3.refs_0_, bf16[2,544,2304]{2,1,0:T(8,128)(2,1)} %bitcast.35, bf16[2,544,2304]{2,1,0:T(8,128)(2,1)} %bitcast.36, bf16[2,544,2304]{2,1,0:T(8,128)(2,1)} %bitcast.37), custom_call_target="tpu_custom_call" | custom-call | flops 21307392 | bytes 26112 | tf_op jit(solution)/shard_map/encoder_attention/pallas_call | solution.py:69
  36.3 24.7 %encoder_feed_forward.1 = (bf16[1088,768]{1,0:T(8,128)(2,1)}, bf16[1088,768]{1,0:T(8,128)(2,1)}, bf16[1088,3072]{1,0:T(8,128)(2,1)}, bf16[1088,3072]{1,0:T(8,128...) custom-call(s32[14]{0:T(128)} %concatenate.3.refs_0_, ...), custom_call_target="tpu_custom_call" | custom-call | flops 48463872 | bytes 148992 | tf_op jit(solution)/shard_map/encoder_feed_forward/pallas_call | solution.py:69
  61.0 8.3 %decoder_packed.1 = (f32[1088,512]{1,0:T(8,128)}, bf16[1088,512]{1,0:T(8,128)(2,1)}, bf16[1088,1536]{1,0:T(8,128)(2,1)}) custom-call(s32[14]{0:T(128)} %concatenate.3.refs_0_, bf16[1088,512]{1,0:T(8,128)(2,1)} %get-tuple-element.160.refs_1_, s32[4,544]{1,0:T(4,128)} %pad.4.refs_2_.refs_4_, bf16[512]{0:T(512)(128)(2,1)} %refs_3_.5, ...), custom_call_target="tpu_custom_call" | custom-call | flops 9052160 | bytes 45312 | tf_op jit(solution)/shard_map/decoder_packed/pallas_call | solution.py:69
  69.3 22.4 %decoder_attention.1 = (bf16[2,544,512]{2,1,0:T(8,128)(2,1)}, f32[2,4,8,544]{3,2,1,0:T(8,128)}) custom-call(s32[14]{0:T(128)} %concatenate.3.refs_0_, bf16[2,544,1536]{2,1,0:T(8,128)(2,1)} %bitcast.44, bf16[2,544,1536]{2,1,0:T(8,128)(2,1)} %bitcast.45, bf16[2,544,1536]{2,1,0:T(8,128)(2,1)} %bitcast.46), custom_call_target="tpu_custom_call" | custom-call | flops 28409856 | bytes 17408 | tf_op jit(solution)/shard_map/decoder_attention/pallas_call | solution.py:69
  91.6 28.6 %decoder_feed_forward.1 = (bf16[2,529,256]{2,1,0:T(8,128)(2,1)}, bf16[2,529,256]{2,1,0:T(8,128)(2,1)}, bf16[1088,512]{1,0:T(8,128)(2,1)}, bf16[1088,512]{1,0:T(8...) custom-call(s32[14]{0:T(128)} %concatenate.3.refs_0_, ...), custom_call_target="tpu_custom_call" | custom-call | flops 60162048 | bytes 71680 | tf_op jit(solution)/shard_map/decoder_feed_forward/pallas_call | solution.py:69
  123.1 38.5 %decoder_attention_back.1 = (bf16[3,2,544,512]{3,2,1,0:T(8,128)(2,1)}, bf16[256,1536]{1,0:T(8,128)(2,1)}, bf16[256,1536]{1,0:T(8,128)(2,1)}) custom-call(s32[14]{0:T(128)} %concatenate.3.refs_0_, bf16[2,544,1536]{2,1,0:T(8,128)(2,1)} %bitcast.47, bf16[2,544,1536]{2,1,0:T(8,128)(2,1)} %bitcast.48, bf16[2,544,1536]{2,1,0:T(8,128)(2,1)} %bitcast.49, ...), custom_call_target="tpu_custom_call" | custom-call | flops 63504384 | bytes 30464 | tf_op jit(solution)/shard_map/decoder_attention_back/pallas_call | solution.py:69
  162.9 3.5 decoded_strips.1.refs_14_
  166.5 14.7 %decoder_packed_back.1 = (bf16[2,544,768]{2,1,0:T(8,128)(2,1)}, f32[8,512]{1,0:T(8,128)}, f32[8,768]{1,0:T(8,128)}, bf16[384,512]{1,0:T(8,128)(2,1)}, bf16[384,512]{1,0:T(8,128)(2,1)}) custom-call(s32[14]{0:T(128)} %concatenate.3.refs_0_, bf16[3,2,544,512]{3,2,1,0:T(8,128)(2,1)} %get-tuple-element.170.refs_3_.refs_1_, bf16[2,544,512]{2,1,0:T(8,128)(2,1)} %bitcast.68, ...), custom_call_target="tpu_custom_call" | custom-call | flops 15736832 | bytes 70144 | tf_op jit(solution)/shard_map/decoder_packed_back/pallas_call | solution.py:69
  181.3 10.7 %grad_enc_down.1 = (bf16[1536,768]{1,0:T(8,128)(2,1)}, bf16[1536,768]{1,0:T(8,128)(2,1)}) custom-call(s32[14]{0:T(128)} %concatenate.3.refs_0_, bf16[1088,3072]{1,0:T(8,128)(2,1)} %get-tuple-element.180.refs_1_.refs_2_, bf16[1088,3072]{1,0:T(8,128)(2,1)} %get-tuple-element.180.refs_1_.refs_2_, bf16[1088,768]{1,0:T(8,128)(2,1)} %bitcast.59, ...), custom_call_target="tpu_custom_call" | custom-call | flops 20054016 | bytes 51072 | tf_op jit(solution)/shard_map/grad_enc_down/pallas_call | solution.py:69
  192.9 5.4 %round_1.1 = (bf16[8,16,6144]{2,1,0:T(8,128)(2,1)}, bf16[8,16,6144]{2,1,0:T(8,128)(2,1)}, bf16[1536,768]{1,0:T(8,128)(2,1)}) custom-call(s32[14]{0:T(128)} %concatenate.3.refs_0_, bf16[16,16,4608]{2,1,0:T(8,128)(2,1)} %bitcast.64, bf16[16,16,4608]{2,1,0:T(8,128)(2,1)} %bitcast.14.refs_2_, ...), custom_call_target="tpu_custom_call", output_to_operand_aliasing={{2}: (7, {})} | custom-call | flops 24576 | bytes 49152 | tf_op jit(solution)/shard_map/round_1/pallas_call | solution.py:69
  201.3 22.3 %encoder_feed_forward_back.1 = (bf16[1088,3072]{1,0:T(8,128)(2,1)}, bf16[1088,768]{1,0:T(8,128)(2,1)}, bf16[1088,768]{1,0:T(8,128)(2,1)}, f32[8,768]{1,0:T(8,128)}, f32[8,3072]{1,0:T(8,128)}) custom-call(s32[14]{0:T(128)} %concatenate.3.refs_0_, bf16[1088,768]{1,0:T(8,128)(2,1)} %bitcast.60, bf16[1088,768]{1,0:T(8,128)(2,1)} %get-tuple-element.176.refs_2_, ...), custom_call_target="tpu_custom_call" | custom-call | flops 45121536 | bytes 145920 | tf_op jit(solution)/shard_map/encoder_feed_forward_back/pallas_call | solution.py:69
  223.6 14.1 %grad_enc_up_out.1 = (bf16[384,3072]{1,0:T(8,128)(2,1)}, bf16[384,3072]{1,0:T(8,128)(2,1)}, bf16[384,768]{1,0:T(8,128)(2,1)}, bf16[384,768]{1,0:T(8,128)(2,1)}) custom-call(s32[14]{0:T(128)} %concatenate.3.refs_0_, bf16[1088,768]{1,0:T(8,128)(2,1)} %get-tuple-element.190.refs_1_.refs_2_, bf16[1088,768]{1,0:T(8,128)(2,1)} %get-tuple-element.190.refs_1_.refs_2_, ...), custom_call_target="tpu_custom_call" | custom-call | flops 25067520 | bytes 68736 | tf_op jit(solution)/shard_map/grad_enc_up_out/pallas_call | solution.py:69
  237.7 6.6 %round_2.1 = (bf16[8,96,768]{2,1,0:T(8,128)(2,1)}, bf16[8,96,768]{2,1,0:T(8,128)(2,1)}, bf16[4,16,6144]{2,1,0:T(8,128)(2,1)}, bf16[4,16,6144]{2,1,0:T(8,128)(2,1...) custom-call(s32[14]{0:T(128)} %concatenate.3.refs_0_, ...), custom_call_target="tpu_custom_call", output_to_operand_aliasing={{4}: (6, {}), {5}: (7, {})} | custom-call | flops 30720 | bytes 61440 | tf_op jit(solution)/shard_map/round_2/pallas_call | solution.py:69
  246.6 20.8 %encoder_attention_back_0.1 = (bf16[3,2,544,384]{3,2,1,0:T(8,128)(2,1)}, bf16[384,1152]{1,0:T(8,128)(2,1)}, bf16[384,1152]{1,0:T(8,128)(2,1)}) custom-call(s32[14]{0:T(128)} %concatenate.3.refs_0_, bf16[2,544,2304]{2,1,0:T(8,128)(2,1)} %bitcast.38, bf16[2,544,2304]{2,1,0:T(8,128)(2,1)} %bitcast.39, bf16[2,544,2304]{2,1,0:T(8,128)(2,1)} %bitcast.40, ...), custom_call_target="tpu_custom_call" | custom-call | flops 28827648 | bytes 22848 | tf_op jit(solution)/shard_map/encoder_attention_back_0/pallas_call | solution.py:69
  267.4 5.6 %collective-permute-done.7.refs_4_ = bf16[8,96,768]{2,1,0:T(8,128)(2,1)} collective-permute-done((bf16[8,96,768]{2,1,0:T(8,128)(2,1)}, bf16[8,96,768]{2,1,0:T(8,128)(2,1)}, u32[]{:S(2)}, u32[]{:S(2)}) %collective-permute-start.7) | collective-permute-done | bytes 1179680 | tf_op jit(solution)/shard_map/ppermute | solution.py:1117
  273.1 8.5 %round_3.1 = (bf16[8,24,3072]{2,1,0:T(8,128)(2,1)}, bf16[8,24,3072]{2,1,0:T(8,128)(2,1)}, bf16[4,96,768]{2,1,0:T(8,128)(2,1)}, bf16[4,96,768]{2,1,0:T(8,128)(2,1...) custom-call(s32[14]{0:T(128)} %concatenate.3.refs_0_, ...), custom_call_target="tpu_custom_call", output_to_operand_aliasing={{8}: (12, {})} | custom-call | flops 41472 | bytes 82944 | tf_op jit(solution)/shard_map/round_3/pallas_call | solution.py:69
  285.8 20.9 %encoder_attention_back_1.1 = (bf16[3,2,544,384]{3,2,1,0:T(8,128)(2,1)}, bf16[384,1152]{1,0:T(8,128)(2,1)}, bf16[384,1152]{1,0:T(8,128)(2,1)}) custom-call(s32[14]{0:T(128)} %concatenate.3.refs_0_, bf16[2,544,2304]{2,1,0:T(8,128)(2,1)} %bitcast.41, bf16[2,544,2304]{2,1,0:T(8,128)(2,1)} %bitcast.42, bf16[2,544,2304]{2,1,0:T(8,128)(2,1)} %bitcast.43, ...), custom_call_target="tpu_custom_call" | custom-call | flops 28827648 | bytes 22848 | tf_op jit(solution)/shard_map/encoder_attention_back_1/pallas_call | solution.py:69
  309.3 6.4 %round_4.1 = (bf16[4,24,3072]{2,1,0:T(8,128)(2,1)}, bf16[4,24,3072]{2,1,0:T(8,128)(2,1)}, bf16[2,96,768]{2,1,0:T(8,128)(2,1)}, bf16[2,96,768]{2,1,0:T(8,128)(2,1...) custom-call(s32[14]{0:T(128)} %concatenate.3.refs_0_, ...), custom_call_target="tpu_custom_call", output_to_operand_aliasing={{10}: (12, {})} | custom-call | flops 27648 | bytes 55296 | tf_op jit(solution)/shard_map/round_4/pallas_call | solution.py:69
  322.3 6.9 %collective-permute-done.17.refs_6_ = bf16[1,16,6144]{2,1,0:T(8,128)(2,1)} collective-permute-done((bf16[1,16,6144]{2,1,0:T(8,128)(2,1)}, bf16[1,16,6144]{2,1,0:T(8,128)(2,1)}, u32[]{:S(2)}, u32[]{:S(2)}) %collective-permute-start.17) | collective-permute-done | bytes 196640 | tf_op jit(solution)/shard_map/ppermute | solution.py:1117
  330.7 8.8 %encoder_packed_back_0.1 = (bf16[1,529,384]{2,1,0:T(8,128)(2,1)}, bf16[1,529,384]{2,1,0:T(8,128)(2,1)}, f32[8,768]{1,0:T(8,128)}) custom-call(s32[14]{0:T(128)} %concatenate.3.refs_0_, bf16[3,2,544,384]{3,2,1,0:T(8,128)(2,1)} %get-tuple-element.200.refs_11_.refs_1_, bf16[3,2,544,384]{3,2,1,0:T(8,128)(2,1)} %get-tuple-element.211.refs_11_.refs_2_, ...), custom_call_target="tpu_custom_call" | custom-call | flops 7520256 | bytes 33408 | tf_op jit(solution)/shard_map/encoder_packed_back_0/pallas_call | solution.py:69
  340.5 5.8 %round_5.1 = (bf16[2,24,3072]{2,1,0:T(8,128)(2,1)}, bf16[2,24,3072]{2,1,0:T(8,128)(2,1)}, bf16[1,96,768]{2,1,0:T(8,128)(2,1)}, bf16[1,96,768]{2,1,0:T(8,128)(2,1...) custom-call(s32[14]{0:T(128)} %concatenate.3.refs_0_, ...), custom_call_target="tpu_custom_call" | custom-call | flops 20736 | bytes 41472 | tf_op jit(solution)/shard_map/round_5/pallas_call | solution.py:69
  348.7 3.4 collective-permute-start.22
  352.1 8.9 %encoder_packed_back_1.1 = (bf16[1,529,384]{2,1,0:T(8,128)(2,1)}, bf16[1,529,384]{2,1,0:T(8,128)(2,1)}, f32[8,768]{1,0:T(8,128)}) custom-call(s32[14]{0:T(128)} %concatenate.3.refs_0_, bf16[3,2,544,384]{3,2,1,0:T(8,128)(2,1)} %get-tuple-element.200.refs_11_.refs_1_, bf16[3,2,544,384]{3,2,1,0:T(8,128)(2,1)} %get-tuple-element.211.refs_11_.refs_2_, ...), custom_call_target="tpu_custom_call" | custom-call | flops 7520256 | bytes 33408 | tf_op jit(solution)/shard_map/encoder_packed_back_1/pallas_call | solution.py:69
  364.2 4.5 %round_6.1 = (bf16[1,24,3072]{2,1,0:T(8,128)(2,1)}, bf16[1,24,3072]{2,1,0:T(8,128)(2,1)}, f32[96,768]{1,0:T(8,128)}, bf16[1,24,1280]{2,1,0:T(8,128)(2,1)}, bf16[...) custom-call(s32[14]{0:T(128)} %concatenate.3.refs_0_, ...), custom_call_target="tpu_custom_call", output_to_operand_aliasing={{9}: (12, {}), {10}: (13, {}), {11}: (14, {})} | custom-call | flops 9600 | bytes 19200 | tf_op jit(solution)/shard_map/round_6/pallas_call | solution.py:69
  374.7 3.9 patch_grad_strips.1.refs_11_
  378.6 4.1 collective-permute-done.29.refs_4_
  383.4 3.9 round_7.1
  393.3 2.9 collective-permute-done.33.refs_2_
  397.0 3.4 round_8.1
  411.2 3.2 copy.74
  (135 shorter events, 65.8 us)
Async XLA Ops:
  120.2 71.9 %collective-permute-start.1 = (bf16[256,4608]{1,0:T(8,128)(2,1)}, bf16[256,4608]{1,0:T(8,128)(2,1)}, u32[]{:S(2)}, u32[]{:S(2)}) collective-permute-start(bf16[256,4608]{1,0:T(8,128)(2,1)} %get-tuple-element.169.refs_8_), channel_id=1, source_target_pairs={{0,16},{16,0},{1,17},{17,1},{2,18},{18,2},{3,19},{19,3},{4,20},{20... | collective-permute-start | bytes 7077896 | tf_op jit(solution)/shard_map/ppermute | solution.py:1253
  123.0 39.0 %collective-permute-start = (bf16[2,529,256]{2,0,1:T(2,128)(2,1)}, bf16[2,529,256]{2,0,1:T(2,128)(2,1)S(1)}, u32[]{:S(2)}, u32[]{:S(2)}) collective-permute-start(bf16[2,529,256]{2,0,1:T(2,128)(2,1)} %copy.69), channel_id=1, source_target_pairs={{0,16},{16,0},{1,17},{17,1},{2,18},{18,2},{3,19},{19,3},{4,20},{20... | collective-permute-start | bytes 1625096 | tf_op jit(solution)/shard_map/ppermute | solution.py:1253
  161.6 30.5 %collective-permute-start.2 = (bf16[256,1536]{1,0:T(8,128)(2,1)}, bf16[256,1536]{1,0:T(8,128)(2,1)}, u32[]{:S(2)}, u32[]{:S(2)}) collective-permute-start(bf16[256,1536]{1,0:T(8,128)(2,1)} %get-tuple-element.174.refs_13_), channel_id=1, source_target_pairs={{0,16},{16,0},{1,17},{17,1},{2,18},{18,2},{3,19},{19,3},{4,20},{20... | collective-permute-start | bytes 2359304 | tf_op jit(solution)/shard_map/ppermute | solution.py:1253
  181.2 10.9 %collective-permute-start.3 = (bf16[384,512]{1,0:T(8,128)(2,1)}, bf16[384,512]{1,0:T(8,128)(2,1)S(1)}, u32[]{:S(2)}, u32[]{:S(2)}) collective-permute-start(bf16[384,512]{1,0:T(8,128)(2,1)} %get-tuple-element.181.refs_4_), channel_id=1, source_target_pairs={{0,16},{16,0},{1,17},{17,1},{2,18},{18,2},{3,19},{19,3},{4,20},{20... | collective-permute-start | bytes 1179656 | tf_op jit(solution)/shard_map/ppermute | solution.py:1253
  198.3 39.4 %collective-permute-start.4 = (bf16[1536,768]{1,0:T(8,128)(2,1)}, bf16[1536,768]{1,0:T(8,128)(2,1)}, u32[]{:S(2)}, u32[]{:S(2)}) collective-permute-start(bf16[1536,768]{1,0:T(8,128)(2,1)} %get-tuple-element.185.refs_10_), channel_id=1, source_target_pairs={{0,16},{16,0},{1,17},{17,1},{2,18},{18,2},{3,19},{19,3},{4,20},{20... | collective-permute-start | bytes 7077896 | tf_op jit(solution)/shard_map/ppermute | solution.py:1253
  198.7 39.0 %collective-permute-start.5 = (bf16[8,16,6144]{2,1,0:T(8,128)(2,1)}, bf16[8,16,6144]{2,1,0:T(8,128)(2,1)}, u32[]{:S(2)}, u32[]{:S(2)}) collective-permute-start(bf16[8,16,6144]{2,1,0:T(8,128)(2,1)} %get-tuple-element.184.refs_9_.refs_7_), channel_id=1, source_target_pairs={{0,1},{1,0},{2,3},{3,2},{4,5},{5,4},{6,7},{7,6},{8,9},{9,8},{10,11... | collective-permute-start | bytes 4718600 | tf_op jit(solution)/shard_map/ppermute | solution.py:1117
  244.3 28.7 %collective-permute-start.6 = (bf16[384,3072]{1,0:T(8,128)(2,1)}, bf16[384,3072]{1,0:T(8,128)(2,1)}, u32[]{:S(2)}, u32[]{:S(2)}) collective-permute-start(bf16[384,3072]{1,0:T(8,128)(2,1)} %get-tuple-element.198.refs_10_), channel_id=1, source_target_pairs={{0,16},{16,0},{1,17},{17,1},{2,18},{18,2},{3,19},{19,3},{4,20},{20... | collective-permute-start | bytes 7077896 | tf_op jit(solution)/shard_map/ppermute | solution.py:1253
  244.6 28.5 %collective-permute-start.7 = (bf16[8,96,768]{2,1,0:T(8,128)(2,1)}, bf16[8,96,768]{2,1,0:T(8,128)(2,1)}, u32[]{:S(2)}, u32[]{:S(2)}) collective-permute-start(bf16[8,96,768]{2,1,0:T(8,128)(2,1)} %get-tuple-element.196.refs_8_), channel_id=1, source_target_pairs={{0,1},{1,0},{2,3},{3,2},{4,5},{5,4},{6,7},{7,6},{8,9},{9,8},{10,11... | collective-permute-start | bytes 3538952 | tf_op jit(solution)/shard_map/ppermute | solution.py:1117
  245.1 22.3 %collective-permute-start.8 = (bf16[4,16,6144]{2,1,0:T(8,128)(2,1)}, bf16[4,16,6144]{2,1,0:T(8,128)(2,1)S(1)}, u32[]{:S(2)}, u32[]{:S(2)}) collective-permute-start(bf16[4,16,6144]{2,1,0:T(8,128)(2,1)} %get-tuple-element.197.refs_9_), channel_id=1, source_target_pairs={{0,2},{1,3},{2,0},{3,1},{4,6},{5,7},{6,4},{7,5},{8,10},{9,11},{10,... | collective-permute-start | bytes 2359304 | tf_op jit(solution)/shard_map/ppermute | solution.py:1117
  246.6 20.8 %collective-permute-start.9 = (bf16[384,768]{1,0:T(8,128)(2,1)}, bf16[384,768]{1,0:T(8,128)(2,1)}, u32[]{:S(2)}, u32[]{:S(2)}) collective-permute-start(bf16[384,768]{1,0:T(8,128)(2,1)} %get-tuple-element.199.refs_11_), channel_id=1, source_target_pairs={{0,16},{16,0},{1,17},{17,1},{2,18},{18,2},{3,19},{19,3},{4,20},{20... | collective-permute-start | bytes 1769480 | tf_op jit(solution)/shard_map/ppermute | solution.py:1253
  281.6 27.7 %collective-permute-start.10 = (bf16[8,24,3072]{2,1,0:T(8,128)(2,1)}, bf16[8,24,3072]{2,1,0:T(8,128)(2,1)}, u32[]{:S(2)}, u32[]{:S(2)}) collective-permute-start(bf16[8,24,3072]{2,1,0:T(8,128)(2,1)} %get-tuple-element.206.refs_8_), channel_id=1, source_target_pairs={{0,2},{1,3},{2,0},{3,1},{4,6},{5,7},{6,4},{7,5},{8,10},{9,11},{10,... | collective-permute-start | bytes 3538952 | tf_op jit(solution)/shard_map/ppermute | solution.py:1117
  283.1 24.5 %collective-permute-start.14 = (bf16[384,1152]{1,0:T(8,128)(2,1)}, bf16[384,1152]{1,0:T(8,128)(2,1)S(1)}, u32[]{:S(2)}, u32[]{:S(2)}) collective-permute-start(bf16[384,1152]{1,0:T(8,128)(2,1)} %get-tuple-element.210.refs_12_), channel_id=1, source_target_pairs={{0,16},{16,0},{1,17},{17,1},{2,18},{18,2},{3,19},{19,3},{4,20},{20... | collective-permute-start | bytes 2654216 | tf_op jit(solution)/shard_map/ppermute | solution.py:1253
  283.1 24.5 %collective-permute-start.11 = (bf16[4,96,768]{2,1,0:T(8,128)(2,1)}, bf16[4,96,768]{2,1,0:T(8,128)(2,1)}, u32[]{:S(2)}, u32[]{:S(2)}) collective-permute-start(bf16[4,96,768]{2,1,0:T(8,128)(2,1)} %get-tuple-element.207.refs_9_), channel_id=1, source_target_pairs={{0,4},{1,5},{2,6},{3,7},{4,0},{5,1},{6,2},{7,3},{8,12},{9,13},{10,... | collective-permute-start | bytes 1769480 | tf_op jit(solution)/shard_map/ppermute | solution.py:1117
  284.7 22.9 %collective-permute-start.13 = (bf16[8,24,1280]{2,1,0:T(8,128)(2,1)}, bf16[8,24,1280]{2,1,0:T(8,128)(2,1)}, u32[]{:S(2)}, u32[]{:S(2)}) collective-permute-start(bf16[8,24,1280]{2,1,0:T(8,128)(2,1)} %get-tuple-element.209.refs_11_), channel_id=1, source_target_pairs={{0,1},{1,0},{2,3},{3,2},{4,5},{5,4},{6,7},{7,6},{8,9},{9,8},{10,11... | collective-permute-start | bytes 1474568 | tf_op jit(solution)/shard_map/ppermute | solution.py:1117
  285.4 22.1 %collective-permute-start.12 = (bf16[2,16,6144]{2,1,0:T(8,128)(2,1)}, bf16[2,16,6144]{2,1,0:T(8,128)(2,1)}, u32[]{:S(2)}, u32[]{:S(2)}) collective-permute-start(bf16[2,16,6144]{2,1,0:T(8,128)(2,1)} %get-tuple-element.208.refs_10_), channel_id=1, source_target_pairs={{0,4},{1,5},{2,6},{3,7},{4,0},{5,1},{6,2},{7,3},{8,12},{9,13},{10,... | collective-permute-start | bytes 1179656 | tf_op jit(solution)/shard_map/ppermute | solution.py:1117
  315.7 23.9 %collective-permute-start.20 = (bf16[384,1152]{1,0:T(8,128)(2,1)}, bf16[384,1152]{1,0:T(8,128)(2,1)S(1)}, u32[]{:S(2)}, u32[]{:S(2)}) collective-permute-start(bf16[384,1152]{1,0:T(8,128)(2,1)} %get-tuple-element.223.refs_14_), channel_id=1, source_target_pairs={{0,16},{16,0},{1,17},{17,1},{2,18},{18,2},{3,19},{19,3},{4,20},{20... | collective-permute-start | bytes 2654216 | tf_op jit(solution)/shard_map/ppermute | solution.py:1253
  315.8 23.8 %collective-permute-start.15 = (bf16[4,24,3072]{2,1,0:T(8,128)(2,1)}, bf16[4,24,3072]{2,1,0:T(8,128)(2,1)}, u32[]{:S(2)}, u32[]{:S(2)}) collective-permute-start(bf16[4,24,3072]{2,1,0:T(8,128)(2,1)} %get-tuple-element.218.refs_9_), channel_id=1, source_target_pairs={{0,1},{1,0},{2,3},{3,2},{4,5},{5,4},{6,7},{7,6},{8,9},{9,8},{10,11... | collective-permute-start | bytes 1769480 | tf_op jit(solution)/shard_map/ppermute | solution.py:1117
  316.7 12.5 %collective-permute-start.17 = (bf16[1,16,6144]{2,1,0:T(8,128)(2,1)}, bf16[1,16,6144]{2,1,0:T(8,128)(2,1)}, u32[]{:S(2)}, u32[]{:S(2)}) collective-permute-start(bf16[1,16,6144]{2,1,0:T(8,128)(2,1)} %get-tuple-element.220.refs_11_), channel_id=1, source_target_pairs={{0,8},{1,9},{2,10},{3,11},{4,12},{5,13},{6,14},{7,15},{8,0},{9,1},... | collective-permute-start | bytes 589832 | tf_op jit(solution)/shard_map/ppermute | solution.py:1117
  319.2 20.3 %collective-permute-start.19 = (bf16[8,24,1152]{2,1,0:T(8,128)(2,1)}, bf16[8,24,1152]{2,1,0:T(8,128)(2,1)}, u32[]{:S(2)}, u32[]{:S(2)}) collective-permute-start(bf16[8,24,1152]{2,1,0:T(8,128)(2,1)} %get-tuple-element.222.refs_13_), channel_id=1, source_target_pairs={{0,4},{1,5},{2,6},{3,7},{4,0},{5,1},{6,2},{7,3},{8,12},{9,13},{10,... | collective-permute-start | bytes 1327112 | tf_op jit(solution)/shard_map/ppermute | solution.py:1117
  320.8 18.7 %collective-permute-start.16 = (bf16[2,96,768]{2,1,0:T(8,128)(2,1)}, bf16[2,96,768]{2,1,0:T(8,128)(2,1)}, u32[]{:S(2)}, u32[]{:S(2)}) collective-permute-start(bf16[2,96,768]{2,1,0:T(8,128)(2,1)} %get-tuple-element.219.refs_10_), channel_id=1, source_target_pairs={{0,2},{1,3},{2,0},{3,1},{4,6},{5,7},{6,4},{7,5},{8,10},{9,11},{10,... | collective-permute-start | bytes 884744 | tf_op jit(solution)/shard_map/ppermute | solution.py:1117
  329.2 10.3 %collective-permute-start.18 = (bf16[4,24,1280]{2,1,0:T(8,128)(2,1)}, bf16[4,24,1280]{2,1,0:T(8,128)(2,1)}, u32[]{:S(2)}, u32[]{:S(2)}) collective-permute-start(bf16[4,24,1280]{2,1,0:T(8,128)(2,1)} %get-tuple-element.221.refs_12_), channel_id=1, source_target_pairs={{0,2},{1,3},{2,0},{3,1},{4,6},{5,7},{6,4},{7,5},{8,10},{9,11},{10,... | collective-permute-start | bytes 737288 | tf_op jit(solution)/shard_map/ppermute | solution.py:1117
  346.3 17.0 %collective-permute-start.25 = (bf16[8,24,1152]{2,1,0:T(8,128)(2,1)}, bf16[8,24,1152]{2,1,0:T(8,128)(2,1)S(1)}, u32[]{:S(2)}, u32[]{:S(2)}) collective-permute-start(bf16[8,24,1152]{2,1,0:T(8,128)(2,1)} %get-tuple-element.236.refs_13_), channel_id=1, source_target_pairs={{0,2},{1,3},{2,0},{3,1},{4,6},{5,7},{6,4},{7,5},{8,10},{9,11},{10,... | collective-permute-start | bytes 1327112 | tf_op jit(solution)/shard_map/ppermute | solution.py:1117
  346.9 16.3 %collective-permute-start.21 = (bf16[2,24,3072]{2,1,0:T(8,128)(2,1)}, bf16[2,24,3072]{2,1,0:T(8,128)(2,1)S(1)}, u32[]{:S(2)}, u32[]{:S(2)}) collective-permute-start(bf16[2,24,3072]{2,1,0:T(8,128)(2,1)} %get-tuple-element.232.refs_9_), channel_id=1, source_target_pairs={{0,4},{1,5},{2,6},{3,7},{4,0},{5,1},{6,2},{7,3},{8,12},{9,13},{10,... | collective-permute-start | bytes 884744 | tf_op jit(solution)/shard_map/ppermute | solution.py:1117
  347.5 15.8 %collective-permute-start.24 = (bf16[4,24,1152]{2,1,0:T(8,128)(2,1)}, bf16[4,24,1152]{2,1,0:T(8,128)(2,1)S(1)}, u32[]{:S(2)}, u32[]{:S(2)}) collective-permute-start(bf16[4,24,1152]{2,1,0:T(8,128)(2,1)} %get-tuple-element.235.refs_12_), channel_id=1, source_target_pairs={{0,1},{1,0},{2,3},{3,2},{4,5},{5,4},{6,7},{7,6},{8,9},{9,8},{10,11... | collective-permute-start | bytes 663560 | tf_op jit(solution)/shard_map/ppermute | solution.py:1117
  348.7 14.6 %collective-permute-start.22 = (bf16[1,96,768]{2,1,0:T(8,128)(2,1)}, bf16[1,96,768]{2,1,0:T(8,128)(2,1)}, u32[]{:S(2)}, u32[]{:S(2)}) collective-permute-start(bf16[1,96,768]{2,1,0:T(8,128)(2,1)} %get-tuple-element.233.refs_10_), channel_id=1, source_target_pairs={{0,8},{1,9},{2,10},{3,11},{4,12},{5,13},{6,14},{7,15},{8,0},{9,1},... | collective-permute-start | bytes 442376 | tf_op jit(solution)/shard_map/ppermute | solution.py:1117
  352.1 11.2 %collective-permute-start.23 = (bf16[2,24,1280]{2,1,0:T(8,128)(2,1)}, bf16[2,24,1280]{2,1,0:T(8,128)(2,1)}, u32[]{:S(2)}, u32[]{:S(2)}) collective-permute-start(bf16[2,24,1280]{2,1,0:T(8,128)(2,1)} %get-tuple-element.234.refs_11_), channel_id=1, source_target_pairs={{0,4},{1,5},{2,6},{3,7},{4,0},{5,1},{6,2},{7,3},{8,12},{9,13},{10,... | collective-permute-start | bytes 368648 | tf_op jit(solution)/shard_map/ppermute | solution.py:1117
  369.3 13.5 %collective-permute-start.31 = (bf16[4,24,1152]{2,1,0:T(8,128)(2,1)}, bf16[4,24,1152]{2,1,0:T(8,128)(2,1)}, u32[]{:S(2)}, u32[]{:S(2)}) collective-permute-start(bf16[4,24,1152]{2,1,0:T(8,128)(2,1)} %get-tuple-element.257.refs_8_), channel_id=1, source_target_pairs={{0,1},{1,0},{2,3},{3,2},{4,5},{5,4},{6,7},{7,6},{8,9},{9,8},{10,11... | collective-permute-start | bytes 663560 | tf_op jit(solution)/shard_map/ppermute | solution.py:1117
  370.2 12.6 %collective-permute-start.28 = (bf16[1,24,3072]{2,1,0:T(8,128)(2,1)}, bf16[1,24,3072]{2,1,0:T(8,128)(2,1)S(1)}, u32[]{:S(2)}, u32[]{:S(2)}) collective-permute-start(bf16[1,24,3072]{2,1,0:T(8,128)(2,1)} %get-tuple-element.254.refs_5_), channel_id=1, source_target_pairs={{0,8},{1,9},{2,10},{3,11},{4,12},{5,13},{6,14},{7,15},{8,0},{9,1},... | collective-permute-start | bytes 442376 | tf_op jit(solution)/shard_map/ppermute | solution.py:1117
  371.1 11.6 %collective-permute-start.30 = (bf16[2,24,1152]{2,1,0:T(8,128)(2,1)}, bf16[2,24,1152]{2,1,0:T(8,128)(2,1)}, u32[]{:S(2)}, u32[]{:S(2)}) collective-permute-start(bf16[2,24,1152]{2,1,0:T(8,128)(2,1)} %get-tuple-element.256.refs_7_), channel_id=1, source_target_pairs={{0,2},{1,3},{2,0},{3,1},{4,6},{5,7},{6,4},{7,5},{8,10},{9,11},{10,... | collective-permute-start | bytes 331784 | tf_op jit(solution)/shard_map/ppermute | solution.py:1117
  400.4 14.1 %collective-permute-start.41 = (f32[8,3072]{1,0:T(8,128)}, f32[8,3072]{1,0:T(8,128)S(1)}, u32[]{:S(2)}, u32[]{:S(2)}) collective-permute-start(f32[8,3072]{1,0:T(8,128)} %get-tuple-element.270.refs_3_), channel_id=1, source_target_pairs={{0,12},{1,13},{2,14},{3,15},{4,8},{5,9},{6,10},{7,11},{8,4},{9,5},... | collective-permute-start | bytes 294920 | tf_op jit(solution)/shard_map/ppermute | solution.py:1134
  402.3 12.2 %collective-permute-start.40 = (f32[8,3072]{1,0:T(8,128)}, f32[8,3072]{1,0:T(8,128)S(1)}, u32[]{:S(2)}, u32[]{:S(2)}) collective-permute-start(f32[8,3072]{1,0:T(8,128)} %get-tuple-element.270.refs_3_), channel_id=1, source_target_pairs={{0,8},{1,9},{2,10},{3,11},{4,12},{5,13},{6,14},{7,15},{8,0},{9,1},... | collective-permute-start | bytes 294920 | tf_op jit(solution)/shard_map/ppermute | solution.py:1134
  403.9 10.6 %collective-permute-start.39 = (f32[8,3072]{1,0:T(8,128)}, f32[8,3072]{1,0:T(8,128)S(1)}, u32[]{:S(2)}, u32[]{:S(2)}) collective-permute-start(f32[8,3072]{1,0:T(8,128)} %get-tuple-element.270.refs_3_), channel_id=1, source_target_pairs={{0,4},{1,5},{2,6},{3,7},{4,0},{5,1},{6,2},{7,3},{8,12},{9,13},{10,... | collective-permute-start | bytes 294920 | tf_op jit(solution)/shard_map/ppermute | solution.py:1134
  (31 other events, 101.3 us)

commit v5 on v4

--- a/solution.py
+++ b/solution.py
@@ -63,7 +63,7 @@
         ),
         input_output_aliases=aliases,
         compiler_params=pltpu.CompilerParams(vmem_limit_bytes=VMEM_BYTES),
-        cost_estimate=pl.CostEstimate(flops=flops // 256, bytes_accessed=moved // 256, transcendentals=0),
+        cost_estimate=pl.CostEstimate(flops=flops, bytes_accessed=moved, transcendentals=exps),
         name=name,
     )
     return lambda *operands: made(*operands, *after, *through)
@@ -82,9 +82,12 @@
     return ref[...].astype(jnp.float32).reshape(1, -1)
 
 
-def live_rows(values, start, count):
-    row = lax.broadcasted_iota(jnp.int32, (values.shape[0], 1), 0) + start
-    return jnp.where(row < count, values.astype(jnp.float32), 0.0)
+def padded_rows(ref, pad_ref):
+    length, padded = ref.shape[0], pad_ref.shape[0]
+    first = length // 8 * 8
+    pad_ref[first:, :] = jnp.zeros((padded - first, pad_ref.shape[1]), jnp.float32)
+    pad_ref[:length, :] = ref[...].astype(jnp.float32)
+    return pad_ref[...]
 
 
 def sds(shape, kind=jnp.bfloat16):
@@ -157,7 +160,7 @@
     def raw(self, width):
         return [
             pl.BlockSpec(
-                (None, self.padded, width), lambda *step, s=s: (step[-1][STRIP + s], 0, 0)
+                (None, self.length, width), lambda *step, s=s: (step[-1][STRIP + s], 0, 0)
             )
             for s in range(self.strips)
         ]
@@ -169,7 +172,7 @@
         return pl.BlockSpec((self.rows, width), lambda i, info: (0, i))
 
     def half(self, width):
-        return pl.BlockSpec((self.strips, self.padded, width), lambda *step: (0, 0, 0))
+        return pl.BlockSpec((self.strips, self.length, width), lambda *step: (0, 0, 0))
 
     def sums(self, width):
         return pl.BlockSpec((8, width), lambda *step: (0, 0))
@@ -187,8 +190,9 @@
 
 
 def store_halves(info_ref, kept_ref, sent_ref, values):
-    half = kept_ref.shape[-1]
+    length, half = kept_ref.shape
     first = info_ref[0] == 0
+    values = values[:length]
     kept_ref[...] = low(jnp.where(first, values[:, :half], values[:, half:]))
     sent_ref[...] = low(jnp.where(first, values[:, half:], values[:, :half]))
 
@@ -200,12 +204,12 @@
 
 def packed_kernel(info_ref, *refs, sizes):
     x_refs = refs[: sizes.strips]
-    gain_ref, shift_ref, w_ref, n_ref, packed_ref = refs[sizes.strips :]
+    gain_ref, shift_ref, w_ref, n_ref, packed_ref, pad_ref = refs[sizes.strips :]
 
     @first_step
     def normalize():
         for strip, x_ref in enumerate(x_refs):
-            x = live_rows(x_ref[...], 0, sizes.length)
+            x = padded_rows(x_ref, pad_ref)
             normed, _, _ = norm(x, row_of(gain_ref, 0), row_of(shift_ref, 0))
             n_ref[sizes.place(strip), :] = low(normed)
 
@@ -224,6 +228,7 @@
         6 * rows * width * width,
         rows * width * 10 + 6 * width * width,
         name="encoder_packed",
+        scratch=[pltpu.VMEM((sizes.padded, width), jnp.float32)],
     )(info, *[x] * sizes.strips, gains, shifts, w_qkv)
 
 
@@ -481,6 +486,7 @@
         projected_ref,
         y_ref,
         bias_ref,
+        pad_ref,
     ) = refs[sizes.strips :]
     places = [sizes.place(strip) for strip in range(sizes.strips)]
 
@@ -488,7 +494,7 @@
     def middle():
         bias_ref[...] = vector_of(bias_up_ref)
         for place, x_ref in zip(places, x_refs):
-            x = live_rows(x_ref[...], 0, sizes.length)
+            x = padded_rows(x_ref, pad_ref)
             mid = x + dot(mixed_ref[place, :], w_out_ref[...], NN) + row_of(bias_out_ref, 0)
             mid_ref[place, :] = low(mid)
             normed, _, _ = norm(mid, row_of(gain_ref, 1), row_of(shift_ref, 1))
@@ -560,7 +566,11 @@
         rows * (width * 16 + units * 4) + 2 * width * (width + 2 * units + narrow),
         exps=rows * units,
         name="encoder_feed_forward",
-        scratch=[pltpu.VMEM((rows, width), jnp.float32), pltpu.VMEM((1, units), jnp.float32)],
+        scratch=[
+            pltpu.VMEM((rows, width), jnp.float32),
+            pltpu.VMEM((1, units), jnp.float32),
+            pltpu.VMEM((sizes.padded, width), jnp.float32),
+        ],
     )(
         info,
         *[x] * sizes.strips,
@@ -608,6 +618,7 @@
         bias_ref,
         beside_ref,
         down_ref,
+        pad_ref,
     ) = refs[sizes.strips :]
     places = [sizes.place(strip) for strip in range(sizes.strips)]
     gain, shift = row_of(gain_ref, 1), row_of(shift_ref, 1)
@@ -622,7 +633,7 @@
             normed, _, _ = norm(mid, gain, shift)
             n_ref[place, :] = low(normed)
             y_ref[place, :] = mid + row_of(bias_out_ref, 1)
-            cot_ref[place, :] = low(live_rows(cot_here[...], 0, sizes.length))
+            cot_ref[place, :] = low(padded_rows(cot_here, pad_ref))
 
     chunk = w_up_ref.shape[1]
     bias = bias_ref[:, pl.ds(pl.multiple_of(pl.program_id(0) * chunk, GROUP), chunk)]
@@ -657,8 +668,8 @@
     @last_step
     def finish():
         totals = []
-        for strip, place in enumerate(places):
-            store_halves(info_ref, kept_ref.at[strip], sent_ref.at[strip], y_ref[place, :])
+        for place in places:
+            store_halves(info_ref, kept_ref.at[place], sent_ref.at[place], y_ref[place, :])
             _, unit, inverse = norm(mid_ref[place, :], gain, shift)
             grad = cot_ref[place, :].astype(jnp.float32)
             dnormed = dnormed_ref[place, :]
@@ -690,7 +701,7 @@
     units = w_up.shape[1]
     chunk = units // 4
     all_rows = sizes.all(width)
-    half = sds((sizes.strips, sizes.length, width // 2))
+    half = sds((rows, width // 2))
     up_sums = pl.BlockSpec((8, chunk), lambda i, info: (0, i))
     folds = units // width if share % 8 == 0 else 0
     beside = units + width + (units if folds else 0)
@@ -716,8 +727,8 @@
             pl.BlockSpec((chunk, width), lambda i, info: (i, 0)),
         ],
         (
-            sizes.half(width // 2),
-            sizes.half(width // 2),
+            sizes.all(width // 2),
+            sizes.all(width // 2),
             all_rows,
             all_rows,
             sizes.sums(width),
@@ -739,6 +750,7 @@
             pltpu.VMEM((1, units), jnp.float32),
             pltpu.VMEM((width, beside), jnp.bfloat16),
             pltpu.VMEM((16 if folds else units, width), jnp.bfloat16),
+            pltpu.VMEM((sizes.padded, width), jnp.float32),
         ],
     )(info, *[cot] * sizes.strips, x, mixed, gains, shifts, w_out, bias_out, w_up, bias_up, w_down)
 
@@ -958,9 +970,10 @@
     )(info, dpacked, gm, x, source, y, encoded, *weights)
 
 
-def encoder_back_kernel(info_ref, *refs, parts, length):
+def encoder_back_kernel(info_ref, *refs, parts):
     grad_refs, w_refs = refs[:parts], refs[parts : 2 * parts]
-    gb_ref, x_ref, gain_ref, shift_ref, kept_ref, sent_ref, sums_ref, dnormed_ref = refs[2 * parts :]
+    gb_ref, x_ref, gain_ref, shift_ref, kept_ref, sent_ref, *rest = refs[2 * parts :]
+    dnormed_ref, pad_ref = rest[-2:]
     term = sum(dot(grad_ref[...], w_ref[...], NT) for grad_ref, w_ref in zip(grad_refs, w_refs))
 
     @first_step
@@ -975,11 +988,10 @@
     def finish():
         dnormed = dnormed_ref[...]
         gain = row_of(gain_ref, 0)
-        x = live_rows(x_ref[...], 0, length)
-        _, unit, inverse = norm(x, gain, row_of(shift_ref, 0))
+        _, unit, inverse = norm(padded_rows(x_ref, pad_ref), gain, row_of(shift_ref, 0))
         dx = gb_ref[...].astype(jnp.float32) + norm_back(dnormed, unit, inverse, gain)
         store_halves(info_ref, kept_ref, sent_ref, dx)
-        set_rows(sums_ref, (col_sum(dnormed * unit), col_sum(dnormed)))
+        set_rows(rest[0], (col_sum(dnormed * unit), col_sum(dnormed)))
 
 
 def encoder_back_call(sizes, info, dpacked, gb, x, gains, shifts, w_qkv, strip, after):
@@ -988,9 +1000,9 @@
     half = sds((1, sizes.length, width // 2))
     parts = len(dpacked)
     here = width // parts
-    half_spec = pl.BlockSpec((None, padded, width // 2), lambda j, info: (0, 0, 0))
+    half_spec = pl.BlockSpec((None, sizes.length, width // 2), lambda j, info: (0, 0, 0))
     return call(
-        functools.partial(encoder_back_kernel, parts=parts, length=sizes.length),
+        functools.partial(encoder_back_kernel, parts=parts),
         (half, half, sds((8, width), jnp.float32)),
         (3,),
         [pl.BlockSpec((None, None, padded, here), lambda j, info: (j, strip, 0, 0))] * parts
@@ -1009,7 +1021,7 @@
         rows * width * 12 // sizes.strips + 6 * width * width,
         after=after,
         name=f"encoder_packed_back_{strip}",
-        scratch=[pltpu.VMEM((padded, width), jnp.float32)],
+        scratch=[pltpu.VMEM((padded, width), jnp.float32)] * 2,
     )(info, *dpacked, *[w_qkv] * parts, gb, x, gains, shifts)
 
 
@@ -1255,23 +1267,24 @@
 
 def arrange_kernel(info_ref, *refs, strips):
     *sources, out_ref = refs
+    length = out_ref.shape[1]
     holder = info_ref[STRIP + 2 * strips + pl.program_id(0)]
     slot = info_ref[STRIP + 4 * strips + pl.program_id(0)]
-    per = len(sources) // 2
     values = None
     for place in range(strips):
-        kept, arrived = (
-            (sources[place][0], sources[per + place][0])
-            if per == strips
-            else (sources[0][place], sources[1][place])
-        )
+        if len(sources) == 2:
+            padded = sources[0].shape[0] // strips
+            rows = slice(place * padded, (place + 1) * padded)
+            kept, arrived = (ref[rows, :] for ref in sources)
+        else:
+            kept, arrived = sources[place][0], sources[strips + place][0]
         chosen = jnp.where(holder == info_ref[0], kept, arrived)
         values = chosen if values is None else jnp.where(slot == place, chosen, values)
-    out_ref[0] = values
-
-
-def arrange_call(info, kept, arrived, strips, name, after=()):
-    _, length, half = kept[0].shape
+    out_ref[0] = values[:length]
+
+
+def arrange_call(info, kept, arrived, strips, length, name, after=()):
+    half = kept[0].shape[-1]
     return call(
         functools.partial(arrange_kernel, strips=strips),
         sds((2 * strips, length, half)),
@@ -1554,7 +1567,6 @@
         "decoder_attention_back",
     )
     arrived_dqkv = across(sent_dqkv)
-    decoded = arrange_call(info, [kept_dec], [arrived_dec], strips, "decoded_strips", (dpacked_dec,))
     grad_enc, sums_dec_in, sums_final, kept_proj, sent_proj = decoder_back_call(
         sizes,
         info,
@@ -1570,7 +1582,7 @@
         enc_proj,
         enc_gains,
         enc_shifts,
-        (sent_dqkv, decoded),
+        (sent_dqkv, arrived_dec),
     )
     grad_enc = row_form(grad_enc)
     arrived_proj = across(sent_proj)
@@ -1631,7 +1643,15 @@
             f"encoder_attention_back_{part}",
         )
         dpacked_enc.append(dpacked)
-        sent, (sent_here,) = round_call(info, active(), f"round_{number}", (dpacked,), (sent_here,))
+        before = (dpacked,)
+        if part == 0:
+            arranged = arrange_call(
+                info, [kept_dec], [arrived_dec], strips, length, "decoded_strips", before
+            )
+            turned = lax.optimization_barrier(jnp.swapaxes(arranged, 0, 1))
+            decoded = jnp.swapaxes(turned, 0, 1)
+            before = (dpacked, turned)
+        sent, (sent_here,) = round_call(info, active(), f"round_{number}", before, (sent_here,))
         chain = Chain(pairs, (by_z, by_y)[part % 2], ((kept, across(sent_here)),))
         number += 1
         qkv_enc.append(chain)
@@ -1671,8 +1691,11 @@
     arrived_enc = [across(array) for array in sent_enc]
     small = Total(pairs, small)
     every.append(small)
-    patch_grad = arrange_call(info, kept_enc, arrived_enc, strips, "patch_grad_strips", after)
+    patch_grad = arrange_call(info, kept_enc, arrived_enc, strips, length, "patch_grad_strips", after)
     after = (patch_grad,)
+    if not apart:
+        dec_shares = decoder_shares_call(info, grads_dec.done[0], narrow, dec_up.shape[1], after)
+        after += (dec_shares[1],)
     while active():
         round_call(info, active(), f"round_{number}", after)
         after = ()
@@ -1693,7 +1716,7 @@
         g_dup, g_dout = g_beside[:, : dec_up.shape[1]], g_beside[:, dec_up.shape[1] :]
         (g_ddown,) = down_dec.done
     else:
-        g_dup, g_dout, g_ddown = decoder_shares_call(info, g_beside, narrow, dec_up.shape[1], ())
+        g_dup, g_dout, g_ddown = dec_shares
     (g_edown,), (g_eup,) = down_enc.done, up_enc.done
     g_eout, g_proj = out_enc.done
     return (

time: 427 us -> 423 us (level)
    unnamed x46 -> x47, local copies, waits for them, and re-layouts: 16.1 us -> 15.1 us
  transfers between devices with their start and end apart: 42 -> 42, of which waited for: 6 -> 5; matrix products, arithmetic and copies ran while one was open for 2% -> 1% of each run, Pallas kernels for 41% -> 41%
where the time goes in v5:
time: 423 us; the launch traced here: 416 us
  Pallas kernels  333 us (79%)
  starting transfers between devices  40.8 us (10%)
  waiting for transfers between devices  20.4 us (5%)
  local copies, waits for them, and re-layouts  19.1 us (5%)
    pallas_call x29, Pallas kernels, call(): return lambda *operands: made(*operands, *after, *through)  333 us
    ppermute x24, starting transfers between devices, take(): self.parts = [(kept, lax.ppermute(sent, 'dp', route))]  30.1 us
    ppermute x24, waiting for transfers between devices, take(): self.parts = [(kept, lax.ppermute(sent, 'dp', route))]  20.3 us
    unnamed x47, local copies, waits for them, and re-layouts  15.1 us
  transfers between devices with their start and end apart: 42, of which 5 were waited for; matrix products, arithmetic and copies ran while one was open for 1% of the time, Pallas kernels for 41%

profile of v5, /device:TPU:0, one launch (start us, length us, event | category | flops | bytes accessed | tf_op | source)
XLA Modules:
  0.0 415.6 jit_solution(18265973329789705385)
XLA Ops:
  1.4 3.5 copy.57.refs_1_.refs_2_
  7.7 9.7 %encoder_packed.1 = (bf16[1088,768]{1,0:T(8,128)(2,1)}, bf16[1088,2304]{1,0:T(8,128)(2,1)}) custom-call(s32[14]{0:T(128)} %concatenate.3.refs_0_, bf16[4,529,768]{2,1,0:T(8,128)(2,1)} %copy.55.refs_1_.refs_2_.refs_6_, bf16[4,529,768]{2,1,0:T(8,128)(2,1)} %copy.55.refs_1_.refs_2_.refs_6_, bf16[3,768]{1,0:T(4,128)(2,1)} %refs_7_.13, bf16[3,768]{1,0:T(4,128)(2,1)} %refs_8_.11, ...), custom_call_target="tpu_custom_call" | custom-call | flops 3850371072 | bytes 11894784 | tf_op jit(solution)/shard_map/encoder_packed/pallas_call | solution.py:69
  17.4 18.3 %encoder_attention.1 = (bf16[2,544,768]{2,1,0:T(8,128)(2,1)}, f32[2,6,8,544]{3,2,1,0:T(8,128)}) custom-call(s32[14]{0:T(128)} %concatenate.3.refs_0_, bf16[2,544,2304]{2,1,0:T(8,128)(2,1)} %bitcast.55, bf16[2,544,2304]{2,1,0:T(8,128)(2,1)} %bitcast.56, bf16[2,544,2304]{2,1,0:T(8,128)(2,1)} %bitcast.57), custom_call_target="tpu_custom_call" | custom-call | flops 5454692352 | bytes 6684672 | tf_op jit(solution)/shard_map/encoder_attention/pallas_call | solution.py:69
  36.3 24.6 %encoder_feed_forward.1 = (bf16[1088,768]{1,0:T(8,128)(2,1)}, bf16[1088,768]{1,0:T(8,128)(2,1)}, bf16[1088,3072]{1,0:T(8,128)(2,1)}, bf16[1088,3072]{1,0:T(8,128...) custom-call(s32[14]{0:T(128)} %concatenate.3.refs_0_, ...), custom_call_target="tpu_custom_call" | custom-call | flops 12406751232 | bytes 38141952 | tf_op jit(solution)/shard_map/encoder_feed_forward/pallas_call | solution.py:69
  60.9 8.2 %decoder_packed.1 = (f32[1088,512]{1,0:T(8,128)}, bf16[1088,512]{1,0:T(8,128)(2,1)}, bf16[1088,1536]{1,0:T(8,128)(2,1)}) custom-call(s32[14]{0:T(128)} %concatenate.3.refs_0_, bf16[1088,512]{1,0:T(8,128)(2,1)} %get-tuple-element.160.refs_1_, s32[4,544]{1,0:T(4,128)} %pad.4.refs_2_.refs_4_, bf16[512]{0:T(512)(128)(2,1)} %refs_3_.5, ...), custom_call_target="tpu_custom_call" | custom-call | flops 2317352960 | bytes 11599872 | tf_op jit(solution)/shard_map/decoder_packed/pallas_call | solution.py:69
  69.1 22.3 %decoder_attention.1 = (bf16[2,544,512]{2,1,0:T(8,128)(2,1)}, f32[2,4,8,544]{3,2,1,0:T(8,128)}) custom-call(s32[14]{0:T(128)} %concatenate.3.refs_0_, bf16[2,544,1536]{2,1,0:T(8,128)(2,1)} %bitcast.64, bf16[2,544,1536]{2,1,0:T(8,128)(2,1)} %bitcast.65, bf16[2,544,1536]{2,1,0:T(8,128)(2,1)} %bitcast.66), custom_call_target="tpu_custom_call" | custom-call | flops 7272923136 | bytes 4456448 | tf_op jit(solution)/shard_map/decoder_attention/pallas_call | solution.py:69
  91.4 28.6 %decoder_feed_forward.1 = (bf16[1088,256]{1,0:T(8,128)(2,1)}, bf16[1088,256]{1,0:T(8,128)(2,1)}, bf16[1088,512]{1,0:T(8,128)(2,1)}, bf16[1088,512]{1,0:T(8,128)(...) custom-call(s32[14]{0:T(128)} %concatenate.3.refs_0_, ...), custom_call_target="tpu_custom_call" | custom-call | flops 15401484288 | bytes 18350080 | tf_op jit(solution)/shard_map/decoder_feed_forward/pallas_call | solution.py:69
  120.6 38.5 %decoder_attention_back.1 = (bf16[3,2,544,512]{3,2,1,0:T(8,128)(2,1)}, bf16[256,1536]{1,0:T(8,128)(2,1)}, bf16[256,1536]{1,0:T(8,128)(2,1)}) custom-call(s32[14]{0:T(128)} %concatenate.3.refs_0_, bf16[2,544,1536]{2,1,0:T(8,128)(2,1)} %bitcast.67, bf16[2,544,1536]{2,1,0:T(8,128)(2,1)} %bitcast.68, bf16[2,544,1536]{2,1,0:T(8,128)(2,1)} %bitcast.69, ...), custom_call_target="tpu_custom_call" | custom-call | flops 16257122304 | bytes 7798784 | tf_op jit(solution)/shard_map/decoder_attention_back/pallas_call | solution.py:69
  160.4 14.7 %decoder_packed_back.1 = (bf16[2,544,768]{2,1,0:T(8,128)(2,1)}, f32[8,512]{1,0:T(8,128)}, f32[8,768]{1,0:T(8,128)}, bf16[384,512]{1,0:T(8,128)(2,1)}, bf16[384,512]{1,0:T(8,128)(2,1)}) custom-call(s32[14]{0:T(128)} %concatenate.3.refs_0_, bf16[3,2,544,512]{3,2,1,0:T(8,128)(2,1)} %get-tuple-element.170.refs_1_, bf16[2,544,512]{2,1,0:T(8,128)(2,1)} %bitcast.82, ...), custom_call_target="tpu_custom_call" | custom-call | flops 4028628992 | bytes 17956864 | tf_op jit(solution)/shard_map/decoder_packed_back/pallas_call | solution.py:69
  175.3 10.7 %grad_enc_down.1 = (bf16[1536,768]{1,0:T(8,128)(2,1)}, bf16[1536,768]{1,0:T(8,128)(2,1)}) custom-call(s32[14]{0:T(128)} %concatenate.3.refs_0_, bf16[1088,3072]{1,0:T(8,128)(2,1)} %get-tuple-element.180.refs_1_.refs_2_, bf16[1088,3072]{1,0:T(8,128)(2,1)} %get-tuple-element.180.refs_1_.refs_2_, bf16[1088,768]{1,0:T(8,128)(2,1)} %bitcast.80, ...), custom_call_target="tpu_custom_call" | custom-call | flops 5133828096 | bytes 13074432 | tf_op jit(solution)/shard_map/grad_enc_down/pallas_call | solution.py:69
  186.8 5.5 %round_1.1 = (bf16[8,16,6144]{2,1,0:T(8,128)(2,1)}, bf16[8,16,6144]{2,1,0:T(8,128)(2,1)}, bf16[1536,768]{1,0:T(8,128)(2,1)}) custom-call(s32[14]{0:T(128)} %concatenate.3.refs_0_, bf16[16,16,4608]{2,1,0:T(8,128)(2,1)} %bitcast.43, bf16[16,16,4608]{2,1,0:T(8,128)(2,1)} %bitcast.14.refs_2_, ...), custom_call_target="tpu_custom_call", output_to_operand_aliasing={{2}: (7, {})} | custom-call | flops 6291456 | bytes 12582912 | tf_op jit(solution)/shard_map/round_1/pallas_call | solution.py:69
  195.2 22.3 %encoder_feed_forward_back.1 = (bf16[1088,3072]{1,0:T(8,128)(2,1)}, bf16[1088,768]{1,0:T(8,128)(2,1)}, bf16[1088,768]{1,0:T(8,128)(2,1)}, f32[8,768]{1,0:T(8,128)}, f32[8,3072]{1,0:T(8,128)}) custom-call(s32[14]{0:T(128)} %concatenate.3.refs_0_, bf16[1088,768]{1,0:T(8,128)(2,1)} %bitcast.81, bf16[1088,768]{1,0:T(8,128)(2,1)} %get-tuple-element.176.refs_2_, ...), custom_call_target="tpu_custom_call" | custom-call | flops 11551113216 | bytes 37355520 | tf_op jit(solution)/shard_map/encoder_feed_forward_back/pallas_call | solution.py:69
  217.6 14.1 %grad_enc_up_out.1 = (bf16[384,3072]{1,0:T(8,128)(2,1)}, bf16[384,3072]{1,0:T(8,128)(2,1)}, bf16[384,768]{1,0:T(8,128)(2,1)}, bf16[384,768]{1,0:T(8,128)(2,1)}) custom-call(s32[14]{0:T(128)} %concatenate.3.refs_0_, bf16[1088,768]{1,0:T(8,128)(2,1)} %get-tuple-element.190.refs_1_.refs_2_, bf16[1088,768]{1,0:T(8,128)(2,1)} %get-tuple-element.190.refs_1_.refs_2_, ...), custom_call_target="tpu_custom_call" | custom-call | flops 6417285120 | bytes 17596416 | tf_op jit(solution)/shard_map/grad_enc_up_out/pallas_call | solution.py:69
  231.7 6.5 %round_2.1 = (bf16[8,96,768]{2,1,0:T(8,128)(2,1)}, bf16[8,96,768]{2,1,0:T(8,128)(2,1)}, bf16[4,16,6144]{2,1,0:T(8,128)(2,1)}, bf16[4,16,6144]{2,1,0:T(8,128)(2,1...) custom-call(s32[14]{0:T(128)} %concatenate.3.refs_0_, ...), custom_call_target="tpu_custom_call", output_to_operand_aliasing={{4}: (6, {}), {5}: (7, {})} | custom-call | flops 7864320 | bytes 15728640 | tf_op jit(solution)/shard_map/round_2/pallas_call | solution.py:69
  240.5 20.9 %encoder_attention_back_0.1 = (bf16[3,2,544,384]{3,2,1,0:T(8,128)(2,1)}, bf16[384,1152]{1,0:T(8,128)(2,1)}, bf16[384,1152]{1,0:T(8,128)(2,1)}) custom-call(s32[14]{0:T(128)} %concatenate.3.refs_0_, bf16[2,544,2304]{2,1,0:T(8,128)(2,1)} %bitcast.58, bf16[2,544,2304]{2,1,0:T(8,128)(2,1)} %bitcast.59, bf16[2,544,2304]{2,1,0:T(8,128)(2,1)} %bitcast.60, ...), custom_call_target="tpu_custom_call" | custom-call | flops 7379877888 | bytes 5849088 | tf_op jit(solution)/shard_map/encoder_attention_back_0/pallas_call | solution.py:69
  261.4 3.7 decoded_strips.1
  268.7 8.1 %round_3.1 = (bf16[8,24,3072]{2,1,0:T(8,128)(2,1)}, bf16[8,24,3072]{2,1,0:T(8,128)(2,1)}, bf16[4,96,768]{2,1,0:T(8,128)(2,1)}, bf16[4,96,768]{2,1,0:T(8,128)(2,1...) custom-call(s32[14]{0:T(128)} %concatenate.3.refs_0_, ...), custom_call_target="tpu_custom_call", output_to_operand_aliasing={{8}: (13, {})} | custom-call | flops 10616832 | bytes 21233664 | tf_op jit(solution)/shard_map/round_3/pallas_call | solution.py:69
  281.1 20.8 %encoder_attention_back_1.1 = (bf16[3,2,544,384]{3,2,1,0:T(8,128)(2,1)}, bf16[384,1152]{1,0:T(8,128)(2,1)}, bf16[384,1152]{1,0:T(8,128)(2,1)}) custom-call(s32[14]{0:T(128)} %concatenate.3.refs_0_, bf16[2,544,2304]{2,1,0:T(8,128)(2,1)} %bitcast.61, bf16[2,544,2304]{2,1,0:T(8,128)(2,1)} %bitcast.62, bf16[2,544,2304]{2,1,0:T(8,128)(2,1)} %bitcast.63, ...), custom_call_target="tpu_custom_call" | custom-call | flops 7379877888 | bytes 5849088 | tf_op jit(solution)/shard_map/encoder_attention_back_1/pallas_call | solution.py:69
  302.0 3.6 collective-permute-done.10.refs_2_
  305.5 6.4 %round_4.1 = (bf16[4,24,3072]{2,1,0:T(8,128)(2,1)}, bf16[4,24,3072]{2,1,0:T(8,128)(2,1)}, bf16[2,96,768]{2,1,0:T(8,128)(2,1)}, bf16[2,96,768]{2,1,0:T(8,128)(2,1...) custom-call(s32[14]{0:T(128)} %concatenate.3.refs_0_, ...), custom_call_target="tpu_custom_call", output_to_operand_aliasing={{10}: (12, {})} | custom-call | flops 7077888 | bytes 14155776 | tf_op jit(solution)/shard_map/round_4/pallas_call | solution.py:69
  318.2 7.9 %collective-permute-done.17.refs_6_ = bf16[1,16,6144]{2,1,0:T(8,128)(2,1)} collective-permute-done((bf16[1,16,6144]{2,1,0:T(8,128)(2,1)}, bf16[1,16,6144]{2,1,0:T(8,128)(2,1)}, u32[]{:S(2)}, u32[]{:S(2)}) %collective-permute-start.17) | collective-permute-done | bytes 196640 | tf_op jit(solution)/shard_map/ppermute | solution.py:1129
  326.6 8.9 %encoder_packed_back_0.1 = (bf16[1,529,384]{2,1,0:T(8,128)(2,1)}, bf16[1,529,384]{2,1,0:T(8,128)(2,1)}, f32[8,768]{1,0:T(8,128)}) custom-call(s32[14]{0:T(128)} %concatenate.3.refs_0_, bf16[3,2,544,384]{3,2,1,0:T(8,128)(2,1)} %get-tuple-element.200.refs_3_.refs_11_.refs_1_, bf16[3,2,544,384]{3,2,1,0:T(8,128)(2,1)} %get-tuple-element.211.refs_11_.refs_2_, ...), custom_call_target="tpu_custom_call" | custom-call | flops 1925185536 | bytes 8552448 | tf_op jit(solution)/shard_map/encoder_packed_back_0/pallas_call | solution.py:69
  336.4 5.8 %round_5.1 = (bf16[2,24,3072]{2,1,0:T(8,128)(2,1)}, bf16[2,24,3072]{2,1,0:T(8,128)(2,1)}, bf16[1,96,768]{2,1,0:T(8,128)(2,1)}, bf16[1,96,768]{2,1,0:T(8,128)(2,1...) custom-call(s32[14]{0:T(128)} %concatenate.3.refs_0_, ...), custom_call_target="tpu_custom_call" | custom-call | flops 5308416 | bytes 10616832 | tf_op jit(solution)/shard_map/round_5/pallas_call | solution.py:69
  348.4 8.9 %encoder_packed_back_1.1 = (bf16[1,529,384]{2,1,0:T(8,128)(2,1)}, bf16[1,529,384]{2,1,0:T(8,128)(2,1)}, f32[8,768]{1,0:T(8,128)}) custom-call(s32[14]{0:T(128)} %concatenate.3.refs_0_, bf16[3,2,544,384]{3,2,1,0:T(8,128)(2,1)} %get-tuple-element.200.refs_3_.refs_11_.refs_1_, bf16[3,2,544,384]{3,2,1,0:T(8,128)(2,1)} %get-tuple-element.211.refs_11_.refs_2_, ...), custom_call_target="tpu_custom_call" | custom-call | flops 1925185536 | bytes 8552448 | tf_op jit(solution)/shard_map/encoder_packed_back_1/pallas_call | solution.py:69
  360.6 4.5 %round_6.1 = (bf16[1,24,3072]{2,1,0:T(8,128)(2,1)}, bf16[1,24,3072]{2,1,0:T(8,128)(2,1)}, f32[96,768]{1,0:T(8,128)}, bf16[1,24,1280]{2,1,0:T(8,128)(2,1)}, bf16[...) custom-call(s32[14]{0:T(128)} %concatenate.3.refs_0_, ...), custom_call_target="tpu_custom_call", output_to_operand_aliasing={{9}: (12, {}), {10}: (13, {}), {11}: (14, {})} | custom-call | flops 2457600 | bytes 4915200 | tf_op jit(solution)/shard_map/round_6/pallas_call | solution.py:69
  370.7 3.9 patch_grad_strips.1.refs_2_.refs_11_
  376.9 2.8 collective-permute-done.29.refs_4_
  380.4 3.9 round_7.1
  390.2 3.0 collective-permute-done.33.refs_2_
  394.0 3.4 round_8.1
  403.2 3.2 copy.62
  406.4 3.1 collective-permute-done.38.refs_2_
  (135 shorter events, 63.5 us)
Async XLA Ops:
  120.0 39.6 %collective-permute-start = (bf16[1088,256]{1,0:T(8,128)(2,1)}, bf16[1088,256]{1,0:T(8,128)(2,1)S(1)}, u32[]{:S(2)}, u32[]{:S(2)}) collective-permute-start(bf16[1088,256]{1,0:T(8,128)(2,1)} %get-tuple-element.165.refs_9_), channel_id=1, source_target_pairs={{0,16},{16,0},{1,17},{17,1},{2,18},{18,2},{3,19},{19,3},{4,20},{20... | collective-permute-start | bytes 1671176 | tf_op jit(solution)/shard_map/ppermute | solution.py:1265
  120.6 65.5 %collective-permute-start.1 = (bf16[256,4608]{1,0:T(8,128)(2,1)}, bf16[256,4608]{1,0:T(8,128)(2,1)}, u32[]{:S(2)}, u32[]{:S(2)}) collective-permute-start(bf16[256,4608]{1,0:T(8,128)(2,1)} %get-tuple-element.169.refs_8_), channel_id=1, source_target_pairs={{0,16},{16,0},{1,17},{17,1},{2,18},{18,2},{3,19},{19,3},{4,20},{20... | collective-permute-start | bytes 7077896 | tf_op jit(solution)/shard_map/ppermute | solution.py:1265
  159.2 26.9 %collective-permute-start.2 = (bf16[256,1536]{1,0:T(8,128)(2,1)}, bf16[256,1536]{1,0:T(8,128)(2,1)}, u32[]{:S(2)}, u32[]{:S(2)}) collective-permute-start(bf16[256,1536]{1,0:T(8,128)(2,1)} %get-tuple-element.174.refs_13_), channel_id=1, source_target_pairs={{0,16},{16,0},{1,17},{17,1},{2,18},{18,2},{3,19},{19,3},{4,20},{20... | collective-permute-start | bytes 2359304 | tf_op jit(solution)/shard_map/ppermute | solution.py:1265
  175.2 10.9 %collective-permute-start.3 = (bf16[384,512]{1,0:T(8,128)(2,1)}, bf16[384,512]{1,0:T(8,128)(2,1)S(1)}, u32[]{:S(2)}, u32[]{:S(2)}) collective-permute-start(bf16[384,512]{1,0:T(8,128)(2,1)} %get-tuple-element.181.refs_4_), channel_id=1, source_target_pairs={{0,16},{16,0},{1,17},{17,1},{2,18},{18,2},{3,19},{19,3},{4,20},{20... | collective-permute-start | bytes 1179656 | tf_op jit(solution)/shard_map/ppermute | solution.py:1265
  192.3 39.4 %collective-permute-start.4 = (bf16[1536,768]{1,0:T(8,128)(2,1)}, bf16[1536,768]{1,0:T(8,128)(2,1)}, u32[]{:S(2)}, u32[]{:S(2)}) collective-permute-start(bf16[1536,768]{1,0:T(8,128)(2,1)} %get-tuple-element.185.refs_10_), channel_id=1, source_target_pairs={{0,16},{16,0},{1,17},{17,1},{2,18},{18,2},{3,19},{19,3},{4,20},{20... | collective-permute-start | bytes 7077896 | tf_op jit(solution)/shard_map/ppermute | solution.py:1265
  192.7 38.9 %collective-permute-start.5 = (bf16[8,16,6144]{2,1,0:T(8,128)(2,1)}, bf16[8,16,6144]{2,1,0:T(8,128)(2,1)}, u32[]{:S(2)}, u32[]{:S(2)}) collective-permute-start(bf16[8,16,6144]{2,1,0:T(8,128)(2,1)} %get-tuple-element.184.refs_9_.refs_7_), channel_id=1, source_target_pairs={{0,1},{1,0},{2,3},{3,2},{4,5},{5,4},{6,7},{7,6},{8,9},{9,8},{10,11... | collective-permute-start | bytes 4718600 | tf_op jit(solution)/shard_map/ppermute | solution.py:1129
  238.2 29.6 %collective-permute-start.6 = (bf16[384,3072]{1,0:T(8,128)(2,1)}, bf16[384,3072]{1,0:T(8,128)(2,1)}, u32[]{:S(2)}, u32[]{:S(2)}) collective-permute-start(bf16[384,3072]{1,0:T(8,128)(2,1)} %get-tuple-element.198.refs_10_), channel_id=1, source_target_pairs={{0,16},{16,0},{1,17},{17,1},{2,18},{18,2},{3,19},{19,3},{4,20},{20... | collective-permute-start | bytes 7077896 | tf_op jit(solution)/shard_map/ppermute | solution.py:1265
  238.4 29.4 %collective-permute-start.7 = (bf16[8,96,768]{2,1,0:T(8,128)(2,1)}, bf16[8,96,768]{2,1,0:T(8,128)(2,1)}, u32[]{:S(2)}, u32[]{:S(2)}) collective-permute-start(bf16[8,96,768]{2,1,0:T(8,128)(2,1)} %get-tuple-element.196.refs_8_), channel_id=1, source_target_pairs={{0,1},{1,0},{2,3},{3,2},{4,5},{5,4},{6,7},{7,6},{8,9},{9,8},{10,11... | collective-permute-start | bytes 3538952 | tf_op jit(solution)/shard_map/ppermute | solution.py:1129
  238.9 28.9 %collective-permute-start.8 = (bf16[4,16,6144]{2,1,0:T(8,128)(2,1)}, bf16[4,16,6144]{2,1,0:T(8,128)(2,1)S(1)}, u32[]{:S(2)}, u32[]{:S(2)}) collective-permute-start(bf16[4,16,6144]{2,1,0:T(8,128)(2,1)} %get-tuple-element.197.refs_9_), channel_id=1, source_target_pairs={{0,2},{1,3},{2,0},{3,1},{4,6},{5,7},{6,4},{7,5},{8,10},{9,11},{10,... | collective-permute-start | bytes 2359304 | tf_op jit(solution)/shard_map/ppermute | solution.py:1129
  240.5 27.3 %collective-permute-start.9 = (bf16[384,768]{1,0:T(8,128)(2,1)}, bf16[384,768]{1,0:T(8,128)(2,1)}, u32[]{:S(2)}, u32[]{:S(2)}) collective-permute-start(bf16[384,768]{1,0:T(8,128)(2,1)} %get-tuple-element.199.refs_11_), channel_id=1, source_target_pairs={{0,16},{16,0},{1,17},{17,1},{2,18},{18,2},{3,19},{19,3},{4,20},{20... | collective-permute-start | bytes 1769480 | tf_op jit(solution)/shard_map/ppermute | solution.py:1265
  276.8 28.8 %collective-permute-start.10 = (bf16[8,24,3072]{2,1,0:T(8,128)(2,1)}, bf16[8,24,3072]{2,1,0:T(8,128)(2,1)}, u32[]{:S(2)}, u32[]{:S(2)}) collective-permute-start(bf16[8,24,3072]{2,1,0:T(8,128)(2,1)} %get-tuple-element.206.refs_8_), channel_id=1, source_target_pairs={{0,2},{1,3},{2,0},{3,1},{4,6},{5,7},{6,4},{7,5},{8,10},{9,11},{10,... | collective-permute-start | bytes 3538952 | tf_op jit(solution)/shard_map/ppermute | solution.py:1129
  277.3 24.6 %collective-permute-start.14 = (bf16[384,1152]{1,0:T(8,128)(2,1)}, bf16[384,1152]{1,0:T(8,128)(2,1)S(1)}, u32[]{:S(2)}, u32[]{:S(2)}) collective-permute-start(bf16[384,1152]{1,0:T(8,128)(2,1)} %get-tuple-element.210.refs_12_), channel_id=1, source_target_pairs={{0,16},{16,0},{1,17},{17,1},{2,18},{18,2},{3,19},{19,3},{4,20},{20... | collective-permute-start | bytes 2654216 | tf_op jit(solution)/shard_map/ppermute | solution.py:1265
  277.5 24.4 %collective-permute-start.12 = (bf16[2,16,6144]{2,1,0:T(8,128)(2,1)}, bf16[2,16,6144]{2,1,0:T(8,128)(2,1)}, u32[]{:S(2)}, u32[]{:S(2)}) collective-permute-start(bf16[2,16,6144]{2,1,0:T(8,128)(2,1)} %get-tuple-element.208.refs_10_), channel_id=1, source_target_pairs={{0,4},{1,5},{2,6},{3,7},{4,0},{5,1},{6,2},{7,3},{8,12},{9,13},{10,... | collective-permute-start | bytes 1179656 | tf_op jit(solution)/shard_map/ppermute | solution.py:1129
  279.1 22.8 %collective-permute-start.13 = (bf16[8,24,1280]{2,1,0:T(8,128)(2,1)}, bf16[8,24,1280]{2,1,0:T(8,128)(2,1)}, u32[]{:S(2)}, u32[]{:S(2)}) collective-permute-start(bf16[8,24,1280]{2,1,0:T(8,128)(2,1)} %get-tuple-element.209.refs_11_), channel_id=1, source_target_pairs={{0,1},{1,0},{2,3},{3,2},{4,5},{5,4},{6,7},{7,6},{8,9},{9,8},{10,11... | collective-permute-start | bytes 1474568 | tf_op jit(solution)/shard_map/ppermute | solution.py:1129
  280.6 21.3 %collective-permute-start.11 = (bf16[4,96,768]{2,1,0:T(8,128)(2,1)}, bf16[4,96,768]{2,1,0:T(8,128)(2,1)}, u32[]{:S(2)}, u32[]{:S(2)}) collective-permute-start(bf16[4,96,768]{2,1,0:T(8,128)(2,1)} %get-tuple-element.207.refs_9_), channel_id=1, source_target_pairs={{0,4},{1,5},{2,6},{3,7},{4,0},{5,1},{6,2},{7,3},{8,12},{9,13},{10,... | collective-permute-start | bytes 1769480 | tf_op jit(solution)/shard_map/ppermute | solution.py:1129
  311.9 23.6 %collective-permute-start.20 = (bf16[384,1152]{1,0:T(8,128)(2,1)}, bf16[384,1152]{1,0:T(8,128)(2,1)S(1)}, u32[]{:S(2)}, u32[]{:S(2)}) collective-permute-start(bf16[384,1152]{1,0:T(8,128)(2,1)} %get-tuple-element.223.refs_14_), channel_id=1, source_target_pairs={{0,16},{16,0},{1,17},{17,1},{2,18},{18,2},{3,19},{19,3},{4,20},{20... | collective-permute-start | bytes 2654216 | tf_op jit(solution)/shard_map/ppermute | solution.py:1265
  312.0 23.5 %collective-permute-start.15 = (bf16[4,24,3072]{2,1,0:T(8,128)(2,1)}, bf16[4,24,3072]{2,1,0:T(8,128)(2,1)}, u32[]{:S(2)}, u32[]{:S(2)}) collective-permute-start(bf16[4,24,3072]{2,1,0:T(8,128)(2,1)} %get-tuple-element.218.refs_9_), channel_id=1, source_target_pairs={{0,1},{1,0},{2,3},{3,2},{4,5},{5,4},{6,7},{7,6},{8,9},{9,8},{10,11... | collective-permute-start | bytes 1769480 | tf_op jit(solution)/shard_map/ppermute | solution.py:1129
  313.6 12.5 %collective-permute-start.17 = (bf16[1,16,6144]{2,1,0:T(8,128)(2,1)}, bf16[1,16,6144]{2,1,0:T(8,128)(2,1)}, u32[]{:S(2)}, u32[]{:S(2)}) collective-permute-start(bf16[1,16,6144]{2,1,0:T(8,128)(2,1)} %get-tuple-element.220.refs_11_), channel_id=1, source_target_pairs={{0,8},{1,9},{2,10},{3,11},{4,12},{5,13},{6,14},{7,15},{8,0},{9,1},... | collective-permute-start | bytes 589832 | tf_op jit(solution)/shard_map/ppermute | solution.py:1129
  316.1 19.3 %collective-permute-start.19 = (bf16[8,24,1152]{2,1,0:T(8,128)(2,1)}, bf16[8,24,1152]{2,1,0:T(8,128)(2,1)}, u32[]{:S(2)}, u32[]{:S(2)}) collective-permute-start(bf16[8,24,1152]{2,1,0:T(8,128)(2,1)} %get-tuple-element.222.refs_13_), channel_id=1, source_target_pairs={{0,4},{1,5},{2,6},{3,7},{4,0},{5,1},{6,2},{7,3},{8,12},{9,13},{10,... | collective-permute-start | bytes 1327112 | tf_op jit(solution)/shard_map/ppermute | solution.py:1129
  317.7 17.7 %collective-permute-start.16 = (bf16[2,96,768]{2,1,0:T(8,128)(2,1)}, bf16[2,96,768]{2,1,0:T(8,128)(2,1)}, u32[]{:S(2)}, u32[]{:S(2)}) collective-permute-start(bf16[2,96,768]{2,1,0:T(8,128)(2,1)} %get-tuple-element.219.refs_10_), channel_id=1, source_target_pairs={{0,2},{1,3},{2,0},{3,1},{4,6},{5,7},{6,4},{7,5},{8,10},{9,11},{10,... | collective-permute-start | bytes 884744 | tf_op jit(solution)/shard_map/ppermute | solution.py:1129
  342.3 17.4 %collective-permute-start.25 = (bf16[8,24,1152]{2,1,0:T(8,128)(2,1)}, bf16[8,24,1152]{2,1,0:T(8,128)(2,1)S(1)}, u32[]{:S(2)}, u32[]{:S(2)}) collective-permute-start(bf16[8,24,1152]{2,1,0:T(8,128)(2,1)} %get-tuple-element.236.refs_13_), channel_id=1, source_target_pairs={{0,2},{1,3},{2,0},{3,1},{4,6},{5,7},{6,4},{7,5},{8,10},{9,11},{10,... | collective-permute-start | bytes 1327112 | tf_op jit(solution)/shard_map/ppermute | solution.py:1129
  343.9 15.8 %collective-permute-start.21 = (bf16[2,24,3072]{2,1,0:T(8,128)(2,1)}, bf16[2,24,3072]{2,1,0:T(8,128)(2,1)S(1)}, u32[]{:S(2)}, u32[]{:S(2)}) collective-permute-start(bf16[2,24,3072]{2,1,0:T(8,128)(2,1)} %get-tuple-element.232.refs_9_), channel_id=1, source_target_pairs={{0,4},{1,5},{2,6},{3,7},{4,0},{5,1},{6,2},{7,3},{8,12},{9,13},{10,... | collective-permute-start | bytes 884744 | tf_op jit(solution)/shard_map/ppermute | solution.py:1129
  344.4 15.2 %collective-permute-start.24 = (bf16[4,24,1152]{2,1,0:T(8,128)(2,1)}, bf16[4,24,1152]{2,1,0:T(8,128)(2,1)S(1)}, u32[]{:S(2)}, u32[]{:S(2)}) collective-permute-start(bf16[4,24,1152]{2,1,0:T(8,128)(2,1)} %get-tuple-element.235.refs_12_), channel_id=1, source_target_pairs={{0,1},{1,0},{2,3},{3,2},{4,5},{5,4},{6,7},{7,6},{8,9},{9,8},{10,11... | collective-permute-start | bytes 663560 | tf_op jit(solution)/shard_map/ppermute | solution.py:1129
  345.0 14.6 %collective-permute-start.23 = (bf16[2,24,1280]{2,1,0:T(8,128)(2,1)}, bf16[2,24,1280]{2,1,0:T(8,128)(2,1)}, u32[]{:S(2)}, u32[]{:S(2)}) collective-permute-start(bf16[2,24,1280]{2,1,0:T(8,128)(2,1)} %get-tuple-element.234.refs_11_), channel_id=1, source_target_pairs={{0,4},{1,5},{2,6},{3,7},{4,0},{5,1},{6,2},{7,3},{8,12},{9,13},{10,... | collective-permute-start | bytes 368648 | tf_op jit(solution)/shard_map/ppermute | solution.py:1129
  346.4 13.2 %collective-permute-start.22 = (bf16[1,96,768]{2,1,0:T(8,128)(2,1)}, bf16[1,96,768]{2,1,0:T(8,128)(2,1)}, u32[]{:S(2)}, u32[]{:S(2)}) collective-permute-start(bf16[1,96,768]{2,1,0:T(8,128)(2,1)} %get-tuple-element.233.refs_10_), channel_id=1, source_target_pairs={{0,8},{1,9},{2,10},{3,11},{4,12},{5,13},{6,14},{7,15},{8,0},{9,1},... | collective-permute-start | bytes 442376 | tf_op jit(solution)/shard_map/ppermute | solution.py:1129
  365.6 14.1 %collective-permute-start.31 = (bf16[4,24,1152]{2,1,0:T(8,128)(2,1)}, bf16[4,24,1152]{2,1,0:T(8,128)(2,1)}, u32[]{:S(2)}, u32[]{:S(2)}) collective-permute-start(bf16[4,24,1152]{2,1,0:T(8,128)(2,1)} %get-tuple-element.257.refs_8_), channel_id=1, source_target_pairs={{0,1},{1,0},{2,3},{3,2},{4,5},{5,4},{6,7},{7,6},{8,9},{9,8},{10,11... | collective-permute-start | bytes 663560 | tf_op jit(solution)/shard_map/ppermute | solution.py:1129
  367.1 12.6 %collective-permute-start.28 = (bf16[1,24,3072]{2,1,0:T(8,128)(2,1)}, bf16[1,24,3072]{2,1,0:T(8,128)(2,1)S(1)}, u32[]{:S(2)}, u32[]{:S(2)}) collective-permute-start(bf16[1,24,3072]{2,1,0:T(8,128)(2,1)} %get-tuple-element.254.refs_5_), channel_id=1, source_target_pairs={{0,8},{1,9},{2,10},{3,11},{4,12},{5,13},{6,14},{7,15},{8,0},{9,1},... | collective-permute-start | bytes 442376 | tf_op jit(solution)/shard_map/ppermute | solution.py:1129
  368.1 11.6 %collective-permute-start.30 = (bf16[2,24,1152]{2,1,0:T(8,128)(2,1)}, bf16[2,24,1152]{2,1,0:T(8,128)(2,1)}, u32[]{:S(2)}, u32[]{:S(2)}) collective-permute-start(bf16[2,24,1152]{2,1,0:T(8,128)(2,1)} %get-tuple-element.256.refs_7_), channel_id=1, source_target_pairs={{0,2},{1,3},{2,0},{3,1},{4,6},{5,7},{6,4},{7,5},{8,10},{9,11},{10,... | collective-permute-start | bytes 331784 | tf_op jit(solution)/shard_map/ppermute | solution.py:1129
  368.5 11.2 %collective-permute-start.32 = (f32[8,3072]{1,0:T(8,128)}, f32[8,3072]{1,0:T(8,128)}, u32[]{:S(2)}, u32[]{:S(2)}) collective-permute-start(f32[8,3072]{1,0:T(8,128)} %get-tuple-element.262.refs_9_), channel_id=1, source_target_pairs={{0,16},{1,17},{2,18},{3,19},{4,20},{5,21},{6,22},{7,23},{8,24},{9,... | collective-permute-start | bytes 294920 | tf_op jit(solution)/shard_map/ppermute | solution.py:1146
  368.6 11.1 %collective-permute-start.29 = (bf16[1,24,1280]{2,1,0:T(8,128)(2,1)}, bf16[1,24,1280]{2,1,0:T(8,128)(2,1)}, u32[]{:S(2)}, u32[]{:S(2)}) collective-permute-start(bf16[1,24,1280]{2,1,0:T(8,128)(2,1)} %get-tuple-element.255.refs_6_), channel_id=1, source_target_pairs={{0,8},{1,9},{2,10},{3,11},{4,12},{5,13},{6,14},{7,15},{8,0},{9,1},... | collective-permute-start | bytes 184328 | tf_op jit(solution)/shard_map/ppermute | solution.py:1129
  397.4 12.1 %collective-permute-start.41 = (f32[8,3072]{1,0:T(8,128)}, f32[8,3072]{1,0:T(8,128)S(1)}, u32[]{:S(2)}, u32[]{:S(2)}) collective-permute-start(f32[8,3072]{1,0:T(8,128)} %get-tuple-element.272.refs_3_), channel_id=1, source_target_pairs={{0,12},{1,13},{2,14},{3,15},{4,8},{5,9},{6,10},{7,11},{8,4},{9,5},... | collective-permute-start | bytes 294920 | tf_op jit(solution)/shard_map/ppermute | solution.py:1146
  399.2 10.3 %collective-permute-start.40 = (f32[8,3072]{1,0:T(8,128)}, f32[8,3072]{1,0:T(8,128)S(1)}, u32[]{:S(2)}, u32[]{:S(2)}) collective-permute-start(f32[8,3072]{1,0:T(8,128)} %get-tuple-element.272.refs_3_), channel_id=1, source_target_pairs={{0,8},{1,9},{2,10},{3,11},{4,12},{5,13},{6,14},{7,15},{8,0},{9,1},... | collective-permute-start | bytes 294920 | tf_op jit(solution)/shard_map/ppermute | solution.py:1146
  (32 other events, 96.2 us)
